TPU v7x, 128 devices: a whole 4x4x4 slice. The times are simulated.
128 devices in a mesh: seq: 16 (over x, y), leaf: 8 (over z, core).
Axes of the slice: x: 4, y: 4, z: 4, core: 2. Of those that a mesh axis runs over, the one named last changes fastest.
Arguments:
- prompt_x: bfloat16 [8, 8192, 4096], P('leaf', 'seq'), may hold values from -6 to 6
- prompt_dt: float32 [8, 8192, 64], P('leaf', 'seq')
- head_rate: float32 [64], replicated
- prompt_b: bfloat16 [8, 8192, 512], P('leaf', 'seq'), may hold values from -6 to 6
- prompt_c: bfloat16 [8, 8192, 512], P('leaf', 'seq'), may hold values from -0.75 to 0.75
- prompt_dy: bfloat16 [8, 8192, 4096], P('leaf', 'seq'), may hold values from -3 to 3
- branch_x: bfloat16 [128, 256, 4096], P(('seq', 'leaf')), may hold values from -6 to 6
- branch_dt: float32 [128, 256, 64], P(('seq', 'leaf'))
- branch_b: bfloat16 [128, 256, 512], P(('seq', 'leaf')), may hold values from -6 to 6
- branch_c: bfloat16 [128, 256, 512], P(('seq', 'leaf')), may hold values from -0.75 to 0.75
- branch_dy: bfloat16 [128, 256, 4096], P(('seq', 'leaf')), may hold values from -3 to 3
- parent: int32 [128], P(('seq', 'leaf')), may hold values from 0 to 7
- lengths: int32 [128], P(('seq', 'leaf')), may hold values from 1 to 256, 16640 in all
Outputs:
- prompt_dx: bfloat16 [8, 8192, 4096], P('leaf', 'seq')
- prompt_db: bfloat16 [8, 8192, 512], P('leaf', 'seq')
- prompt_dc: bfloat16 [8, 8192, 512], P('leaf', 'seq')
- branch_dx: bfloat16 [128, 256, 4096], P(('seq', 'leaf'))
- branch_db: bfloat16 [128, 256, 512], P(('seq', 'leaf'))
- branch_dc: bfloat16 [128, 256, 512], P(('seq', 'leaf'))
All inputs are finite; a program needn't handle non-finite values. No bound on the sum of `lengths` on one device may be relied on, other than what follows from the above.
Results may differ from a plain program's by a relative error of at most 0.001.
Values sent between devices are 32-bit elements; how exact they have to be, the bound alone decides.
No kernel may reach another device: no remote copies, remote signals or barrier semaphores. Data moves between devices by JAX's collectives and lax.ppermute only.
A program may use at most 192 MiB of HBM per device.

v0:
```python
import jax
import jax.numpy as jnp
from jax import lax
from jax.sharding import PartitionSpec as P

P_SIZE = 64
N = 64


highest = lax.Precision.HIGHEST


def prefix(part, axis, combine, identity, reverse):
    count = lax.axis_size(axis)
    place = lax.axis_index(axis)
    ahead = count - 1 - place if reverse else place
    gathered = jax.tree.map(lambda a: lax.all_gather(a, axis), part)
    state = jax.tree.map(lambda a, e: jnp.zeros_like(a) + jnp.asarray(e, a.dtype), part, identity)

    def one(step, state):
        source = count - 1 - step if reverse else step
        return combine(
            state, jax.tree.map(lambda a: lax.dynamic_index_in_dim(a, source, 0, False), gathered)
        )

    return lax.fori_loop(0, ahead, one, state)


def broadcast(block, axis, owner):
    block = jnp.where(lax.axis_index(axis) == owner, block, jnp.zeros_like(block))
    return lax.psum(block, axis)


def segment(inputs, step_rates, head_rate, b_proj, c_proj, initial):
    length = inputs.shape[0]
    head_count = step_rates.shape[1]
    head_width = initial.shape[1]
    states = initial.shape[2]
    groups = b_proj.shape[1] // states
    per_group = head_count // groups
    cumlog = jnp.cumsum(-step_rates * head_rate[None, :], axis=0)
    x_groups = inputs.reshape(length, groups, per_group, head_width).transpose(1, 0, 2, 3)
    b_groups = b_proj.reshape(length, groups, states).transpose(1, 0, 2)
    c_groups = c_proj.reshape(length, groups, states).transpose(1, 0, 2)
    cum_groups = cumlog.reshape(length, groups, per_group).transpose(1, 0, 2)
    rate_groups = step_rates.reshape(length, groups, per_group).transpose(1, 0, 2)
    init_groups = initial.reshape(groups, per_group, head_width, states)
    positions = jnp.arange(length)
    causal = (positions[:, None] >= positions[None, :])[None]

    def one_group(packed):
        x_one, b_one, c_one, cum_one, rate_one, init_one = packed
        scores = jnp.dot(c_one, b_one.T, precision=highest)
        spread = cum_one.T[:, :, None] - cum_one.T[:, None, :]
        decays = jnp.where(causal, jnp.exp(jnp.where(causal, spread, 0.0)), 0.0)
        weights = decays * scores[None] * rate_one.T[:, None, :]
        output = jnp.einsum("hts,shp->thp", weights, x_one, precision=highest)
        carried = jnp.einsum("tn,hpn->thp", c_one, init_one, precision=highest)
        output = output + jnp.exp(cum_one)[:, :, None] * carried
        final_log = cum_one[-1]
        weighting = jnp.exp(final_log[None, :] - cum_one) * rate_one
        closing = jnp.exp(final_log)[:, None, None] * init_one + jnp.einsum(
            "shp,sn->hpn", weighting[:, :, None] * x_one, b_one, precision=highest
        )
        return (output, closing)

    outputs, closings = lax.map(
        jax.checkpoint(one_group),
        (x_groups, b_groups, c_groups, cum_groups, rate_groups, init_groups),
    )
    return (
        outputs.transpose(1, 0, 2, 3).reshape(length, head_count * head_width),
        closings.reshape(head_count, head_width, states),
    )


def block_summary(inputs, step_rates, head_rate, b_proj):
    length, head_count = step_rates.shape
    groups = b_proj.shape[1] // N
    cumlog = jnp.cumsum(-step_rates * head_rate[None, :], axis=0)
    final_log = cumlog[-1]
    weighting = jnp.exp(final_log[None, :] - cumlog) * step_rates
    scaled = (weighting[:, :, None] * inputs.reshape(length, head_count, P_SIZE)).reshape(
        length, groups, head_count // groups, P_SIZE
    )
    b_groups = b_proj.reshape(length, groups, N)
    summary = jnp.einsum("tghp,tgn->ghpn", scaled, b_groups, precision=highest)
    return (final_log, summary.reshape(head_count, P_SIZE * N))


def carried_gradient(grad_out, step_rates, head_rate, c_proj):
    length, head_count = step_rates.shape
    groups = c_proj.shape[1] // N
    cumlog = jnp.cumsum(-step_rates * head_rate[None, :], axis=0)
    scaled = (jnp.exp(cumlog)[:, :, None] * grad_out.reshape(length, head_count, P_SIZE)).reshape(
        length, groups, head_count // groups, P_SIZE
    )
    c_groups = c_proj.reshape(length, groups, N)
    gathered_terms = jnp.einsum("tghp,tgn->ghpn", scaled, c_groups, precision=highest)
    return gathered_terms.reshape(head_count, P_SIZE * N)


def compose(earlier, later):
    return (earlier[0] + later[0], jnp.exp(later[0])[:, None] * earlier[1] + later[1])


def local(
    prompt_x,
    prompt_dt,
    head_rate,
    prompt_b,
    prompt_c,
    prompt_dy,
    branch_x,
    branch_dt,
    branch_b,
    branch_c,
    branch_dy,
    parent,
    lengths,
):
    inputs = prompt_x[0].astype(jnp.float32)
    step_rates = prompt_dt[0]
    b_proj = prompt_b[0].astype(jnp.float32)
    c_proj = prompt_c[0].astype(jnp.float32)
    head_count = step_rates.shape[1]
    flat_size = P_SIZE * N
    rows = lax.axis_size("seq")
    trees = lax.axis_size("leaf")
    final_log, summary = block_summary(inputs, step_rates, head_rate, b_proj)
    neutral = (
        jnp.zeros((head_count,), jnp.float32),
        jnp.zeros((head_count, flat_size), jnp.float32),
    )
    before = prefix((final_log, summary), "seq", compose, neutral, False)
    initial = before[1]
    closing = jnp.exp(final_log)[:, None] * initial + summary
    row_all = lax.all_gather(closing[None], "leaf", axis=0, tiled=True)
    ends_all = broadcast(row_all, "seq", rows - 1)
    select = (jnp.arange(trees) == parent[0]).astype(jnp.float32)
    branch_init = jnp.sum(select[:, None, None] * ends_all, axis=0)
    slot_count = branch_x.shape[1]
    live = (jnp.arange(slot_count) < lengths[0]).astype(jnp.float32)
    branch_rates = branch_dt[0] * live[:, None]

    def branch_out(x_in, b_in, c_in, init_in):
        return segment(
            x_in, branch_rates, head_rate, b_in, c_in, init_in.reshape(head_count, P_SIZE, N)
        )[0]

    _, branch_pull = jax.vjp(
        branch_out,
        branch_x[0].astype(jnp.float32),
        branch_b[0].astype(jnp.float32),
        branch_c[0].astype(jnp.float32),
        branch_init,
    )
    branch_gx, branch_gb, branch_gc, init_grad = branch_pull(
        branch_dy[0].astype(jnp.float32) * live[:, None]
    )
    term = select[:, None, None] * init_grad[None]
    partial_sum = lax.psum_scatter(term, "leaf", scatter_dimension=0, tiled=True)
    total = lax.psum(partial_sum[0], "seq")
    carry_terms = carried_gradient(prompt_dy[0].astype(jnp.float32), step_rates, head_rate, c_proj)
    after = prefix((final_log, carry_terms), "seq", compose, neutral, True)
    end_grad = jnp.exp(after[0])[:, None] * total + after[1]

    def prompt_out(x_in, b_in, c_in):
        return segment(
            x_in, step_rates, head_rate, b_in, c_in, initial.reshape(head_count, P_SIZE, N)
        )

    _, prompt_pull = jax.vjp(prompt_out, inputs, b_proj, c_proj)
    prompt_gx, prompt_gb, prompt_gc = prompt_pull(
        (prompt_dy[0].astype(jnp.float32), end_grad.reshape(head_count, P_SIZE, N))
    )
    return (
        prompt_gx.astype(jnp.bfloat16)[None],
        prompt_gb.astype(jnp.bfloat16)[None],
        prompt_gc.astype(jnp.bfloat16)[None],
        branch_gx.astype(jnp.bfloat16)[None],
        branch_gb.astype(jnp.bfloat16)[None],
        branch_gc.astype(jnp.bfloat16)[None],
    )


def solution(mesh):
    in_specs = (
        P("leaf", "seq", None),
        P("leaf", "seq", None),
        P(),
        P("leaf", "seq", None),
        P("leaf", "seq", None),
        P("leaf", "seq", None),
        P(("seq", "leaf"), None, None),
        P(("seq", "leaf"), None, None),
        P(("seq", "leaf"), None, None),
        P(("seq", "leaf"), None, None),
        P(("seq", "leaf"), None, None),
        P(("seq", "leaf")),
        P(("seq", "leaf")),
    )
    out_specs = (
        P("leaf", "seq", None),
        P("leaf", "seq", None),
        P("leaf", "seq", None),
        P(("seq", "leaf"), None, None),
        P(("seq", "leaf"), None, None),
        P(("seq", "leaf"), None, None),
    )
    return jax.shard_map(local, mesh=mesh, in_specs=in_specs, out_specs=out_specs, check_vma=False)
```

profile of v0, /device:TPU:0, one launch (start us, length us, event | category | flops | bytes accessed | tf_op | source)
XLA Modules:
  0.0 1066.0 jit_solution(13525762690374908839)
XLA Ops:
  12.3 7.1 copy.77
  19.6 6.6 fusion.60
  28.6 21.0 %all-gather.1 = f32[16,1,64]{2,1,0:T(1,128)S(1)} all-gather(f32[1,1,64]{2,1,0:T(1,128)S(1)} %bitcast.414), channel_id=1, replica_groups=mesh['seq'=16,'leaf'=8] {'seq'}, dimensions={0}, use_global_device_ids=true | all-gather | bytes 4352 | tf_op jit(solution)/shard_map/all_gather | solution.py:17
  49.6 92.1 %all-gather.6.cloned.1.call-done = f32[16,64,4096]{2,1,0:T(8,128)} async-done(((f32[1,64,4096]{2,1,0:T(8,128)}), f32[16,64,4096]{2,1,0:T(8,128)}) %all-gather.6.cloned.1.call-update) | async-done | bytes 16777232 | tf_op jit(solution)/shard_map/all_gather | solution.py:17
  143.0 72.3 %all-gather.10.cloned.1.call-done = f32[512,4096]{1,0:T(8,128)} async-done(((f32[64,4096]{1,0:T(8,128)}), f32[512,4096]{1,0:T(8,128)}) %all-gather.10.cloned.1.call-update) | async-done | bytes 8388624 | tf_op jit(solution)/shard_map/all_gather | solution.py:138
  215.3 4.3 broadcast_select_fusion
  222.5 3.0 copy.88
  225.5 4.3 copy.83
  232.3 4.7 multiply_bitcast_fusion
  237.0 126.9 %all-reduce.3.cloned.1.call-done = f32[8,64,4096]{2,1,0:T(8,128)} async-done(((f32[8,64,4096]{2,1,0:T(8,128)}), f32[8,64,4096]{2,1,0:T(8,128)}) %all-reduce.3.cloned.1.call-update) | async-done | bytes 8388624 | tf_op jit(solution)/shard_map/psum | solution.py:31
  363.9 4.4 multiply_reduce_fusion.2
  374.5 102.0 %while.68 = (s32[]{:T(128)}, bf16[8,256,8,64]{1,3,2,0:T(8,128)(2,1)}, bf16[8,256,64]{1,2,0:T(8,128)(2,1)S(1)}, bf16[8,256,64]{1,2,0:T(8,128)(2,1)}, f32[8,8,64,6...) while((s32[]{:T(128)}, ...), condition=%wide.region_12.13_spmd.clone, body=%wide.region_10.12_spmd.clone.sunk | while | flops 1163673600 | bytes 8757429 | solution.py:67
  384.5 2.7 fusion.152
  397.3 2.7 fusion.152
  410.0 2.7 fusion.152
  422.8 2.7 fusion.152
  431.4 2.4 multiply_reduce_fusion.5
  435.5 2.7 fusion.152
  448.3 2.7 fusion.152
  461.0 2.7 fusion.152
  473.8 2.7 fusion.152
  478.6 4.9 broadcast_multiply_fusion
  483.8 7.1 copy.82
  491.9 6.9 fusion.58
  504.8 30.5 %reduce-scatter.2.cloned.1.call-done = f32[1,64,4096]{2,1,0:T(8,128)} async-done(((f32[8,64,4096]{2,1,0:T(8,128)}), f32[1,64,4096]{2,1,0:T(8,128)}) %reduce-scatter.2.cloned.1.call-update) | async-done | bytes 1048592 | tf_op jit(solution)/shard_map/reduce_scatter | solution.py:162
  535.4 113.4 %all-gather.8.cloned.1.call-done = f32[16,64,4096]{2,1,0:T(8,128)} async-done(((f32[1,64,4096]{2,1,0:T(8,128)}), f32[16,64,4096]{2,1,0:T(8,128)}) %all-gather.8.cloned.1.call-update) | async-done | bytes 16777232 | tf_op jit(solution)/shard_map/all_gather | solution.py:17
  648.9 33.7 %while.67 = (s32[]{:T(128)}, f32[64]{0:T(128)S(1)}, f32[64,4096]{1,0:T(8,128)S(1)}, s32[]{:T(128)}, f32[16,64]{1,0:T(8,128)}, /*index=5*/f32[16,64,4096]{2,1,0:T(8,128)}, s32[]{:T(128)}, s32[]{:T(128)}, s32[]{:T(128)}, s32[]{:T(128)}) while((s32[]{:T(128)}, f32[64]{0:T(128)S(1)}, f32[64,4096]{1,0:T(8,128)S(1)}, s32[]{:T(128)}, ...), condition=%wide.region_3.4_spmd, body=%wide.region_2.3_spmd.sunk | while | flops 524358 | bytes 3147163 | solution.py:26
  684.8 4.1 copy.99
  690.5 48.3 %all-reduce.5.cloned.1.call-done = f32[64,4096]{1,0:T(8,128)} async-done(((f32[64,4096]{1,0:T(8,128)}), f32[64,4096]{1,0:T(8,128)}) %all-reduce.5.cloned.1.call-update) | async-done | bytes 1048592 | tf_op jit(solution)/shard_map/psum | solution.py:163
  742.4 2.5 broadcast_in_dim.199
  746.5 303.9 %while.69 = (s32[]{:T(128)}, bf16[8,512,8,64]{1,3,2,0:T(8,128)(2,1)}, bf16[8,512,64]{1,2,0:T(8,128)(2,1)}, bf16[8,512,64]{1,2,0:T(8,128)(2,1)}, f32[8,512,8,64]{...) while((s32[]{:T(128)}, ...), condition=%wide.region_17.18_spmd.clone, body=%wide.region_15.17_spmd.clone.sunk | while | flops 4453376000 | bytes 25018808 | solution.py:67
  757.6 10.4 multiply_reduce_fusion.6
  775.2 7.7 fusion.173
  795.5 10.4 multiply_reduce_fusion.6
  813.1 7.7 fusion.173
  833.5 10.4 multiply_reduce_fusion.6
  851.1 7.7 fusion.173
  871.5 10.4 multiply_reduce_fusion.6
  889.1 7.7 fusion.173
  909.5 10.4 multiply_reduce_fusion.6
  927.0 7.7 fusion.173
  947.4 10.4 multiply_reduce_fusion.6
  965.0 7.7 fusion.173
  985.4 10.4 multiply_reduce_fusion.6
  1003.0 7.7 fusion.173
  1023.3 10.4 multiply_reduce_fusion.6
  1040.9 7.7 fusion.173
  1050.5 6.4 copy.96
  (518 shorter events, 307.7 us)
Async XLA Ops:
  7.2 134.5 %all-gather.6.cloned.1.call-start = ((), (), s32[]{:S(2)}) async-start(), calls=%async_computation.1 | async-start | bytes 17825792 | tf_op jit(solution)/shard_map/all_gather | solution.py:17
  12.2 7.1 copy-start.9
  19.6 6.6 copy-start.3
  27.8 187.5 %all-gather.10.cloned.1.call-start = ((), (), s32[]{:S(2)}) async-start(), calls=%async_computation.6 | async-start | bytes 9437184 | tf_op jit(solution)/shard_map/all_gather | solution.py:138
  141.7 77.9 %copy-start.17 = (f32[16,64]{1,0:T(8,128)}, f32[16,64]{1,0:T(8,128)S(1)}, u32[]{:S(2)}) copy-start(f32[16,64]{1,0:T(8,128)S(1)} %get-tuple-element.1330) | copy-start | bytes 12292
  142.9 221.0 %all-reduce.3.cloned.1.call-start = ((), (), s32[]{:S(2)}) async-start(), calls=%async_computation.3 | async-start | bytes 16777216 | tf_op jit(solution)/shard_map/psum | solution.py:31
  219.6 315.7 %reduce-scatter.2.cloned.1.call-start = ((), (), s32[]{:S(2)}) async-start(), calls=%async_computation.4 | async-start | bytes 9437184 | tf_op jit(solution)/shard_map/reduce_scatter | solution.py:162
  225.5 4.3 copy-start.15
  225.5 4.5 copy-start.14
  230.1 133.8 %copy-start.19 = (f32[8]{0:T(128)}, f32[8]{0:T(128)S(1)}, u32[]{:S(2)}) copy-start(f32[8]{0:T(128)S(1)} %compare_convert_fusion.1) | copy-start | bytes 100
  483.5 7.3 copy-start.10
  483.6 8.3 copy-start.8
  483.6 165.2 %all-gather.8.cloned.1.call-start = ((), (), s32[]{:S(2)}) async-start(), calls=%async_computation.2 | async-start | bytes 17825792 | tf_op jit(solution)/shard_map/all_gather | solution.py:17
  500.5 238.3 %all-reduce.5.cloned.1.call-start = ((), (), s32[]{:S(2)}) async-start(), calls=%async_computation.5 | async-start | bytes 2097152 | tf_op jit(solution)/shard_map/psum | solution.py:163
  682.6 7.1 copy-start.7
  756.9 11.2 %copy-start.11 = (f32[8,512]{1,0:T(8,128)}, f32[8,512]{1,0:T(8,128)S(1)}, u32[]{:S(2)}) copy-start(f32[8,512]{1,0:T(8,128)S(1)} %copy.143) | copy-start | bytes 49156 | tf_op jit(solution)/shard_map/transpose(jvp())/while
  757.6 10.5 copy-start.1
  775.1 7.7 copy-start
  794.8 11.2 %copy-start.11 = (f32[8,512]{1,0:T(8,128)}, f32[8,512]{1,0:T(8,128)S(1)}, u32[]{:S(2)}) copy-start(f32[8,512]{1,0:T(8,128)S(1)} %copy.143) | copy-start | bytes 49156 | tf_op jit(solution)/shard_map/transpose(jvp())/while
  795.5 10.5 copy-start.1
  808.8 4.3 copy-start.13
  813.1 7.7 copy-start
  832.8 11.2 %copy-start.11 = (f32[8,512]{1,0:T(8,128)}, f32[8,512]{1,0:T(8,128)S(1)}, u32[]{:S(2)}) copy-start(f32[8,512]{1,0:T(8,128)S(1)} %copy.143) | copy-start | bytes 49156 | tf_op jit(solution)/shard_map/transpose(jvp())/while
  833.5 10.5 copy-start.1
  846.8 4.3 copy-start.13
  851.1 7.7 copy-start
  870.8 11.2 %copy-start.11 = (f32[8,512]{1,0:T(8,128)}, f32[8,512]{1,0:T(8,128)S(1)}, u32[]{:S(2)}) copy-start(f32[8,512]{1,0:T(8,128)S(1)} %copy.143) | copy-start | bytes 49156 | tf_op jit(solution)/shard_map/transpose(jvp())/while
  871.5 10.5 copy-start.1
  884.8 4.3 copy-start.13
  889.1 7.7 copy-start
  908.7 11.2 %copy-start.11 = (f32[8,512]{1,0:T(8,128)}, f32[8,512]{1,0:T(8,128)S(1)}, u32[]{:S(2)}) copy-start(f32[8,512]{1,0:T(8,128)S(1)} %copy.143) | copy-start | bytes 49156 | tf_op jit(solution)/shard_map/transpose(jvp())/while
  909.5 10.5 copy-start.1
  922.7 4.3 copy-start.13
  927.0 7.7 copy-start
  946.7 11.2 %copy-start.11 = (f32[8,512]{1,0:T(8,128)}, f32[8,512]{1,0:T(8,128)S(1)}, u32[]{:S(2)}) copy-start(f32[8,512]{1,0:T(8,128)S(1)} %copy.143) | copy-start | bytes 49156 | tf_op jit(solution)/shard_map/transpose(jvp())/while
  947.4 10.5 copy-start.1
  960.7 4.3 copy-start.13
  965.0 7.7 copy-start
  984.7 11.2 %copy-start.11 = (f32[8,512]{1,0:T(8,128)}, f32[8,512]{1,0:T(8,128)S(1)}, u32[]{:S(2)}) copy-start(f32[8,512]{1,0:T(8,128)S(1)} %copy.143) | copy-start | bytes 49156 | tf_op jit(solution)/shard_map/transpose(jvp())/while
  985.4 10.5 copy-start.1
  998.7 4.3 copy-start.13
  1002.9 7.7 copy-start
  1022.6 11.2 %copy-start.11 = (f32[8,512]{1,0:T(8,128)}, f32[8,512]{1,0:T(8,128)S(1)}, u32[]{:S(2)}) copy-start(f32[8,512]{1,0:T(8,128)S(1)} %copy.143) | copy-start | bytes 49156 | tf_op jit(solution)/shard_map/transpose(jvp())/while
  1023.3 10.5 copy-start.1
  1036.6 4.3 copy-start.13
  1040.9 7.7 copy-start
  1050.5 6.4 copy-start.5
  1050.5 7.4 copy-start.6
  (20 other events, 79.4 us)
Sparse Core Ops, SparseCore 0:
  28.0 113.6 all-gather.5
  143.9 71.3 all-gather.9
  219.8 144.1 all-reduce.2
  483.7 51.6 reduce-scatter.1
  538.1 110.6 all-gather.7
  652.2 86.5 all-reduce.4
where the time goes:
time: 1080 us; the launch traced here: 1070 us
  waiting for transfers between devices  484 us (45%)
  matrix products  302 us (28%)
  local copies, waits for them, and re-layouts  161 us (15%)
  other arithmetic  78.8 us (7%)
  blocking collectives  21 us (2%)
  between operations  16 us (1%)
    all_gather x2, waiting for transfers between devices, prefix(): gathered = jax.tree.map(lambda a: lax.all_gather(a, axis), part)  205 us
    dot_general x32, matrix products, one_group(): output = jnp.einsum('hts,shp->thp', weights, x_one, precision=highest)  186 us
    psum x1, waiting for transfers between devices, broadcast(): return lax.psum(block, axis)  127 us
    all_gather x1, waiting for transfers between devices, local(): row_all = lax.all_gather(closing[None], 'leaf', axis=0, tiled=True)  72.3 us
    dynamic_slice x96, local copies, waits for them, and re-layouts, segment(): lax.map(jax.checkpoint(one_group), (x_groups, b_groups, c_groups, cum_gro...  48.9 us
    psum x1, waiting for transfers between devices, local(): total = lax.psum(partial_sum[0], 'seq')  48.3 us
    dot_general x48, matrix products, one_group(): scores = jnp.dot(c_one, b_one.T, precision=highest)  46.9 us
    squeeze x40, local copies, waits for them, and re-layouts, segment(): lax.map(jax.checkpoint(one_group), (x_groups, b_groups, c_groups, cum_gro...  38 us
  transfers between devices with their start and end apart: 6, of which 6 were waited for; matrix products, arithmetic and copies ran while one was open for 7% of the time, Pallas kernels for 0%

commit v1 on v0

v1 whole, which is shorter than its diff:
```python
import functools
import math

import jax
import jax.numpy as jnp
from jax import lax
from jax.experimental import pallas as pl
from jax.experimental.pallas import tpu as pltpu
from jax.sharding import PartitionSpec as P

P_SIZE = 64
N = 64
CH = 128
LOG2E = math.log2(math.e)
F32 = jnp.float32
BF16 = jnp.bfloat16
ROWS = 200
HIGHEST = lax.Precision.HIGHEST


def split(value):
    hi = value.astype(BF16)
    return hi, (value - hi.astype(F32)).astype(BF16)


def dot(a, b, ca, cb):
    return lax.dot_general(a, b, (((ca,), (cb,)), ((), ())), preferred_element_type=F32)


def halves(rows):
    return lax.broadcasted_iota(jnp.int32, (rows, 128), 1) < 64


def summary_kernel(
    x_ref, dy_ref, b_ref, c_ref, wt_ref, et_ref, ydy_ref, yc_ref, yet_ref, row_ref, out_ref
):
    first = halves(64)

    def one(proj, weight_ref, value_ref, base):
        proj_t = proj.astype(F32).T
        for k in range(8):
            part = proj_t[(k // 4) * 64 : (k // 4) * 64 + 64]
            h0, l0 = split(part * weight_ref[2 * k : 2 * k + 1, :])
            h1, l1 = split(part * weight_ref[2 * k + 1 : 2 * k + 2, :])
            lhs = jnp.concatenate([h0, l0, h1, l1], axis=0)
            res = dot(lhs, value_ref[:, k * 128 : (k + 1) * 128], 1, 0)
            pair = jnp.where(first, res[0:64] + res[64:128], res[128:192] + res[192:256])
            lanes = slice((k % 2) * 128, (k % 2) * 128 + 128)
            out_ref[k // 2, base : base + 64, lanes] = pair

    one(b_ref[...], wt_ref, x_ref, 0)
    one(c_ref[...], et_ref, dy_ref, 64)
    one(yc_ref[...], yet_ref, ydy_ref, 128)
    out_ref[:, 192:200, :] = row_ref[...]


def summaries(x, dy, b, c, wt, et, ydy, yc, yet, rows):
    length, width = x.shape
    ylen = ydy.shape[0]
    steps = width // 1024

    def cols(n, w):
        return pl.BlockSpec((n, w), lambda i: (0, i))

    def heads(n):
        return pl.BlockSpec((16, n), lambda i: (i, 0))

    return pl.pallas_call(
        summary_kernel,
        grid=(steps,),
        out_shape=jax.ShapeDtypeStruct((16, ROWS, 256), F32),
        in_specs=[
            cols(length, 1024),
            cols(length, 1024),
            cols(length, 128),
            cols(length, 128),
            heads(length),
            heads(length),
            cols(ylen, 1024),
            cols(ylen, 128),
            heads(ylen),
            pl.BlockSpec((4, 8, 256), lambda i: (i, 0, 0)),
        ],
        out_specs=pl.BlockSpec((4, ROWS, 256), lambda i: (i, 0, 0)),
        compiler_params=pltpu.CompilerParams(vmem_limit_bytes=40 * 2**20),
        name="summaries",
    )(x, dy, b, c, wt, et, ydy, yc, yet, rows)


def forward_kernel(core_ref, got_ref, init_ref, end_ref, keep_ref, send_ref):
    core = core_ref[0].astype(F32)
    state = jnp.zeros((64, 256), F32)
    for i in range(16):
        init_ref[i] = state
        state = got_ref[i, 192:193, :] * state + got_ref[i, 0:64, :]
    end_ref[...] = state
    for z in range(4):
        keep = jnp.zeros((64, 256), F32)
        send = jnp.zeros((64, 256), F32)
        for i in range(16):
            owner = got_ref[i, 193:194, :] - 2.0 * z
            term = got_ref[i, 128:192, :]
            keep = keep + jnp.where(owner == core, term, 0.0)
            send = send + jnp.where(owner == 1.0 - core, term, 0.0)
        keep_ref[z] = keep
        send_ref[z] = send


def forward(core, got):
    full = lambda *s: jax.ShapeDtypeStruct(s, F32)
    return pl.pallas_call(
        forward_kernel,
        out_shape=(full(16, 64, 256), full(64, 256), full(4, 64, 256), full(4, 64, 256)),
        in_specs=[pl.BlockSpec(memory_space=pltpu.SMEM), pl.BlockSpec(memory_space=pltpu.VMEM)],
        out_specs=(pl.BlockSpec(memory_space=pltpu.VMEM),) * 4,
        compiler_params=pltpu.CompilerParams(vmem_limit_bytes=40 * 2**20),
        name="forward_scan",
    )(core, got)


def pack_kernel(place_ref, end_ref, keep_ref, recv_ref, m1_ref, m2_ref, m3_ref, own_ref):
    z = place_ref[0]
    own_ref[...] = keep_ref[z] + recv_ref[z]
    for d, ref in ((1, m1_ref), (2, m2_ref), (3, m3_ref)):
        to = lax.rem(z + d, 4)
        ref[0:64] = end_ref[...]
        ref[64:128] = keep_ref[to] + recv_ref[to]


def pack(place, end, keep, recv):
    vmem = pl.BlockSpec(memory_space=pltpu.VMEM)
    msg = jax.ShapeDtypeStruct((128, 256), F32)
    return pl.pallas_call(
        pack_kernel,
        out_shape=(msg, msg, msg, jax.ShapeDtypeStruct((64, 256), F32)),
        in_specs=[pl.BlockSpec(memory_space=pltpu.SMEM)] + [vmem] * 3,
        out_specs=(vmem,) * 4,
        name="pack_leaf",
    )(place, end, keep, recv)


def backward_kernel(
    place_ref, got_ref, init_ref, end_ref, own_ref, r1, r2, r3, s0, s1, s2, s3, out_ref
):
    z = place_ref[0]
    core = place_ref[1]
    grad = own_ref[...] + r1[64:128] + r2[64:128] + r3[64:128]
    for i in range(15, -1, -1):
        out_ref[i, 64:128, :] = grad
        grad = got_ref[i, 192:193, :] * grad + got_ref[i, 64:128, :]
    mine = (end_ref, r1, r2, r3)
    theirs = (s0, s1, s2, s3)
    for i in range(16):
        out_ref[i, 0:64, :] = init_ref[i]
        owner = got_ref[i, 193:194, :]
        start = jnp.zeros((64, 256), F32)
        for d in range(4):
            place = 2 * lax.rem(z + 4 - d, 4)
            here = (place + core).astype(F32)
            there = (place + 1 - core).astype(F32)
            start = start + jnp.where(owner == here, mine[d][0:64], 0.0)
            start = start + jnp.where(owner == there, theirs[d][0:64], 0.0)
        out_ref[i, 128:192, :] = start


def backward(place, got, init, end, own, received, swapped):
    vmem = pl.BlockSpec(memory_space=pltpu.VMEM)
    return pl.pallas_call(
        backward_kernel,
        out_shape=jax.ShapeDtypeStruct((16, 192, 256), F32),
        in_specs=[pl.BlockSpec(memory_space=pltpu.SMEM)] + [vmem] * 11,
        out_specs=vmem,
        compiler_params=pltpu.CompilerParams(vmem_limit_bytes=40 * 2**20),
        name="backward_scan",
    )(place, got, init, end, own, *received, *swapped)


def gradient_kernel(
    chunks,
    init_at,
    grad_at,
    x_ref,
    dy_ref,
    b_ref,
    c_ref,
    cum_ref,
    rate_ref,
    cumt_ref,
    last_ref,
    state_ref,
    dx_ref,
    db_ref,
    dc_ref,
    xh,
    xl,
    yh,
    yl,
    weight,
    carry,
    dci,
    dbo,
    dco,
):
    first = halves(CH)
    causal = lax.broadcasted_iota(jnp.int32, (CH, CH), 1) >= lax.broadcasted_iota(
        jnp.int32, (CH, CH), 0
    )

    def spread(ref, rows, head):
        return jnp.broadcast_to(ref[0, rows, head : head + 1], (CH, 128))

    for g in range(2):
        gcol = g * 512
        pcol = slice(g * 64, g * 64 + 64)

        def start_state(base):
            return jnp.concatenate(
                [state_ref[2 * g, base : base + 64, :], state_ref[2 * g + 1, base : base + 64, :]],
                axis=1,
            )

        def ahead(c, state):
            rows = pl.ds(pl.multiple_of(c * CH, CH), CH)
            for k in range(4):
                head = g * 8 + 2 * k
                lanes = slice(gcol + k * 128, gcol + k * 128 + 128)
                here = slice(k * 128, k * 128 + 128)
                cum = jnp.where(first, spread(cum_ref, rows, head), spread(cum_ref, rows, head + 1))
                rate = jnp.where(
                    first, spread(rate_ref, rows, head), spread(rate_ref, rows, head + 1)
                )
                w = rate * jnp.exp2(last_ref[c, :, lanes] - cum)
                weight[c, :, here] = w
                hi, lo = split(w * x_ref[rows, lanes].astype(F32))
                xh[c, :, here] = hi
                xl[c, :, here] = lo
                hi, lo = split(jnp.exp2(cum) * dy_ref[rows, lanes].astype(F32))
                yh[c, :, here] = hi
                yl[c, :, here] = lo
            b_one = b_ref[rows, pcol]
            c_one = c_ref[rows, pcol]
            added = dot(b_one, xh[c], 0, 0) + dot(b_one, xl[c], 0, 0)
            carry[c] = dot(c_one, yh[c], 0, 0) + dot(c_one, yl[c], 0, 0)
            hi, lo = split(state)
            res = dot(yh[c], jnp.concatenate([hi, lo], axis=0), 1, 1)
            dci[c] = res[:, 0:64] + res[:, 64:128] + dot(yl[c], hi, 1, 1)
            return jnp.exp2(last_ref[c, :, gcol : gcol + 512]) * state + added

        lax.fori_loop(0, chunks, ahead, start_state(init_at))

        def back(step, grad):
            c = chunks - 1 - step
            rows = pl.ds(pl.multiple_of(c * CH, CH), CH)
            b_one = b_ref[rows, pcol]
            c_one = c_ref[rows, pcol]
            ghi, glo = split(grad)
            both = jnp.concatenate([ghi, glo], axis=0)
            dxi = dot(jnp.concatenate([b_one, b_one], axis=1), both, 1, 0) * weight[c]
            res = dot(xh[c], both, 1, 1)
            db = res[:, 0:64] + res[:, 64:128] + dot(xl[c], ghi, 1, 1)
            scores = dot(b_one, c_one, 1, 1)
            total = jnp.zeros((CH, CH), F32)
            for k in range(4):
                lanes = slice(gcol + k * 128, gcol + k * 128 + 128)
                dy = dy_ref[rows, lanes]
                zero = jnp.zeros_like(dy)
                stacked = jnp.concatenate(
                    [jnp.where(first, dy, zero), jnp.where(first, zero, dy)], axis=0
                )
                pairs = dot(x_ref[rows, lanes], stacked, 1, 1)
                his, los = [], []
                for e in range(2):
                    head = g * 8 + 2 * k + e
                    cum_t = cumt_ref[0, c, head : head + 1, :]
                    gap = jnp.where(causal, cum_t - spread(cum_ref, rows, head), -jnp.inf)
                    decay = jnp.exp2(gap) * spread(rate_ref, rows, head)
                    total = total + decay * pairs[:, e * 128 : e * 128 + 128]
                    hi, lo = split(decay * scores)
                    his.append(hi)
                    los.append(lo)
                lhs = jnp.concatenate(
                    [jnp.concatenate(his, axis=1), jnp.concatenate(los, axis=1)], axis=0
                )
                res = dot(lhs, stacked, 1, 0)
                dx = res[0:CH] + res[CH : 2 * CH] + dxi[:, k * 128 : k * 128 + 128]
                dx_ref[rows, lanes] = dx.astype(BF16)
            hi, lo = split(total)
            db = db + dot(hi, c_one, 1, 0) + dot(lo, c_one, 1, 0)
            dc = dci[c] + dot(hi, b_one, 0, 0) + dot(lo, b_one, 0, 0)
            dbo[g, rows, :] = db
            dco[g, rows, :] = dc
            return jnp.exp2(last_ref[c, :, gcol : gcol + 512]) * grad + carry[c]

        if grad_at is None:
            grad = jnp.zeros((64, 512), F32)
        else:
            grad = start_state(grad_at)
        lax.fori_loop(0, chunks, back, grad)
    db_ref[...] = jnp.concatenate([dbo[0], dbo[1]], axis=1).astype(BF16)
    dc_ref[...] = jnp.concatenate([dco[0], dco[1]], axis=1).astype(BF16)


def gradients(x, dy, b, c, cum, rate, cumt, last, states, init_at, grad_at, name):
    length, width = x.shape
    chunks = length // CH
    steps = width // 1024

    def cols(w):
        return pl.BlockSpec((length, w), lambda i: (0, i))

    def scratch(*shape, dtype=F32):
        return pltpu.VMEM(shape, dtype)

    return pl.pallas_call(
        functools.partial(gradient_kernel, chunks, init_at, grad_at),
        grid=(steps,),
        out_shape=(
            jax.ShapeDtypeStruct(x.shape, BF16),
            jax.ShapeDtypeStruct(b.shape, BF16),
            jax.ShapeDtypeStruct(c.shape, BF16),
        ),
        in_specs=[
            cols(1024),
            cols(1024),
            cols(128),
            cols(128),
            pl.BlockSpec((1, length, 16), lambda i: (i, 0, 0)),
            pl.BlockSpec((1, length, 16), lambda i: (i, 0, 0)),
            pl.BlockSpec((1, chunks, 16, CH), lambda i: (i, 0, 0, 0)),
            pl.BlockSpec((chunks, 1, 1024), lambda i: (0, 0, i)),
            pl.BlockSpec((4, 192, 256), lambda i: (i, 0, 0)),
        ],
        out_specs=(cols(1024), cols(128), cols(128)),
        scratch_shapes=[
            scratch(chunks, CH, 512, dtype=BF16),
            scratch(chunks, CH, 512, dtype=BF16),
            scratch(chunks, CH, 512, dtype=BF16),
            scratch(chunks, CH, 512, dtype=BF16),
            scratch(chunks, CH, 512),
            scratch(chunks, 64, 512),
            scratch(chunks, CH, 64),
            scratch(2, length, 64),
            scratch(2, length, 64),
        ],
        compiler_params=pltpu.CompilerParams(vmem_limit_bytes=48 * 2**20),
        name=name,
    )(x, dy, b, c, cum, rate, cumt, last, states)


def rates(step_rates, head_rate):
    length, heads = step_rates.shape
    chunks = length // CH
    logs = (-step_rates * head_rate[None, :]) * LOG2E
    lower = jnp.tril(jnp.ones((CH, CH), F32))
    cum = jnp.einsum("ts,csh->cth", lower, logs.reshape(chunks, CH, heads), precision=HIGHEST)
    last = cum[:, -1]
    by_step = lambda a: a.reshape(length, heads // 16, 16).transpose(1, 0, 2)
    cumt = cum.transpose(0, 2, 1)
    ends = jnp.cumsum(last, axis=0)
    whole = (cumt + (ends - last)[:, :, None]).transpose(1, 0, 2).reshape(heads, length)
    return dict(
        cum=by_step(cum.reshape(length, heads)),
        rate=by_step(step_rates),
        cumt=cumt.reshape(chunks, heads // 16, 16, CH).transpose(1, 0, 2, 3),
        last=jnp.repeat(last, P_SIZE, axis=1)[:, None, :],
        whole=whole,
        end=ends[-1],
    )


def local(
    prompt_x,
    prompt_dt,
    head_rate,
    prompt_b,
    prompt_c,
    prompt_dy,
    branch_x,
    branch_dt,
    branch_b,
    branch_c,
    branch_dy,
    parent,
    lengths,
):
    leaf = lax.axis_index("leaf")
    z, core = leaf // 2, leaf % 2
    place = jnp.stack([z, core]).astype(jnp.int32)
    slots = branch_x.shape[1]
    live = jnp.arange(slots) < lengths[0]
    branch_rates = branch_dt[0] * live[:, None].astype(F32)
    branch_grad = jnp.where(live[:, None], branch_dy[0], jnp.zeros((), BF16))
    pr = rates(prompt_dt[0], head_rate)
    br = rates(branch_rates, head_rate)
    wt = prompt_dt[0].T * jnp.exp2(pr["end"][:, None] - pr["whole"])
    rows = jnp.concatenate(
        [
            jnp.repeat(jnp.exp2(pr["end"]), P_SIZE).reshape(16, 1, 256),
            jnp.broadcast_to(parent[0].astype(F32), (16, 7, 256)),
        ],
        axis=1,
    )
    sent = summaries(
        prompt_x[0],
        prompt_dy[0],
        prompt_b[0],
        prompt_c[0],
        wt,
        jnp.exp2(pr["whole"]),
        branch_grad,
        branch_c[0],
        jnp.exp2(br["whole"]),
        rows,
    )
    got = lax.all_to_all(sent, "seq", 0, 0, tiled=True)
    init, end, keep, send = forward(place[1:], got)
    swap = [(s, s ^ 1) for s in range(8)]
    recv = lax.ppermute(send, "leaf", swap)
    m1, m2, m3, own = pack(place, end, keep, recv)
    received = [
        lax.ppermute(m, "leaf", [(s, (s + 2 * d) % 8) for s in range(8)])
        for d, m in ((1, m1), (2, m2), (3, m3))
    ]
    swapped = [lax.ppermute(m, "leaf", swap) for m in [end] + [m[0:64] for m in received]]
    back = backward(place, got, init, end, own, received, swapped)
    states = lax.all_to_all(back, "seq", 0, 0, tiled=True)
    py = gradients(
        prompt_x[0],
        prompt_dy[0],
        prompt_b[0],
        prompt_c[0],
        pr["cum"],
        pr["rate"],
        pr["cumt"],
        pr["last"],
        states,
        0,
        64,
        "prompt_gradients",
    )
    by = gradients(
        branch_x[0],
        branch_grad,
        branch_b[0],
        branch_c[0],
        br["cum"],
        br["rate"],
        br["cumt"],
        br["last"],
        states,
        128,
        None,
        "branch_gradients",
    )
    return tuple(a[None] for a in py + by)


def solution(mesh):
    seq = P("leaf", "seq", None)
    own = P(("seq", "leaf"), None, None)
    ids = P(("seq", "leaf"))
    in_specs = (seq, seq, P(), seq, seq, seq, own, own, own, own, own, ids, ids)
    out_specs = (seq, seq, seq, own, own, own)
    return jax.shard_map(local, mesh=mesh, in_specs=in_specs, out_specs=out_specs, check_vma=False)
```

time: 1080 us -> 241 us (0.22)
  waiting for transfers between devices: 484 us -> 88.7 us
  matrix products: 302 us -> 1.93 us
  local copies, waits for them, and re-layouts: 161 us -> 19.5 us
  Pallas kernels: 0 us -> 94.3 us
  other arithmetic: 78.8 us -> 6.05 us
  starting transfers between devices: 0.88 us -> 23 us
  blocking collectives: 21 us -> 0 us
  between operations: 16 us -> 2.53 us
    dot_general x122 -> x2, matrix products: 302 us -> 1.93 us  [rates(): jnp.einsum('ts,csh->cth', lower, logs.reshape(chunks, CH, heads), precisi...]
    all_gather x3 -> x0, waiting for transfers between devices: 278 us -> none  [the longest x2 205 us: prefix(): gathered = jax.tree.map(lambda a: lax.all_gather(a, axis), part)]
    psum x2 -> x0, waiting for transfers between devices: 175 us -> none  [the longest x1 127 us: broadcast(): return lax.psum(block, axis)]
    pallas_call x0 -> x6, Pallas kernels: none -> 94.3 us  [the longest x2 81.5 us: gradients(): pl.pallas_call(functools.partial(gradient_kernel, chunks, init_at, grad_a...]
    all_to_all x0 -> x2, waiting for transfers between devices: none -> 81 us  [the longest x1 43.9 us: local(): got = lax.all_to_all(sent, 'seq', 0, 0, tiled=True)]
    dynamic_slice x96 -> x0, local copies, waits for them, and re-layouts: 48.9 us -> none  [segment(): lax.map(jax.checkpoint(one_group), (x_groups, b_groups, c_groups, cum_gro...]
    squeeze x40 -> x2, local copies, waits for them, and re-layouts: 38 us -> 1.87 us  [local(): branch_rates = branch_dt[0] * live[:, None].astype(F32)]
    reduce_scatter x1 -> x0, waiting for transfers between devices: 30.5 us -> none  [local(): lax.psum_scatter(term, 'leaf', scatter_dimension=0, tiled=True)]
  transfers between devices with their start and end apart: 6 -> 10, of which waited for: 6 -> 7; matrix products, arithmetic and copies ran while one was open for 7% -> 3% of each run, Pallas kernels for 0% -> 0%
where the time goes in v1:
time: 241 us; the launch traced here: 236 us
  Pallas kernels  94.3 us (39%)
  waiting for transfers between devices  88.7 us (37%)
  starting transfers between devices  23 us (10%)
  local copies, waits for them, and re-layouts  19.5 us (8%)
  other arithmetic  6.05 us (3%)
  between operations  2.53 us (1%)
    pallas_call x2, Pallas kernels, gradients(): pl.pallas_call(functools.partial(gradient_kernel, chunks, init_at, grad_a...  81.5 us
    all_to_all x1, waiting for transfers between devices, local(): got = lax.all_to_all(sent, 'seq', 0, 0, tiled=True)  43.9 us
    all_to_all x1, waiting for transfers between devices, local(): states = lax.all_to_all(back, 'seq', 0, 0, tiled=True)  37.1 us
    unnamed x56, local copies, waits for them, and re-layouts  13.5 us
    all_to_all x1, starting transfers between devices, local(): states = lax.all_to_all(back, 'seq', 0, 0, tiled=True)  8.8 us
    pallas_call x1, Pallas kernels, summaries(): pl.pallas_call(summary_kernel, grid=(steps,), out_shape=jax.ShapeDtypeStr...  8.45 us
    all_to_all x1, starting transfers between devices, local(): got = lax.all_to_all(sent, 'seq', 0, 0, tiled=True)  7.12 us
    ppermute x3, starting transfers between devices, local(): lax.ppermute(m, 'leaf', [(s, (s + 2 * d) % 8) for s in range(8)])  6.52 us
  transfers between devices with their start and end apart: 10, of which 7 were waited for; matrix products, arithmetic and copies ran while one was open for 3% of the time, Pallas kernels for 0%

profile of v1, /device:TPU:0, one launch (start us, length us, event | category | flops | bytes accessed | tf_op | source)
XLA Modules:
  0.0 236.0 jit_solution(12663051109865909422)
XLA Ops:
  0.7 1.0 neg.11
  1.7 1.0 fusion.6
  2.7 0.2 slice_reduce_fusion
  3.7 0.9 squeeze.56
  4.5 1.0 fusion.11
  6.9 1.2 fusion.3
  8.1 1.8 bitcast_select_fusion.ydy_ref.dy_ref
  10.0 8.4 %summaries.1 = f32[16,200,256]{2,1,0:T(8,128)S(1)} custom-call(bf16[512,4096]{1,0:T(8,128)(2,1)S(1)} %bitcast.96, bf16[512,4096]{1,0:T(8,128)(2,1)} %bitcast.110, bf16[512,512]{1,0:T(8,128)(2,1)S(1)} %bitcast.101, bf16[512,512]{1,0:T(8,128)(2,1)S(1)} %bitcast.103, f32[64,512]{1,0:T(8,128)S(1)} %get-tuple-element.35.wt_ref, ...), custom_call_target="tpu_custom_call" | custom-call | tf_op jit(solution)/shard_map/summaries/pallas_call | solution.py:68
  18.5 1.3 copy-done
  19.8 1.7 copy-done.3
  21.5 7.1 %all-to-all-start = ((f32[16,200,256]{2,1,0:T(8,128)}), f32[16,200,256]{2,1,0:T(8,128)S(1)}, u32[]{:S(2)}, u32[]{:S(2)}) async-start(f32[16,200,256]{2,1,0:T(8,128)} %copy-done.3), calls=%async_computation | async-start | bytes 6553600 | tf_op jit(solution)/shard_map/all_to_all | solution.py:415
  28.6 43.9 %all-to-all-done.got_ref = f32[16,200,256]{2,1,0:T(8,128)S(1)} async-done(((f32[16,200,256]{2,1,0:T(8,128)}), f32[16,200,256]{2,1,0:T(8,128)S(1)}, u32[]{:S(2)}, u32[]{:S(2)}) %all-to-all-start) | async-done | bytes 3276832 | tf_op jit(solution)/shard_map/all_to_all | solution.py:415
  72.6 1.2 forward_scan.1
  73.8 1.0 copy-done.11
  74.8 0.6 copy-done.15
  75.4 0.7 copy-done.18
  76.1 0.7 pad_add_fusion.place_ref
  76.7 1.2 collective-permute-done.recv_ref
  78.0 1.9 pack_leaf.1
  79.8 1.9 collective-permute-start.1
  81.8 3.6 %collective-permute-start.2 = (f32[128,256]{1,0:T(8,128)}, f32[128,256]{1,0:T(8,128)S(1)}, u32[]{:S(2)}, u32[]{:S(2)}) collective-permute-start(f32[128,256]{1,0:T(8,128)} %get-tuple-element.26), channel_id=1, source_target_pairs={{0,4},{1,5},{2,6},{3,7},{4,0},{5,1},{6,2},{7,3},{8,12},{9,13},{10,... | collective-permute-start | bytes 393224 | tf_op jit(solution)/shard_map/ppermute | solution.py:421
  85.3 1.0 collective-permute-start.3
  86.3 1.5 collective-permute-done.1.r1
  87.9 4.0 %collective-permute-done.2.r2 = f32[128,256]{1,0:T(8,128)S(1)} collective-permute-done((f32[128,256]{1,0:T(8,128)}, f32[128,256]{1,0:T(8,128)S(1)}, u32[]{:S(2)}, u32[]{:S(2)}) %collective-permute-start.2) | collective-permute-done | bytes 131104 | tf_op jit(solution)/shard_map/ppermute | solution.py:421
  91.9 0.6 collective-permute-start.7
  92.5 0.6 collective-permute-done.6.s2
  93.1 0.2 collective-permute-done.7.s3
  93.4 1.2 copy-done.12
  94.6 0.8 copy-done.16
  95.4 0.8 copy-done.20
  96.3 0.7 copy-done.21
  97.0 1.3 backward_scan.1
  98.3 1.7 copy-done.4
  99.9 8.8 %all-to-all-start.1 = ((f32[16,192,256]{2,1,0:T(8,128)}), f32[16,192,256]{2,1,0:T(8,128)}, u32[]{:S(2)}, u32[]{:S(2)}) async-start(f32[16,192,256]{2,1,0:T(8,128)} %copy-done.4), calls=%async_computation.1 | async-start | bytes 6291456 | tf_op jit(solution)/shard_map/all_to_all | solution.py:426
  109.0 0.7 broadcast_in_dim_reshape.7.last_ref
  109.8 0.2 copy.44
  110.0 0.6 copy.68
  110.6 1.0 copy.45
  111.7 0.8 broadcast_in_dim_reshape.6.last_ref
  112.6 0.3 copy.37
  112.9 0.3 copy.38
  113.3 1.1 multiply_bitcast_fusion.rate_ref
  114.4 37.1 %all-to-all-done.1.state_ref = f32[16,192,256]{2,1,0:T(8,128)} async-done(((f32[16,192,256]{2,1,0:T(8,128)}), f32[16,192,256]{2,1,0:T(8,128)}, u32[]{:S(2)}, u32[]{:S(2)}) %all-to-all-start.1) | async-done | bytes 3145760 | tf_op jit(solution)/shard_map/all_to_all | solution.py:426
  151.5 1.0 copy-done.7
  152.6 1.0 copy-done.9
  153.6 0.8 copy-done.13
  154.5 53.7 %prompt_gradients.1 = (bf16[512,4096]{1,0:T(8,128)(2,1)}, bf16[512,512]{1,0:T(8,128)(2,1)}, bf16[512,512]{1,0:T(8,128)(2,1)}) custom-call(bf16[512,4096]{1,0:T(8,128)(2,1)} %bitcast.95, bf16[512,4096]{1,0:T(8,128)(2,1)} %bitcast.111, bf16[512,512]{1,0:T(8,128)(2,1)S(1)} %bitcast.102, bf16[512,512]{1,0:T(8,128)(2,1)S(1)} %bitcast.104, ...), custom_call_target="tpu_custom_call" | custom-call | tf_op jit(solution)/shard_map/prompt_gradients/pallas_call | solution.py:314
  208.2 27.8 %branch_gradients.1 = (bf16[256,4096]{1,0:T(8,128)(2,1)}, bf16[256,512]{1,0:T(8,128)(2,1)}, bf16[256,512]{1,0:T(8,128)(2,1)}) custom-call(bf16[256,4096]{1,0:T(8,128)(2,1)S(1)} %bitcast.99, bf16[256,4096]{1,0:T(8,128)(2,1)S(1)} %copy-done.1, bf16[256,512]{1,0:T(8,128)(2,1)S(1)} %bitcast.109, bf16[256,512]{1,0:T(8,128)(2,1)S(1)} %bitcast.106, ...), custom_call_target="tpu_custom_call" | custom-call | tf_op jit(solution)/shard_map/branch_gradients/pallas_call | solution.py:314
  (75 shorter events, 1.3 us)
Async XLA Ops:
  0.6 9.3 %copy-start.6 = (bf16[1,512,512]{2,1,0:T(8,128)(2,1)S(1)}, bf16[1,512,512]{2,1,0:T(8,128)(2,1)}, u32[]{:S(2)}) copy-start(bf16[1,512,512]{2,1,0:T(8,128)(2,1)} %param.16) | copy-start | bytes 1572868
  0.6 9.3 %copy-start.10 = (bf16[1,256,512]{2,1,0:T(8,128)(2,1)S(1)}, bf16[1,256,512]{2,1,0:T(8,128)(2,1)}, u32[]{:S(2)}) copy-start(bf16[1,256,512]{2,1,0:T(8,128)(2,1)} %param.22) | copy-start | bytes 786436
  0.7 9.3 %copy-start.8 = (bf16[1,512,512]{2,1,0:T(8,128)(2,1)S(1)}, bf16[1,512,512]{2,1,0:T(8,128)(2,1)}, u32[]{:S(2)}) copy-start(bf16[1,512,512]{2,1,0:T(8,128)(2,1)} %param.17) | copy-start | bytes 1572868
  2.7 15.7 %copy-start.22 = (f32[4,64,128]{2,1,0:T(8,128)}, f32[4,64,128]{2,1,0:T(8,128)S(1)}, u32[]{:S(2)}) copy-start(f32[4,64,128]{2,1,0:T(8,128)S(1)} %fusion.6) | copy-start | bytes 393220
  5.5 13.0 %copy-start.25 = (f32[2,64,128]{2,1,0:T(8,128)}, f32[2,64,128]{2,1,0:T(8,128)S(1)}, u32[]{:S(2)}) copy-start(f32[2,64,128]{2,1,0:T(8,128)S(1)} %fusion.11) | copy-start | bytes 196612
  6.1 3.9 %copy-start.2 = (bf16[1,512,4096]{2,1,0:T(8,128)(2,1)S(1)}, bf16[1,512,4096]{2,1,0:T(8,128)(2,1)}, u32[]{:S(2)}) copy-start(bf16[1,512,4096]{2,1,0:T(8,128)(2,1)} %param.13) | copy-start | bytes 12582916
  18.5 1.3 copy-start
  19.8 1.7 copy-start.3
  21.5 51.1 %all-to-all-start = ((f32[16,200,256]{2,1,0:T(8,128)}), f32[16,200,256]{2,1,0:T(8,128)S(1)}, u32[]{:S(2)}, u32[]{:S(2)}) async-start(f32[16,200,256]{2,1,0:T(8,128)} %copy-done.3), calls=%async_computation | async-start | bytes 6553600 | tf_op jit(solution)/shard_map/all_to_all | solution.py:415
  73.8 1.0 copy-start.11
  74.8 0.6 copy-start.15
  75.4 0.7 copy-start.18
  76.1 1.9 collective-permute-start
  79.8 8.1 %collective-permute-start.1 = (f32[128,256]{1,0:T(8,128)}, f32[128,256]{1,0:T(8,128)S(1)}, u32[]{:S(2)}, u32[]{:S(2)}) collective-permute-start(f32[128,256]{1,0:T(8,128)} %get-tuple-element.25), channel_id=1, source_target_pairs={{0,2},{1,3},{2,4},{3,5},{4,6},{5,7},{6,0},{7,1},{8,10},{9,11},{10,... | collective-permute-start | bytes 393224 | tf_op jit(solution)/shard_map/ppermute | solution.py:421
  81.8 10.1 %collective-permute-start.2 = (f32[128,256]{1,0:T(8,128)}, f32[128,256]{1,0:T(8,128)S(1)}, u32[]{:S(2)}, u32[]{:S(2)}) collective-permute-start(f32[128,256]{1,0:T(8,128)} %get-tuple-element.26), channel_id=1, source_target_pairs={{0,4},{1,5},{2,6},{3,7},{4,0},{5,1},{6,2},{7,3},{8,12},{9,13},{10,... | collective-permute-start | bytes 393224 | tf_op jit(solution)/shard_map/ppermute | solution.py:421
  85.3 6.5 %collective-permute-start.3 = (f32[128,256]{1,0:T(8,128)}, f32[128,256]{1,0:T(8,128)S(1)}, u32[]{:S(2)}, u32[]{:S(2)}) collective-permute-start(f32[128,256]{1,0:T(8,128)} %get-tuple-element.27), channel_id=1, source_target_pairs={{0,6},{1,7},{2,0},{3,1},{4,2},{5,3},{6,4},{7,5},{8,14},{9,15},{10,... | collective-permute-start | bytes 393224 | tf_op jit(solution)/shard_map/ppermute | solution.py:421
  86.3 6.1 %collective-permute-start.4 = (f32[64,256]{1,0:T(8,128)}, f32[64,256]{1,0:T(8,128)S(1)}, u32[]{:S(2)}, u32[]{:S(2)}) collective-permute-start(f32[64,256]{1,0:T(8,128)} %copy-done.15), channel_id=1, source_target_pairs={{0,1},{1,0},{2,3},{3,2},{4,5},{5,4},{6,7},{7,6},{8,9},{9,8},{10,11... | collective-permute-start | bytes 196616 | tf_op jit(solution)/shard_map/ppermute | solution.py:424
  87.9 4.6 %collective-permute-start.5 = (f32[64,256]{1,0:T(8,128)S(1)}, f32[64,256]{1,0:T(8,128)S(1)}, u32[]{:S(2)}, u32[]{:S(2)}) collective-permute-start(f32[64,256]{1,0:T(8,128)S(1)} %slice.26), channel_id=1, source_target_pairs={{0,1},{1,0},{2,3},{3,2},{4,5},{5,4},{6,7},{7,6},{8,9},{9,8},{10,11... | collective-permute-start | bytes 196616 | tf_op jit(solution)/shard_map/ppermute | solution.py:424
  91.9 1.3 collective-permute-start.6
  91.9 1.5 collective-permute-start.7
  93.4 1.2 copy-start.12
  94.6 0.8 copy-start.16
  95.4 0.8 copy-start.20
  96.3 0.7 copy-start.21
  98.3 1.7 copy-start.4
  99.9 8.8 %copy-start.26 = (f32[2,64,128]{2,1,0:T(8,128)S(1)}, f32[2,64,128]{2,1,0:T(8,128)}, u32[]{:S(2)}) copy-start(f32[2,64,128]{2,1,0:T(8,128)} %copy-done.25) | copy-start | bytes 196612
  99.9 8.9 %copy-start.23 = (f32[4,64,128]{2,1,0:T(8,128)S(1)}, f32[4,64,128]{2,1,0:T(8,128)}, u32[]{:S(2)}) copy-start(f32[4,64,128]{2,1,0:T(8,128)} %copy-done.22) | copy-start | bytes 393220
  99.9 10.7 %copy-start.27 = (f32[1,256,64]{1,2,0:T(8,128)S(1)}, f32[1,256,64]{1,2,0:T(8,128)}, u32[]{:S(2)}) copy-start(f32[1,256,64]{1,2,0:T(8,128)} %param.20) | copy-start | bytes 196612
  99.9 51.6 %all-to-all-start.1 = ((f32[16,192,256]{2,1,0:T(8,128)}), f32[16,192,256]{2,1,0:T(8,128)}, u32[]{:S(2)}, u32[]{:S(2)}) async-start(f32[16,192,256]{2,1,0:T(8,128)} %copy-done.4), calls=%async_computation.1 | async-start | bytes 6291456 | tf_op jit(solution)/shard_map/all_to_all | solution.py:426
  108.8 4.1 %copy-start.24 = (f32[1,512,64]{1,2,0:T(8,128)S(1)}, f32[1,512,64]{1,2,0:T(8,128)}, u32[]{:S(2)}) copy-start(f32[1,512,64]{1,2,0:T(8,128)} %param.14) | copy-start | bytes 393220
  151.5 1.0 copy-start.7
  152.6 1.0 copy-start.9
  153.6 0.8 copy-start.13
  154.4 53.7 %copy-start.1 = (bf16[256,4096]{1,0:T(8,128)(2,1)S(1)}, bf16[256,4096]{1,0:T(8,128)(2,1)}, u32[]{:S(2)}) copy-start(bf16[256,4096]{1,0:T(8,128)(2,1)} %copy-done) | copy-start | bytes 6291460
  154.4 53.7 %copy-start.5 = (bf16[1,256,4096]{2,1,0:T(8,128)(2,1)S(1)}, bf16[1,256,4096]{2,1,0:T(8,128)(2,1)}, u32[]{:S(2)}) copy-start(bf16[1,256,4096]{2,1,0:T(8,128)(2,1)} %param.19) | copy-start | bytes 6291460
  154.4 53.7 %copy-start.14 = (f32[2,4,16,128]{3,2,0,1:T(8,128)S(1)}, f32[2,4,16,128]{3,2,0,1:T(8,128)}, u32[]{:S(2)}) copy-start(f32[2,4,16,128]{3,2,0,1:T(8,128)} %copy.68) | copy-start | bytes 196612
  154.4 53.7 %copy-start.17 = (bf16[1,256,512]{2,1,0:T(8,128)(2,1)S(1)}, bf16[1,256,512]{2,1,0:T(8,128)(2,1)}, u32[]{:S(2)}) copy-start(bf16[1,256,512]{2,1,0:T(8,128)(2,1)} %param.21) | copy-start | bytes 786436
  154.5 53.7 %copy-start.19 = (f32[2,1,4096]{2,1,0:T(1,128)S(1)}, f32[2,1,4096]{2,1,0:T(1,128)}, u32[]{:S(2)}) copy-start(f32[2,1,4096]{2,1,0:T(1,128)} %broadcast_in_dim_reshape.7.last_ref) | copy-start | bytes 98308

commit v2 on v0

v2 whole, which is shorter than its diff:
```python
import functools
import math

import jax
import jax.numpy as jnp
from jax import lax
from jax.experimental import pallas as pl
from jax.experimental.pallas import tpu as pltpu
from jax.sharding import PartitionSpec as P

P_SIZE = 64
N = 64
CH = 128
LOG2E = math.log2(math.e)
F32 = jnp.float32
BF16 = jnp.bfloat16
BIG = 56
MOST = 56
VMEM = pl.BlockSpec(memory_space=pltpu.VMEM)
SMEM = pl.BlockSpec(memory_space=pltpu.SMEM)


def split(value):
    hi = value.astype(BF16)
    return hi, (value - hi.astype(F32)).astype(BF16)


def dot(a, b, ca, cb):
    return lax.dot_general(a, b, (((ca,), (cb,)), ((), ())), preferred_element_type=F32)


def halves(rows):
    return lax.broadcasted_iota(jnp.int32, (rows, 128), 1) < 64


def cost(micros):
    return pl.CostEstimate(flops=0, bytes_accessed=int(micros * 3.69e6), transcendentals=0)


def limits(mib):
    return pltpu.CompilerParams(vmem_limit_bytes=mib * 2**20)


def call(kernel, in_specs, out_specs, out_shape, args, after=(), **options):
    count, extra = len(args), len(after)

    def body(*refs):
        inner = refs[:count] + refs[count + extra :]
        at = count + len(out_shape)
        inner[at][...] = jnp.zeros((8, 128), F32)
        kernel(*inner[:at], *inner[at + 1 :])

    if "grid" in options:
        token = pl.BlockSpec((8, 128), lambda i: (0, 0))
    else:
        token = VMEM
    return pl.pallas_call(
        body,
        in_specs=in_specs + [pl.BlockSpec(memory_space=pl.ANY)] * extra,
        out_specs=(*out_specs, token),
        out_shape=(*out_shape, jax.ShapeDtypeStruct((8, 128), F32)),
        **options,
    )(*args, *after)


def decay_rates(rate_ref, step):
    head = lax.broadcasted_iota(jnp.int32, (16, 1), 0)
    column = jnp.zeros((16, 1), F32)
    for h in range(16):
        column = jnp.where(head == h, rate_ref[step * 16 + h], column)
    return column * LOG2E


def masked_steps(step_ref, length_ref):
    steps = step_ref[...]
    if length_ref is None:
        return steps, None
    live = lax.broadcasted_iota(jnp.int32, steps.shape, 1) < length_ref[0]
    return jnp.where(live, steps, 0.0), live


def sums(logs, whole):
    row = lax.broadcasted_iota(jnp.int32, (CH, 2 * CH), 0)
    col = lax.broadcasted_iota(jnp.int32, (CH, 2 * CH), 1)
    ones = jnp.where((row <= col) & (col < CH) | (row > col - CH) & (col >= CH), 1.0, 0.0).astype(BF16)
    heads = logs.shape[0]
    chunks = logs.shape[1] // CH
    upto, after, lasts = [], [], []
    for c in range(chunks):
        part = logs[:, c * CH : (c + 1) * CH]
        p1 = part.astype(BF16)
        rest = part - p1.astype(F32)
        p2 = rest.astype(BF16)
        p3 = (rest - p2.astype(F32)).astype(BF16)
        res = dot(jnp.concatenate([p1, p2, p3], axis=0), ones, 1, 0)
        res = res[0:heads] + res[heads : 2 * heads] + res[2 * heads : 3 * heads]
        upto.append(res[:, 0:CH])
        after.append(res[:, CH:])
        lasts.append(res[:, CH - 1 : CH])
    if whole:
        total = jnp.zeros((heads, 1), F32)
        for c in range(chunks):
            upto[c] = upto[c] + total
            total = total + lasts[c]
        total = jnp.zeros((heads, 1), F32)
        for c in range(chunks - 1, -1, -1):
            after[c] = after[c] + total
            total = total + lasts[c]
    return upto, after, lasts


def widen(small):
    row = lax.broadcasted_iota(jnp.int32, (32, 1024), 0)
    lane = lax.broadcasted_iota(jnp.int32, (32, 1024), 1)
    pick = jnp.where(lane // 64 == row % 16, 1.0, 0.0).astype(BF16)
    hi, lo = split(small)
    return dot(jnp.concatenate([hi, lo], axis=0), pick, 0, 0)


def summary(proj_ref, weight, value_ref, out_ref, base):
    first = halves(64)
    proj_t = proj_ref[...].astype(F32).T
    for k in range(8):
        part = proj_t[(k // 4) * 64 : (k // 4) * 64 + 64]
        h0, l0 = split(part * weight[2 * k : 2 * k + 1, :])
        h1, l1 = split(part * weight[2 * k + 1 : 2 * k + 2, :])
        lhs = jnp.concatenate([h0, l0, h1, l1], axis=0)
        res = dot(lhs, value_ref[:, k * 128 : (k + 1) * 128], 1, 0)
        pair = jnp.where(first, res[0:64] + res[64:128], res[128:192] + res[192:256])
        lanes = slice((k % 2) * 128, (k % 2) * 128 + 128)
        out_ref[k // 2, base : base + 64, lanes] = pair


def first_kernel(len_ref, par_ref, rate_ref, x_ref, b_ref, dt_ref, ydy_ref, yc_ref, ydt_ref, out_ref):
    rate = decay_rates(rate_ref, pl.program_id(0))
    steps = dt_ref[...]
    _, after, lasts = sums(-steps * rate, True)
    summary(b_ref, steps * jnp.exp2(jnp.concatenate(after, axis=1)), x_ref, out_ref, 0)
    ysteps, live = masked_steps(ydt_ref, len_ref)
    upto, _, _ = sums(-ysteps * rate, True)
    weight = jnp.where(live, jnp.exp2(jnp.concatenate(upto, axis=1)), 0.0)
    summary(yc_ref, weight, ydy_ref, out_ref, 64)
    decay = jnp.exp2(jnp.broadcast_to(sum(lasts), (16, 256)))
    parent = jnp.zeros((4, 256), F32) + par_ref[0].astype(F32)
    for q in range(4):
        out_ref[q, 128:132, :] = decay[4 * q : 4 * q + 4]
        out_ref[q, 132:136, :] = parent


def carry_kernel(rate_ref, dy_ref, c_ref, dt_ref, out_ref):
    upto, _, _ = sums(-dt_ref[...] * decay_rates(rate_ref, pl.program_id(0)), True)
    summary(c_ref, jnp.exp2(jnp.concatenate(upto, axis=1)), dy_ref, out_ref, 0)


def cols(n, w):
    return pl.BlockSpec((n, w), lambda i: (0, i))


def heads(n):
    return pl.BlockSpec((16, n), lambda i: (i, 0))


def first_message(length, parent, rate, x, b, dt, ydy, yc, ydt):
    n, m = x.shape[0], ydy.shape[0]
    return call(
        first_kernel,
        [SMEM, SMEM, SMEM, cols(n, 1024), cols(n, 128), heads(n)]
        + [cols(m, 1024), cols(m, 128), heads(m)],
        (pl.BlockSpec((4, 136, 256), lambda i: (i, 0, 0)),),
        (jax.ShapeDtypeStruct((16, 136, 256), F32),),
        (length, parent, rate, x, b, dt, ydy, yc, ydt),
        grid=(4,),
        compiler_params=limits(BIG),
        cost_estimate=cost(8),
        name="first_message",
    )


def carry_message(rate, dy, c, dt, after):
    n = dy.shape[0]
    return call(
        carry_kernel,
        [SMEM, cols(n, 1024), cols(n, 128), heads(n)],
        (pl.BlockSpec((4, 64, 256), lambda i: (i, 0, 0)),),
        (jax.ShapeDtypeStruct((16, 64, 256), F32),),
        (rate, dy, c, dt),
        after,
        grid=(4,),
        compiler_params=limits(MOST),
        cost_estimate=cost(6),
        name="carry_message",
    )


def decay_row(got_ref, i):
    lane = lax.broadcasted_iota(jnp.int32, (1, 256), 1)
    row = [got_ref[i, 128 + q : 129 + q, :] for q in range(4)]
    low = jnp.where(lane < 64, row[0], row[1])
    return jnp.where(lane < 128, low, jnp.where(lane < 192, row[2], row[3]))


def forward_kernel(got_ref, carry_ref, out_ref, end_ref):
    state = jnp.zeros((64, 256), F32)
    for i in range(16):
        out_ref[i, 0:64, :] = carry_ref[i]
        out_ref[i, 64:128, :] = state
        state = decay_row(got_ref, i) * state + got_ref[i, 0:64, :]
    end_ref[...] = state


def forward(got, carry, after):
    return call(
        forward_kernel,
        [VMEM] * 2,
        (VMEM,) * 2,
        (jax.ShapeDtypeStruct((16, 128, 256), F32), jax.ShapeDtypeStruct((64, 256), F32)),
        (got, carry),
        after,
        compiler_params=limits(BIG),
        cost_estimate=cost(1),
        name="forward_scan",
    )


def buckets_kernel(place_ref, got_ref, end_ref, keep_ref, send_ref):
    core = place_ref[1].astype(F32)
    send_ref[4] = end_ref[...]
    for z in range(4):
        keep = jnp.zeros((64, 256), F32)
        send = jnp.zeros((64, 256), F32)
        for i in range(16):
            owner = got_ref[i, 132:133, :] - 2.0 * z
            term = got_ref[i, 64:128, :]
            keep = keep + jnp.where(owner == core, term, 0.0)
            send = send + jnp.where(owner == 1.0 - core, term, 0.0)
        keep_ref[z] = keep
        send_ref[z] = send


def buckets(place, got, end):
    return call(
        buckets_kernel,
        [SMEM, VMEM, VMEM],
        (VMEM,) * 2,
        (jax.ShapeDtypeStruct((4, 64, 256), F32), jax.ShapeDtypeStruct((5, 64, 256), F32)),
        (place, got, end),
        compiler_params=limits(BIG),
        cost_estimate=cost(1),
        name="buckets",
    )


def pack_kernel(place_ref, end_ref, keep_ref, recv_ref, m1_ref, m2_ref, m3_ref, own_ref):
    z = place_ref[0]
    own_ref[...] = keep_ref[z] + recv_ref[z]
    for d, ref in ((1, m1_ref), (2, m2_ref), (3, m3_ref)):
        to = lax.rem(z + d, 4)
        ref[0] = end_ref[...]
        ref[1] = recv_ref[4]
        ref[2] = keep_ref[to] + recv_ref[to]


def pack(place, end, keep, recv):
    msg = jax.ShapeDtypeStruct((3, 64, 256), F32)
    return call(
        pack_kernel,
        [SMEM] + [VMEM] * 3,
        (VMEM,) * 4,
        (msg, msg, msg, jax.ShapeDtypeStruct((64, 256), F32)),
        (place, end, keep, recv),
        compiler_params=limits(BIG),
        cost_estimate=cost(1),
        name="pack_leaf",
    )


def backward_kernel(got_ref, carry_ref, own_ref, r1, r2, r3, grad_ref):
    grad = own_ref[...] + r1[2] + r2[2] + r3[2]
    for i in range(15, -1, -1):
        grad_ref[i] = grad
        grad = decay_row(got_ref, i) * grad + carry_ref[i, 0:64, :]


def starts_kernel(place_ref, gotb_ref, end_ref, recv_ref, r1, r2, r3, start_ref):
    z = place_ref[0]
    core = place_ref[1]
    mine = (end_ref[...], r1[0], r2[0], r3[0])
    theirs = (recv_ref[4], r1[1], r2[1], r3[1])
    for i in range(16):
        owner = gotb_ref[i, 132:133, :]
        start = jnp.zeros((64, 256), F32)
        for d in range(4):
            place = 2 * lax.rem(z + 4 - d, 4)
            here = (place + core).astype(F32)
            there = (place + 1 - core).astype(F32)
            start = start + jnp.where(owner == here, mine[d], 0.0)
            start = start + jnp.where(owner == there, theirs[d], 0.0)
        start_ref[i] = start


def states_back(kernel, scalars, args, after, name):
    return call(
        kernel,
        [SMEM] * len(scalars) + [VMEM] * len(args),
        (VMEM,),
        (jax.ShapeDtypeStruct((16, 64, 256), F32),),
        (*scalars, *args),
        after,
        compiler_params=limits(BIG),
        cost_estimate=cost(1.5),
        name=name,
    )


def inside_kernel(chunks, has_length, *refs):
    step = pl.program_id(0)
    if has_length:
        len_ref, refs = refs[0], refs[1:]
    else:
        len_ref = None
    rate_ref, x_ref, dy_ref, b_ref, c_ref, dt_ref, dx_ref, db_ref, dc_ref = refs[:9]
    xh, xl, yh, yl, weight = refs[9:]
    first = halves(CH)
    causal = lax.broadcasted_iota(jnp.int32, (CH, CH), 1) >= lax.broadcasted_iota(
        jnp.int32, (CH, CH), 0
    )
    steps, _ = masked_steps(dt_ref, len_ref)
    upto, after, _ = sums(-steps * decay_rates(rate_ref, step), False)
    state = [jnp.zeros((64, 512), F32)] * 2
    carry, ends, dci = {}, {}, {}

    def grads_out(c):
        dy = dy_ref[c * CH : (c + 1) * CH, :]
        if len_ref is None:
            return dy
        token = lax.broadcasted_iota(jnp.int32, (CH, 1024), 0) + c * CH
        return jnp.where(token < len_ref[0], dy.astype(F32), 0.0).astype(BF16)

    def cross(lhs_hi, lhs_lo, rhs):
        hi, lo = split(rhs)
        res = dot(lhs_hi, jnp.concatenate([hi, lo], axis=0), 1, 1)
        return res[:, 0:64] + res[:, 64:128] + dot(lhs_lo, hi, 1, 1)

    for c in range(chunks):
        rows = slice(c * CH, (c + 1) * CH)
        rate_c = steps[:, rows]
        w = widen(rate_c * jnp.exp2(after[c]))
        e = widen(jnp.exp2(upto[c]))
        ends[c] = e[CH - 1 : CH]
        weight[c] = w
        xh[c], xl[c] = split(w * x_ref[rows, :].astype(F32))
        yh[c], yl[c] = split(e * grads_out(c).astype(F32))
        for g in range(2):
            wide = slice(g * 512, g * 512 + 512)
            thin = slice(g * 64, g * 64 + 64)
            if c > 0:
                dci[c, g] = cross(yh[c, :, wide], yl[c, :, wide], state[g])
            if c < chunks - 1:
                b_one = b_ref[rows, thin]
                added = dot(b_one, xh[c, :, wide], 0, 0) + dot(b_one, xl[c, :, wide], 0, 0)
                state[g] = added if c == 0 else ends[c][:, wide] * state[g] + added
            if c > 0:
                c_one = c_ref[rows, thin]
                carry[c, g] = dot(c_one, yh[c, :, wide], 0, 0) + dot(c_one, yl[c, :, wide], 0, 0)
    grad = [None, None]
    for c in range(chunks - 1, -1, -1):
        rows = slice(c * CH, (c + 1) * CH)
        cum_t = upto[c]
        cum_s = cum_t.T
        rate_s = steps[:, rows].T
        dy_c = grads_out(c)
        for g in range(2):
            wide = slice(g * 512, g * 512 + 512)
            thin = slice(g * 64, g * 64 + 64)
            b_one = b_ref[rows, thin]
            c_one = c_ref[rows, thin]
            dxi = None
            if c < chunks - 1:
                hi, lo = split(grad[g])
                dxi = dot(
                    jnp.concatenate([b_one, b_one], axis=1),
                    jnp.concatenate([hi, lo], axis=0),
                    1,
                    0,
                )
                dxi = dxi * weight[c, :, wide]
                dbi = cross(xh[c, :, wide], xl[c, :, wide], grad[g])
            scores = dot(b_one, c_one, 1, 1)
            total = jnp.zeros((CH, CH), F32)
            for k in range(4):
                lanes = slice(g * 512 + k * 128, g * 512 + k * 128 + 128)
                dy = dy_c[:, lanes]
                zero = jnp.zeros_like(dy)
                stacked = jnp.concatenate(
                    [jnp.where(first, dy, zero), jnp.where(first, zero, dy)], axis=0
                )
                pairs = dot(x_ref[rows, lanes], stacked, 1, 1)
                his, los = [], []
                for e in range(2):
                    h = g * 8 + 2 * k + e
                    gap = cum_t[h : h + 1, :] - jnp.broadcast_to(cum_s[:, h : h + 1], (CH, CH))
                    decay = jnp.exp2(jnp.where(causal, gap, -jnp.inf))
                    decay = decay * jnp.broadcast_to(rate_s[:, h : h + 1], (CH, CH))
                    total = total + decay * pairs[:, e * CH : (e + 1) * CH]
                    hi, lo = split(decay * scores)
                    his.append(hi)
                    los.append(lo)
                lhs = jnp.concatenate(
                    [jnp.concatenate(his, axis=1), jnp.concatenate(los, axis=1)], axis=0
                )
                res = dot(lhs, stacked, 1, 0)
                dx = res[0:CH] + res[CH : 2 * CH]
                if dxi is not None:
                    dx = dx + dxi[:, k * 128 : k * 128 + 128]
                dx_ref[rows, lanes] = dx.astype(dx_ref.dtype)
            hi, lo = split(total)
            db = dot(hi, c_one, 1, 0) + dot(lo, c_one, 1, 0)
            dc = dot(hi, b_one, 0, 0) + dot(lo, b_one, 0, 0)
            if c < chunks - 1:
                db = db + dbi
            if c > 0:
                dc = dc + dci[c, g]
                first_grad = c == chunks - 1
                grad[g] = carry[c, g] if first_grad else ends[c][:, wide] * grad[g] + carry[c, g]
            db_ref[rows, thin] = db.astype(db_ref.dtype)
            dc_ref[rows, thin] = dc


def inside(length, rate, x, dy, b, c, dt, kind, after, micros, name):
    n = x.shape[0]
    chunks = n // CH

    def scratch(dtype):
        return pltpu.VMEM((chunks, CH, 1024), dtype)

    has_length = length is not None
    return call(
        functools.partial(inside_kernel, chunks, has_length),
        [SMEM] * has_length + [SMEM, cols(n, 1024), cols(n, 1024), cols(n, 128), cols(n, 128), heads(n)],
        (cols(n, 1024), cols(n, 128), cols(n, 128)),
        (
            jax.ShapeDtypeStruct(x.shape, kind),
            jax.ShapeDtypeStruct(b.shape, kind),
            jax.ShapeDtypeStruct(c.shape, F32),
        ),
        (*([length] if has_length else []), rate, x, dy, b, c, dt),
        after,
        grid=(4,),
        scratch_shapes=[scratch(BF16)] * 4 + [scratch(F32)],
        compiler_params=limits(MOST),
        cost_estimate=cost(micros),
        name=name,
    )


def state_of(ref, g, base):
    return jnp.concatenate(
        [ref[2 * g, base : base + 64, :], ref[2 * g + 1, base : base + 64, :]], axis=1
    )


def start_kernel(base, has_length, *refs):
    if has_length:
        len_ref, refs = refs[0], refs[1:]
    else:
        len_ref = None
    rate_ref, dy_ref, dt_ref, state_ref, part_ref, dc_ref = refs
    steps, live = masked_steps(dt_ref, len_ref)
    upto, _, _ = sums(-steps * decay_rates(rate_ref, pl.program_id(0)), True)
    weight = jnp.exp2(jnp.concatenate(upto, axis=1))
    if live is not None:
        weight = jnp.where(live, weight, 0.0)
    yh, yl = split(widen(weight) * dy_ref[...].astype(F32))
    out = []
    for g in range(2):
        wide = slice(g * 512, g * 512 + 512)
        hi, lo = split(state_of(state_ref, g, base))
        res = dot(yh[:, wide], jnp.concatenate([hi, lo], axis=0), 1, 1)
        out.append(res[:, 0:64] + res[:, 64:128] + dot(yl[:, wide], hi, 1, 1))
    dc_ref[...] = (part_ref[...] + jnp.concatenate(out, axis=1)).astype(BF16)


def from_start(length, rate, dy, dt, states, base, part, after, name):
    n = dy.shape[0]
    has_length = length is not None
    return call(
        functools.partial(start_kernel, base, has_length),
        [SMEM] * has_length
        + [SMEM, cols(n, 1024), heads(n)]
        + [pl.BlockSpec((4,) + states.shape[1:], lambda i: (i, 0, 0)), cols(n, 128)],
        (cols(n, 128),),
        (jax.ShapeDtypeStruct((n, 512), BF16),),
        (*([length] if has_length else []), rate, dy, dt, states, part),
        after,
        grid=(4,),
        compiler_params=limits(MOST),
        cost_estimate=cost(n / 64),
        name=name,
    )


def end_kernel(base, rate_ref, x_ref, b_ref, dt_ref, state_ref, dxp_ref, dbp_ref, dx_ref, db_ref):
    steps = dt_ref[...]
    _, after, _ = sums(-steps * decay_rates(rate_ref, pl.program_id(0)), True)
    w = widen(steps * jnp.exp2(jnp.concatenate(after, axis=1)))
    xh, xl = split(w * x_ref[...].astype(F32))
    out = []
    for g in range(2):
        wide = slice(g * 512, g * 512 + 512)
        b_one = b_ref[:, g * 64 : g * 64 + 64]
        hi, lo = split(state_of(state_ref, g, base))
        both = jnp.concatenate([hi, lo], axis=0)
        dx = dot(jnp.concatenate([b_one, b_one], axis=1), both, 1, 0) * w[:, wide]
        dx_ref[:, wide] = (dxp_ref[:, wide] + dx).astype(BF16)
        res = dot(xh[:, wide], both, 1, 1)
        out.append(res[:, 0:64] + res[:, 64:128] + dot(xl[:, wide], hi, 1, 1))
    db_ref[...] = (dbp_ref[...] + jnp.concatenate(out, axis=1)).astype(BF16)


def from_end(rate, x, b, dt, states, base, dx_part, db_part):
    n = x.shape[0]
    return call(
        functools.partial(end_kernel, base),
        [SMEM, cols(n, 1024), cols(n, 128), heads(n)]
        + [pl.BlockSpec((4,) + states.shape[1:], lambda i: (i, 0, 0)), cols(n, 1024), cols(n, 128)],
        (cols(n, 1024), cols(n, 128)),
        (jax.ShapeDtypeStruct(x.shape, BF16), jax.ShapeDtypeStruct(b.shape, BF16)),
        (rate, x, b, dt, states, dx_part, db_part),
        grid=(4,),
        compiler_params=limits(MOST),
        cost_estimate=cost(10),
        name="from_end",
    )


def local(
    prompt_x,
    prompt_dt,
    head_rate,
    prompt_b,
    prompt_c,
    prompt_dy,
    branch_x,
    branch_dt,
    branch_b,
    branch_c,
    branch_dy,
    parent,
    lengths,
):
    x, dy, b, c = prompt_x[0], prompt_dy[0], prompt_b[0], prompt_c[0]
    yx, ydy, yb, yc = branch_x[0], branch_dy[0], branch_b[0], branch_c[0]
    dt, ydt = prompt_dt[0].T, branch_dt[0].T
    rate = head_rate
    leaf = lax.axis_index("leaf")
    place = jnp.stack([leaf // 2, leaf % 2]).astype(jnp.int32)
    swap = [(s, s ^ 1) for s in range(8)]

    def turn(value):
        return lax.all_to_all(value, "seq", 0, 0, tiled=True)

    sent, t = first_message(lengths, parent, rate, x, b, dt, ydy, yc, ydt)
    got = turn(sent)
    csent, t = carry_message(rate, dy, c, dt, (t,))
    dx_part, db_part, dc_part, t = inside(
        None, rate, x, dy, b, c, dt, F32, (t,), 28, "prompt_inside"
    )
    second, end, _ = forward(got, csent, (t,))
    back = turn(second)
    keep, send, _ = buckets(place, got, end)
    recv = lax.ppermute(send, "leaf", swap)
    m1, m2, m3, own, t = pack(place, end, keep, recv)
    received = [
        lax.ppermute(m, "leaf", [(s, (s + 2 * d) % 8) for s in range(8)])
        for d, m in ((1, m1), (2, m2), (3, m3))
    ]
    ydx, ydb, ydc_part, t = inside(
        lengths, rate, yx, ydy, yb, yc, ydt, BF16, (t,), 14, "branch_inside"
    )
    grads, t = states_back(
        backward_kernel, (), (got, back, own, *received), (t,), "end_gradients"
    )
    grads = turn(grads)
    dc, t = from_start(None, rate, dy, dt, back, 64, dc_part, (t,), "prompt_from_start")
    starts, t = states_back(
        starts_kernel, (place,), (got, end, recv, *received), (t,), "branch_starts"
    )
    starts = turn(starts)
    dx, db, t = from_end(rate, x, b, dt, grads, 0, dx_part, db_part)
    ydc, _ = from_start(lengths, rate, ydy, ydt, starts, 0, ydc_part, (t,), "branch_from_start")
    return tuple(a[None] for a in (dx, db, dc, ydx, ydb, ydc))


def solution(mesh):
    seq = P("leaf", "seq", None)
    own = P(("seq", "leaf"), None, None)
    ids = P(("seq", "leaf"))
    in_specs = (seq, seq, P(), seq, seq, seq, own, own, own, own, own, ids, ids)
    out_specs = (seq, seq, seq, own, own, own)
    return jax.shard_map(local, mesh=mesh, in_specs=in_specs, out_specs=out_specs, check_vma=False)
```

time: 1080 us -> 150 us (0.14); the launches traced: 1070 us -> 149 us
  waiting for transfers between devices: 484 us -> 12 us
  matrix products: 302 us -> 0 us
  local copies, waits for them, and re-layouts: 161 us -> 4.57 us
  Pallas kernels: 0 us -> 98.2 us
  other arithmetic: 78.8 us -> 0.61 us
  starting transfers between devices: 0.88 us -> 31.7 us
  blocking collectives: 21 us -> 0 us
  between operations: 16 us -> 2.07 us
    dot_general x122 -> x0, matrix products: 302 us -> none  [the longest x32 186 us: one_group(): output = jnp.einsum('hts,shp->thp', weights, x_one, precision=highest)]
    all_gather x3 -> x0, waiting for transfers between devices: 278 us -> none  [the longest x2 205 us: prefix(): gathered = jax.tree.map(lambda a: lax.all_gather(a, axis), part)]
    psum x2 -> x0, waiting for transfers between devices: 175 us -> none  [the longest x1 127 us: broadcast(): return lax.psum(block, axis)]
    pallas_call x0 -> x12, Pallas kernels: none -> 98.2 us  [call(): pl.pallas_call(body, in_specs=in_specs + [pl.BlockSpec(memory_space=pl.AN...]
    dynamic_slice x96 -> x0, local copies, waits for them, and re-layouts: 48.9 us -> none  [segment(): lax.map(jax.checkpoint(one_group), (x_groups, b_groups, c_groups, cum_gro...]
    squeeze x40 -> x0, local copies, waits for them, and re-layouts: 38 us -> none  [segment(): lax.map(jax.checkpoint(one_group), (x_groups, b_groups, c_groups, cum_gro...]
    reduce_scatter x1 -> x0, waiting for transfers between devices: 30.5 us -> none  [local(): lax.psum_scatter(term, 'leaf', scatter_dimension=0, tiled=True)]
    add x17 -> x0, other arithmetic: 25.3 us -> none  [the longest x15 22.8 us: compose(): jnp.exp(later[0])[:, None] * earlier[1] + later[1]]
  transfers between devices with their start and end apart: 6 -> 8, of which waited for: 6 -> 3; matrix products, arithmetic and copies ran while one was open for 7% -> 0% of each run, Pallas kernels for 0% -> 52%
where the time goes in v2:
time: 150 us; the launch traced here: 149 us
  Pallas kernels  98.2 us (65%)
  starting transfers between devices  31.7 us (21%)
  waiting for transfers between devices  12 us (8%)
  local copies, waits for them, and re-layouts  4.57 us (3%)
  between operations  2.07 us (1%)
    pallas_call x12, Pallas kernels, call(): pl.pallas_call(body, in_specs=in_specs + [pl.BlockSpec(memory_space=pl.AN...  98.2 us
    all_to_all x4, starting transfers between devices, turn(): return lax.all_to_all(value, 'seq', 0, 0, tiled=True)  25.2 us
    all_to_all x4, waiting for transfers between devices, turn(): return lax.all_to_all(value, 'seq', 0, 0, tiled=True)  10.2 us
    ppermute x3, starting transfers between devices, local(): lax.ppermute(m, 'leaf', [(s, (s + 2 * d) % 8) for s in range(8)])  6.51 us
    unnamed x16, local copies, waits for them, and re-layouts  4.57 us
  transfers between devices with their start and end apart: 8, of which 3 were waited for; matrix products, arithmetic and copies ran while one was open for 0% of the time, Pallas kernels for 52%

profile of v2, /device:TPU:0, one launch (start us, length us, event | category | flops | bytes accessed | tf_op | source)
XLA Modules:
  0.0 149.1 jit_solution(8255655053094672348)
XLA Ops:
  1.9 8.4 %first_message.1 = (f32[16,136,256]{2,1,0:T(8,128)}, f32[8,128]{1,0:T(8,128)}) custom-call(s32[1]{0:T(128)S(6)} %copy.20.refs_0_, s32[1]{0:T(128)S(6)} %copy.19.refs_1_, f32[64]{0:T(128)} %refs_1_.4, bf16[512,4096]{1,0:T(8,128)(2,1)} %bitcast.25, bf16[512,512]{1,0:T(8,128)(2,1)} %bitcast.31, f32[64,512]{1,0:T(8,128)} %bitcast.34, ...), custom_call_target="tpu_custom_call" | custom-call | bytes 29520000 | tf_op jit(solution)/shard_map/first_message/pallas_call | solution.py:57
  10.3 7.1 %all-to-all-start = ((f32[16,136,256]{2,1,0:T(8,128)}), f32[16,136,256]{2,1,0:T(8,128)S(1)}, u32[]{:S(2)}, u32[]{:S(2)}) async-start(f32[16,136,256]{2,1,0:T(8,128)} %get-tuple-element.36), calls=%async_computation | async-start | bytes 4456448 | tf_op jit(solution)/shard_map/all_to_all | solution.py:560
  17.5 6.5 %carry_message.1 = (f32[16,64,256]{2,1,0:T(8,128)}, f32[8,128]{1,0:T(8,128)}) custom-call(f32[64]{0:T(128)} %refs_1_.4, bf16[512,4096]{1,0:T(8,128)(2,1)} %bitcast.22, bf16[512,512]{1,0:T(8,128)(2,1)} %bitcast.39, f32[64,512]{1,0:T(8,128)} %bitcast.35, f32[8,128]{1,0:T(8,128)} %get-tuple-element.37.refs_4_), custom_call_target="tpu_custom_call" | custom-call | bytes 22140000 | tf_op jit(solution)/shard_map/carry_message/pallas_call | solution.py:57
  23.9 28.8 %prompt_inside.1 = (f32[512,4096]{1,0:T(8,128)}, f32[512,512]{1,0:T(8,128)}, f32[512,512]{1,0:T(8,128)}, f32[8,128]{1,0:T(8,128)}) custom-call(f32[64]{0:T(128)} %refs_1_.4, bf16[512,4096]{1,0:T(8,128)(2,1)} %bitcast.26, bf16[512,4096]{1,0:T(8,128)(2,1)} %bitcast.23, bf16[512,512]{1,0:T(8,128)(2,1)} %bitcast.32, bf16[512,512]{1,0:T(8,128)(2,1)} %bitcast.40, ...), custom_call_target="tpu_custom_call" | custom-call | bytes 103320000 | tf_op jit(solution)/shard_map/prompt_inside/pallas_call | solution.py:57
  52.7 0.0 all-to-all-done.refs_0_.refs_1_
  52.7 0.0 copy-start
  52.7 1.4 copy-done
  54.0 3.5 %forward_scan.1 = (f32[16,128,256]{2,1,0:T(8,128)}, f32[64,256]{1,0:T(8,128)}, f32[8,128]{1,0:T(8,128)}) custom-call(f32[16,136,256]{2,1,0:T(8,128)} %copy-done, f32[16,64,256]{2,1,0:T(8,128)} %get-tuple-element.38.refs_1_, f32[8,128]{1,0:T(8,128)} %get-tuple-element.40.refs_2_), custom_call_target="tpu_custom_call" | custom-call | bytes 3690000 | tf_op jit(solution)/shard_map/forward_scan/pallas_call | solution.py:57
  57.5 7.2 %all-to-all-start.1 = ((f32[16,128,256]{2,1,0:T(8,128)}), f32[16,128,256]{2,1,0:T(8,128)S(1)}, u32[]{:S(2)}, u32[]{:S(2)}) async-start(f32[16,128,256]{2,1,0:T(8,128)} %get-tuple-element.41), calls=%async_computation.1 | async-start | bytes 4194304 | tf_op jit(solution)/shard_map/all_to_all | solution.py:560
  64.7 0.6 pad_add_fusion.refs_0_
  65.3 3.2 %buckets.1 = (f32[4,64,256]{2,1,0:T(8,128)}, f32[5,64,256]{2,1,0:T(8,128)}, f32[8,128]{1,0:T(8,128)}) custom-call(s32[2]{0:T(128)} %pad_add_fusion.refs_0_, f32[16,136,256]{2,1,0:T(8,128)} %copy-done, f32[64,256]{1,0:T(8,128)} %get-tuple-element.42.refs_2_.refs_1_), custom_call_target="tpu_custom_call" | custom-call | bytes 3690000 | tf_op jit(solution)/shard_map/buckets/pallas_call | solution.py:57
  68.5 0.0 collective-permute-start
  68.5 1.8 %collective-permute-done.refs_3_ = f32[5,64,256]{2,1,0:T(8,128)S(1)} collective-permute-done((f32[5,64,256]{2,1,0:T(8,128)}, f32[5,64,256]{2,1,0:T(8,128)S(1)}, u32[]{:S(2)}, u32[]{:S(2)}) %collective-permute-start) | collective-permute-done | bytes 327712 | tf_op jit(solution)/shard_map/ppermute | solution.py:571
  70.4 0.0 copy-start.4
  70.4 0.7 copy-done.4
  71.1 2.0 %pack_leaf.1 = (f32[3,64,256]{2,1,0:T(8,128)}, f32[3,64,256]{2,1,0:T(8,128)}, f32[3,64,256]{2,1,0:T(8,128)}, f32[64,256]{1,0:T(8,128)}, f32[8,128]{1,0:T(8,128)}) custom-call(s32[2]{0:T(128)} %pad_add_fusion.refs_0_, f32[64,256]{1,0:T(8,128)} %get-tuple-element.42.refs_2_.refs_1_, f32[4,64,256]{2,1,0:T(8,128)} %get-tuple-element.43.refs_2_, ...), custom_call_target="tpu_custom_call" | custom-call | bytes 3690000 | tf_op jit(solution)/shard_map/pack_leaf/pallas_call | solution.py:57
  73.1 1.9 %collective-permute-start.1 = (f32[3,64,256]{2,1,0:T(8,128)}, f32[3,64,256]{2,1,0:T(8,128)S(1)}, u32[]{:S(2)}, u32[]{:S(2)}) collective-permute-start(f32[3,64,256]{2,1,0:T(8,128)} %get-tuple-element.46), channel_id=1, source_target_pairs={{0,2},{1,3},{2,4},{3,5},{4,6},{5,7},{6,0},{7,1},{8,10},{9,11},{10,... | collective-permute-start | bytes 589832 | tf_op jit(solution)/shard_map/ppermute | solution.py:574
  75.0 3.6 %collective-permute-start.2 = (f32[3,64,256]{2,1,0:T(8,128)}, f32[3,64,256]{2,1,0:T(8,128)S(1)}, u32[]{:S(2)}, u32[]{:S(2)}) collective-permute-start(f32[3,64,256]{2,1,0:T(8,128)} %get-tuple-element.47), channel_id=1, source_target_pairs={{0,4},{1,5},{2,6},{3,7},{4,0},{5,1},{6,2},{7,3},{8,12},{9,13},{10,... | collective-permute-start | bytes 589832 | tf_op jit(solution)/shard_map/ppermute | solution.py:574
  78.6 1.0 collective-permute-start.3
  79.6 14.6 %branch_inside.1 = (bf16[256,4096]{1,0:T(8,128)(2,1)}, bf16[256,512]{1,0:T(8,128)(2,1)}, f32[256,512]{1,0:T(8,128)}, f32[8,128]{1,0:T(8,128)}) custom-call(s32[1]{0:T(128)S(6)} %copy.20.refs_0_, f32[64]{0:T(128)} %refs_1_.4, bf16[256,4096]{1,0:T(8,128)(2,1)} %bitcast.41, bf16[256,4096]{1,0:T(8,128)(2,1)} %bitcast.29, bf16[256,512]{1,0:T(8,128)(2,1)} %bitcast.47, ...), custom_call_target="tpu_custom_call" | custom-call | bytes 51660000 | tf_op jit(solution)/shard_map/branch_inside/pallas_call | solution.py:57
  94.1 0.0 collective-permute-done.1.refs_3_.refs_4_
  94.2 0.0 copy-start.5
  94.2 0.0 collective-permute-done.2.refs_4_.refs_5_
  94.2 0.0 copy-start.6
  94.2 0.0 collective-permute-done.3.refs_5_.refs_6_
  94.2 0.0 copy-start.7
  94.2 0.0 all-to-all-done.1.refs_1_.refs_3_
  94.2 0.0 copy-start.1
  94.2 0.6 copy-done.5
  94.8 0.1 copy-done.6
  94.9 0.1 copy-done.7
  95.0 0.7 copy-done.1
  95.7 3.5 %end_gradients.1 = (f32[16,64,256]{2,1,0:T(8,128)}, f32[8,128]{1,0:T(8,128)}) custom-call(f32[16,136,256]{2,1,0:T(8,128)} %copy-done, f32[16,128,256]{2,1,0:T(8,128)} %copy-done.1, f32[64,256]{1,0:T(8,128)} %get-tuple-element.45.refs_2_, f32[3,64,256]{2,1,0:T(8,128)} %copy-done.5, f32[3,64,256]{2,1,0:T(8,128)} %copy-done.6, f32[3,64,256]{2,1,0:T(8,128)} %copy-done.7, ...), custom_call_target="tpu_custom_call" | custom-call | bytes 5535000 | tf_op jit(solution)/shard_map/end_gradients/pallas_call | solution.py:57
  99.2 7.2 %all-to-all-start.2 = ((f32[16,64,256]{2,1,0:T(8,128)}), f32[16,64,256]{2,1,0:T(8,128)S(1)}, u32[]{:S(2)}, u32[]{:S(2)}) async-start(f32[16,64,256]{2,1,0:T(8,128)} %get-tuple-element.51), calls=%async_computation.2 | async-start | bytes 2097152 | tf_op jit(solution)/shard_map/all_to_all | solution.py:560
  106.4 7.8 %prompt_from_start.1 = (bf16[512,512]{1,0:T(8,128)(2,1)}, f32[8,128]{1,0:T(8,128)}) custom-call(f32[64]{0:T(128)} %refs_1_.4, bf16[512,4096]{1,0:T(8,128)(2,1)} %bitcast.24, f32[64,512]{1,0:T(8,128)} %bitcast.37, f32[16,128,256]{2,1,0:T(8,128)} %copy-done.1, f32[512,512]{1,0:T(8,128)} %get-tuple-element.56.refs_4_, f32[8,128]{1,0:T(8,128)} %get-tuple-element.57.refs_5_), custom_call_target="tpu_custom_call" | custom-call | bytes 29520000 | tf_op jit(solution)/shard_map/prompt_from_start/pallas_call | solution.py:57
  114.2 3.6 %branch_starts.1 = (f32[16,64,256]{2,1,0:T(8,128)}, f32[8,128]{1,0:T(8,128)}) custom-call(s32[2]{0:T(128)} %pad_add_fusion.refs_0_, f32[16,136,256]{2,1,0:T(8,128)} %copy-done, f32[64,256]{1,0:T(8,128)} %get-tuple-element.42.refs_2_.refs_1_, f32[5,64,256]{2,1,0:T(8,128)} %copy-done.4, f32[3,64,256]{2,1,0:T(8,128)} %copy-done.5, f32[3,64,256]{2,1,0:T(8,128)} %copy-done.6, ...), custom_call_target="tpu_custom_call" | custom-call | bytes 5535000 | tf_op jit(solution)/shard_map/branch_starts/pallas_call | solution.py:57
  117.8 5.5 %all-to-all-done.2.refs_4_ = f32[16,64,256]{2,1,0:T(8,128)S(1)} async-done(((f32[16,64,256]{2,1,0:T(8,128)}), f32[16,64,256]{2,1,0:T(8,128)S(1)}, u32[]{:S(2)}, u32[]{:S(2)}) %all-to-all-start.2) | async-done | bytes 1048608 | tf_op jit(solution)/shard_map/all_to_all | solution.py:560
  123.3 0.0 copy-start.2
  123.3 3.7 %all-to-all-start.3 = ((f32[16,64,256]{2,1,0:T(8,128)}), f32[16,64,256]{2,1,0:T(8,128)S(1)}, u32[]{:S(2)}, u32[]{:S(2)}) async-start(f32[16,64,256]{2,1,0:T(8,128)} %get-tuple-element.62), calls=%async_computation.3 | async-start | bytes 2097152 | tf_op jit(solution)/shard_map/all_to_all | solution.py:560
  126.9 0.0 copy-done.2
  126.9 10.5 %from_end.1 = (bf16[512,4096]{1,0:T(8,128)(2,1)}, bf16[512,512]{1,0:T(8,128)(2,1)}, f32[8,128]{1,0:T(8,128)}) custom-call(f32[64]{0:T(128)} %refs_1_.4, bf16[512,4096]{1,0:T(8,128)(2,1)} %bitcast.27, bf16[512,512]{1,0:T(8,128)(2,1)} %bitcast.33, f32[64,512]{1,0:T(8,128)} %bitcast.38, f32[16,64,256]{2,1,0:T(8,128)} %copy-done.2, ...), custom_call_target="tpu_custom_call" | custom-call | bytes 36900000 | tf_op jit(solution)/shard_map/from_end/pallas_call | solution.py:57
  137.5 4.7 %all-to-all-done.3.refs_4_ = f32[16,64,256]{2,1,0:T(8,128)S(1)} async-done(((f32[16,64,256]{2,1,0:T(8,128)}), f32[16,64,256]{2,1,0:T(8,128)S(1)}, u32[]{:S(2)}, u32[]{:S(2)}) %all-to-all-start.3) | async-done | bytes 1048608 | tf_op jit(solution)/shard_map/all_to_all | solution.py:560
  142.2 0.0 copy-start.3
  142.2 1.0 copy-done.3
  143.1 6.0 %branch_from_start.1 = (bf16[256,512]{1,0:T(8,128)(2,1)}, f32[8,128]{1,0:T(8,128)}) custom-call(s32[1]{0:T(128)S(6)} %copy.20.refs_0_, f32[64]{0:T(128)} %refs_1_.4, bf16[256,4096]{1,0:T(8,128)(2,1)} %bitcast.30, f32[64,256]{1,0:T(8,128)} %bitcast.46, f32[16,64,256]{2,1,0:T(8,128)} %copy-done.3, f32[256,512]{1,0:T(8,128)} %get-tuple-element.63.refs_5_, ...), custom_call_target="tpu_custom_call" | custom-call | bytes 14760000 | tf_op jit(solution)/shard_map/branch_from_start/pallas_call | solution.py:57
Async XLA Ops:
  10.3 42.3 %all-to-all-start = ((f32[16,136,256]{2,1,0:T(8,128)}), f32[16,136,256]{2,1,0:T(8,128)S(1)}, u32[]{:S(2)}, u32[]{:S(2)}) async-start(f32[16,136,256]{2,1,0:T(8,128)} %get-tuple-element.36), calls=%async_computation | async-start | bytes 4456448 | tf_op jit(solution)/shard_map/all_to_all | solution.py:560
  52.7 1.4 copy-start
  57.5 36.7 %all-to-all-start.1 = ((f32[16,128,256]{2,1,0:T(8,128)}), f32[16,128,256]{2,1,0:T(8,128)S(1)}, u32[]{:S(2)}, u32[]{:S(2)}) async-start(f32[16,128,256]{2,1,0:T(8,128)} %get-tuple-element.41), calls=%async_computation.1 | async-start | bytes 4194304 | tf_op jit(solution)/shard_map/all_to_all | solution.py:560
  68.5 1.8 %collective-permute-start = (f32[5,64,256]{2,1,0:T(8,128)}, f32[5,64,256]{2,1,0:T(8,128)S(1)}, u32[]{:S(2)}, u32[]{:S(2)}) collective-permute-start(f32[5,64,256]{2,1,0:T(8,128)} %get-tuple-element.44), channel_id=1, source_target_pairs={{0,1},{1,0},{2,3},{3,2},{4,5},{5,4},{6,7},{7,6},{8,9},{9,8},{10,11... | collective-permute-start | bytes 983048 | tf_op jit(solution)/shard_map/ppermute | solution.py:571
  70.4 0.7 copy-start.4
  73.1 21.1 %collective-permute-start.1 = (f32[3,64,256]{2,1,0:T(8,128)}, f32[3,64,256]{2,1,0:T(8,128)S(1)}, u32[]{:S(2)}, u32[]{:S(2)}) collective-permute-start(f32[3,64,256]{2,1,0:T(8,128)} %get-tuple-element.46), channel_id=1, source_target_pairs={{0,2},{1,3},{2,4},{3,5},{4,6},{5,7},{6,0},{7,1},{8,10},{9,11},{10,... | collective-permute-start | bytes 589832 | tf_op jit(solution)/shard_map/ppermute | solution.py:574
  75.0 19.2 %collective-permute-start.2 = (f32[3,64,256]{2,1,0:T(8,128)}, f32[3,64,256]{2,1,0:T(8,128)S(1)}, u32[]{:S(2)}, u32[]{:S(2)}) collective-permute-start(f32[3,64,256]{2,1,0:T(8,128)} %get-tuple-element.47), channel_id=1, source_target_pairs={{0,4},{1,5},{2,6},{3,7},{4,0},{5,1},{6,2},{7,3},{8,12},{9,13},{10,... | collective-permute-start | bytes 589832 | tf_op jit(solution)/shard_map/ppermute | solution.py:574
  78.6 15.6 %collective-permute-start.3 = (f32[3,64,256]{2,1,0:T(8,128)}, f32[3,64,256]{2,1,0:T(8,128)S(1)}, u32[]{:S(2)}, u32[]{:S(2)}) collective-permute-start(f32[3,64,256]{2,1,0:T(8,128)} %get-tuple-element.48), channel_id=1, source_target_pairs={{0,6},{1,7},{2,0},{3,1},{4,2},{5,3},{6,4},{7,5},{8,14},{9,15},{10,... | collective-permute-start | bytes 589832 | tf_op jit(solution)/shard_map/ppermute | solution.py:574
  94.2 0.7 copy-start.5
  94.2 0.7 copy-start.6
  94.2 0.8 copy-start.7
  94.2 1.5 %copy-start.1 = (f32[16,128,256]{2,1,0:T(8,128)}, f32[16,128,256]{2,1,0:T(8,128)S(1)}, u32[]{:S(2)}) copy-start(f32[16,128,256]{2,1,0:T(8,128)S(1)} %all-to-all-done.1.refs_1_.refs_3_) | copy-start | bytes 6291460
  99.2 24.1 %all-to-all-start.2 = ((f32[16,64,256]{2,1,0:T(8,128)}), f32[16,64,256]{2,1,0:T(8,128)S(1)}, u32[]{:S(2)}, u32[]{:S(2)}) async-start(f32[16,64,256]{2,1,0:T(8,128)} %get-tuple-element.51), calls=%async_computation.2 | async-start | bytes 2097152 | tf_op jit(solution)/shard_map/all_to_all | solution.py:560
  123.3 3.7 %copy-start.2 = (f32[16,64,256]{2,1,0:T(8,128)}, f32[16,64,256]{2,1,0:T(8,128)S(1)}, u32[]{:S(2)}) copy-start(f32[16,64,256]{2,1,0:T(8,128)S(1)} %all-to-all-done.2.refs_4_) | copy-start | bytes 3145732
  123.3 18.9 %all-to-all-start.3 = ((f32[16,64,256]{2,1,0:T(8,128)}), f32[16,64,256]{2,1,0:T(8,128)S(1)}, u32[]{:S(2)}, u32[]{:S(2)}) async-start(f32[16,64,256]{2,1,0:T(8,128)} %get-tuple-element.62), calls=%async_computation.3 | async-start | bytes 2097152 | tf_op jit(solution)/shard_map/all_to_all | solution.py:560
  142.2 1.0 copy-start.3

commit v3 on v2

--- a/solution.py
+++ b/solution.py
@@ -42,33 +42,11 @@
 
 
 def call(kernel, in_specs, out_specs, out_shape, args, after=(), **options):
-    count, extra = len(args), len(after)
-
-    def body(*refs):
-        inner = refs[:count] + refs[count + extra :]
-        at = count + len(out_shape)
-        inner[at][...] = jnp.zeros((8, 128), F32)
-        kernel(*inner[:at], *inner[at + 1 :])
-
-    if "grid" in options:
-        token = pl.BlockSpec((8, 128), lambda i: (0, 0))
-    else:
-        token = VMEM
+    if after:
+        *args, _ = lax.optimization_barrier((*args, after))
     return pl.pallas_call(
-        body,
-        in_specs=in_specs + [pl.BlockSpec(memory_space=pl.ANY)] * extra,
-        out_specs=(*out_specs, token),
-        out_shape=(*out_shape, jax.ShapeDtypeStruct((8, 128), F32)),
-        **options,
-    )(*args, *after)
-
-
-def decay_rates(rate_ref, step):
-    head = lax.broadcasted_iota(jnp.int32, (16, 1), 0)
-    column = jnp.zeros((16, 1), F32)
-    for h in range(16):
-        column = jnp.where(head == h, rate_ref[step * 16 + h], column)
-    return column * LOG2E
+        kernel, in_specs=in_specs, out_specs=out_specs, out_shape=out_shape, **options
+    )(*args)
 
 
 def masked_steps(step_ref, length_ref):
@@ -79,11 +57,11 @@
     return jnp.where(live, steps, 0.0), live
 
 
-def sums(logs, whole):
+def sums(logs):
     row = lax.broadcasted_iota(jnp.int32, (CH, 2 * CH), 0)
     col = lax.broadcasted_iota(jnp.int32, (CH, 2 * CH), 1)
     ones = jnp.where((row <= col) & (col < CH) | (row > col - CH) & (col >= CH), 1.0, 0.0).astype(BF16)
-    heads = logs.shape[0]
+    count = logs.shape[0]
     chunks = logs.shape[1] // CH
     upto, after, lasts = [], [], []
     for c in range(chunks):
@@ -93,28 +71,27 @@
         p2 = rest.astype(BF16)
         p3 = (rest - p2.astype(F32)).astype(BF16)
         res = dot(jnp.concatenate([p1, p2, p3], axis=0), ones, 1, 0)
-        res = res[0:heads] + res[heads : 2 * heads] + res[2 * heads : 3 * heads]
+        res = res[0:count] + res[count : 2 * count] + res[2 * count : 3 * count]
         upto.append(res[:, 0:CH])
         after.append(res[:, CH:])
         lasts.append(res[:, CH - 1 : CH])
-    if whole:
-        total = jnp.zeros((heads, 1), F32)
-        for c in range(chunks):
-            upto[c] = upto[c] + total
-            total = total + lasts[c]
-        total = jnp.zeros((heads, 1), F32)
-        for c in range(chunks - 1, -1, -1):
-            after[c] = after[c] + total
-            total = total + lasts[c]
-    return upto, after, lasts
-
-
-def widen(small):
+    zero = jnp.zeros((count, 1), F32)
+    before, behind = [zero], [zero]
+    for c in range(chunks):
+        before.append(before[c] + lasts[c])
+        behind.append(behind[c] + lasts[chunks - 1 - c])
+    return upto, after, before[:chunks], behind[chunks - 1 :: -1] if chunks > 1 else behind[:1], before[chunks]
+
+
+def picker():
     row = lax.broadcasted_iota(jnp.int32, (32, 1024), 0)
     lane = lax.broadcasted_iota(jnp.int32, (32, 1024), 1)
-    pick = jnp.where(lane // 64 == row % 16, 1.0, 0.0).astype(BF16)
-    hi, lo = split(small)
-    return dot(jnp.concatenate([hi, lo], axis=0), pick, 0, 0)
+    return jnp.where(lane // 64 == row % 16, 1.0, 0.0).astype(BF16)
+
+
+def turned(small):
+    hi = small.astype(BF16).astype(F32)
+    return jnp.concatenate([hi, small - hi], axis=0).T.astype(BF16)
 
 
 def summary(proj_ref, weight, value_ref, out_ref, base):
@@ -131,25 +108,63 @@
         out_ref[k // 2, base : base + 64, lanes] = pair
 
 
-def first_kernel(len_ref, par_ref, rate_ref, x_ref, b_ref, dt_ref, ydy_ref, yc_ref, ydt_ref, out_ref):
-    rate = decay_rates(rate_ref, pl.program_id(0))
-    steps = dt_ref[...]
-    _, after, lasts = sums(-steps * rate, True)
-    summary(b_ref, steps * jnp.exp2(jnp.concatenate(after, axis=1)), x_ref, out_ref, 0)
-    ysteps, live = masked_steps(ydt_ref, len_ref)
-    upto, _, _ = sums(-ysteps * rate, True)
-    weight = jnp.where(live, jnp.exp2(jnp.concatenate(upto, axis=1)), 0.0)
-    summary(yc_ref, weight, ydy_ref, out_ref, 64)
-    decay = jnp.exp2(jnp.broadcast_to(sum(lasts), (16, 256)))
+def first_kernel(
+    len_ref,
+    par_ref,
+    rate_ref,
+    x_ref,
+    b_ref,
+    dt_ref,
+    ydy_ref,
+    yc_ref,
+    ydt_ref,
+    out_ref,
+    upto_ref,
+    after_ref,
+    yupto_ref,
+    yafter_ref,
+    e_ref,
+    w_ref,
+    ye_ref,
+    w_all,
+    e_all,
+    ye_all,
+    end_all,
+):
+    step = pl.program_id(0)
+
+    @pl.when(step == 0)
+    def _():
+        rate = jnp.broadcast_to(rate_ref[...], (CH, 64)).T[:, 0:1] * LOG2E
+        steps = dt_ref[...]
+        upto, after, before, behind, end = sums(-steps * rate)
+        for c in range(len(upto)):
+            here = slice(c * CH, (c + 1) * CH)
+            upto_ref[:, here] = upto[c]
+            after_ref[:, here] = after[c]
+            e_all[:, here] = jnp.exp2(upto[c] + before[c])
+            w_all[:, here] = steps[:, here] * jnp.exp2(after[c] + behind[c])
+        end_all[...] = jnp.exp2(jnp.broadcast_to(end, end_all.shape))
+        ysteps, live = masked_steps(ydt_ref, len_ref)
+        upto, after, before, _, _ = sums(-ysteps * rate)
+        for c in range(len(upto)):
+            here = slice(c * CH, (c + 1) * CH)
+            yupto_ref[:, here] = upto[c]
+            yafter_ref[:, here] = after[c]
+            ye_all[:, here] = jnp.where(live[:, here], jnp.exp2(upto[c] + before[c]), 0.0)
+
+    rows = pl.ds(pl.multiple_of(step * 16, 16), 16)
+    w, ye = w_all[rows, :], ye_all[rows, :]
+    summary(b_ref, w, x_ref, out_ref, 0)
+    summary(yc_ref, ye, ydy_ref, out_ref, 64)
+    decay = end_all[rows, :]
     parent = jnp.zeros((4, 256), F32) + par_ref[0].astype(F32)
     for q in range(4):
         out_ref[q, 128:132, :] = decay[4 * q : 4 * q + 4]
         out_ref[q, 132:136, :] = parent
-
-
-def carry_kernel(rate_ref, dy_ref, c_ref, dt_ref, out_ref):
-    upto, _, _ = sums(-dt_ref[...] * decay_rates(rate_ref, pl.program_id(0)), True)
-    summary(c_ref, jnp.exp2(jnp.concatenate(upto, axis=1)), dy_ref, out_ref, 0)
+    e_ref[0] = turned(e_all[rows, :])
+    w_ref[0] = turned(w)
+    ye_ref[0] = turned(ye)
 
 
 def cols(n, w):
@@ -160,35 +175,39 @@
     return pl.BlockSpec((16, n), lambda i: (i, 0))
 
 
+def whole(*shape):
+    return pl.BlockSpec(shape, lambda i: (0,) * len(shape))
+
+
+def turns(n):
+    return pl.BlockSpec((1, n, 32), lambda i: (i, 0, 0))
+
+
 def first_message(length, parent, rate, x, b, dt, ydy, yc, ydt):
     n, m = x.shape[0], ydy.shape[0]
+    f32 = lambda *shape: jax.ShapeDtypeStruct(shape, F32)
+    bf16 = lambda *shape: jax.ShapeDtypeStruct(shape, BF16)
     return call(
         first_kernel,
-        [SMEM, SMEM, SMEM, cols(n, 1024), cols(n, 128), heads(n)]
-        + [cols(m, 1024), cols(m, 128), heads(m)],
-        (pl.BlockSpec((4, 136, 256), lambda i: (i, 0, 0)),),
-        (jax.ShapeDtypeStruct((16, 136, 256), F32),),
+        [SMEM, SMEM, whole(1, 64), cols(n, 1024), cols(n, 128), whole(64, n)]
+        + [cols(m, 1024), cols(m, 128), whole(64, m)],
+        (pl.BlockSpec((4, 136, 256), lambda i: (i, 0, 0)),)
+        + (whole(64, n),) * 2
+        + (whole(64, m),) * 2
+        + (turns(n), turns(n), turns(m)),
+        (f32(16, 136, 256), f32(64, n), f32(64, n), f32(64, m), f32(64, m))
+        + (bf16(4, n, 32), bf16(4, n, 32), bf16(4, m, 32)),
         (length, parent, rate, x, b, dt, ydy, yc, ydt),
         grid=(4,),
+        scratch_shapes=[
+            pltpu.VMEM((64, n), F32),
+            pltpu.VMEM((64, n), F32),
+            pltpu.VMEM((64, m), F32),
+            pltpu.VMEM((64, 256), F32),
+        ],
         compiler_params=limits(BIG),
         cost_estimate=cost(8),
         name="first_message",
-    )
-
-
-def carry_message(rate, dy, c, dt, after):
-    n = dy.shape[0]
-    return call(
-        carry_kernel,
-        [SMEM, cols(n, 1024), cols(n, 128), heads(n)],
-        (pl.BlockSpec((4, 64, 256), lambda i: (i, 0, 0)),),
-        (jax.ShapeDtypeStruct((16, 64, 256), F32),),
-        (rate, dy, c, dt),
-        after,
-        grid=(4,),
-        compiler_params=limits(MOST),
-        cost_estimate=cost(6),
-        name="carry_message",
     )
 
 
@@ -216,7 +235,7 @@
         (jax.ShapeDtypeStruct((16, 128, 256), F32), jax.ShapeDtypeStruct((64, 256), F32)),
         (got, carry),
         after,
-        compiler_params=limits(BIG),
+        compiler_params=limits(12),
         cost_estimate=cost(1),
         name="forward_scan",
     )
@@ -244,7 +263,7 @@
         (VMEM,) * 2,
         (jax.ShapeDtypeStruct((4, 64, 256), F32), jax.ShapeDtypeStruct((5, 64, 256), F32)),
         (place, got, end),
-        compiler_params=limits(BIG),
+        compiler_params=limits(12),
         cost_estimate=cost(1),
         name="buckets",
     )
@@ -268,7 +287,7 @@
         (VMEM,) * 4,
         (msg, msg, msg, jax.ShapeDtypeStruct((64, 256), F32)),
         (place, end, keep, recv),
-        compiler_params=limits(BIG),
+        compiler_params=limits(12),
         cost_estimate=cost(1),
         name="pack_leaf",
     )
@@ -306,26 +325,32 @@
         (jax.ShapeDtypeStruct((16, 64, 256), F32),),
         (*scalars, *args),
         after,
-        compiler_params=limits(BIG),
+        compiler_params=limits(12),
         cost_estimate=cost(1.5),
         name=name,
     )
 
 
 def inside_kernel(chunks, has_length, *refs):
-    step = pl.program_id(0)
     if has_length:
         len_ref, refs = refs[0], refs[1:]
     else:
         len_ref = None
-    rate_ref, x_ref, dy_ref, b_ref, c_ref, dt_ref, dx_ref, db_ref, dc_ref = refs[:9]
-    xh, xl, yh, yl, weight = refs[9:]
+    x_ref, dy_ref, b_ref, c_ref, dt_ref, upto_ref, after_ref, dx_ref, db_ref, dc_ref = refs[:10]
+    if has_length:
+        carry_ref = None
+        xh, xl, yh, yl, weight = refs[10:]
+    else:
+        carry_ref = refs[10]
+        xh, xl, yh, yl, weight = refs[11:]
+    pick = picker()
     first = halves(CH)
     causal = lax.broadcasted_iota(jnp.int32, (CH, CH), 1) >= lax.broadcasted_iota(
         jnp.int32, (CH, CH), 0
     )
     steps, _ = masked_steps(dt_ref, len_ref)
-    upto, after, _ = sums(-steps * decay_rates(rate_ref, step), False)
+    upto = [upto_ref[:, c * CH : (c + 1) * CH] for c in range(chunks)]
+    after = [after_ref[:, c * CH : (c + 1) * CH] for c in range(chunks)]
     state = [jnp.zeros((64, 512), F32)] * 2
     carry, ends, dci = {}, {}, {}
 
@@ -344,12 +369,19 @@
     for c in range(chunks):
         rows = slice(c * CH, (c + 1) * CH)
         rate_c = steps[:, rows]
-        w = widen(rate_c * jnp.exp2(after[c]))
-        e = widen(jnp.exp2(upto[c]))
-        ends[c] = e[CH - 1 : CH]
-        weight[c] = w
-        xh[c], xl[c] = split(w * x_ref[rows, :].astype(F32))
-        yh[c], yl[c] = split(e * grads_out(c).astype(F32))
+        w_turned = turned(rate_c * jnp.exp2(after[c]))
+        e_turned = turned(jnp.exp2(upto[c]))
+        dy_c = grads_out(c)
+        tails = []
+        for q in range(4):
+            lanes = slice(q * 256, q * 256 + 256)
+            w = dot(w_turned, pick[:, lanes], 1, 0)
+            weight[c, :, lanes] = w
+            xh[c, :, lanes], xl[c, :, lanes] = split(w * x_ref[rows, lanes].astype(F32))
+            e = dot(e_turned, pick[:, lanes], 1, 0)
+            tails.append(e[CH - 1 : CH])
+            yh[c, :, lanes], yl[c, :, lanes] = split(e * dy_c[:, lanes].astype(F32))
+        ends[c] = jnp.concatenate(tails, axis=1)
         for g in range(2):
             wide = slice(g * 512, g * 512 + 512)
             thin = slice(g * 64, g * 64 + 64)
@@ -359,7 +391,7 @@
                 b_one = b_ref[rows, thin]
                 added = dot(b_one, xh[c, :, wide], 0, 0) + dot(b_one, xl[c, :, wide], 0, 0)
                 state[g] = added if c == 0 else ends[c][:, wide] * state[g] + added
-            if c > 0:
+            if c > 0 or carry_ref is not None:
                 c_one = c_ref[rows, thin]
                 carry[c, g] = dot(c_one, yh[c, :, wide], 0, 0) + dot(c_one, yl[c, :, wide], 0, 0)
     grad = [None, None]
@@ -420,13 +452,19 @@
                 db = db + dbi
             if c > 0:
                 dc = dc + dci[c, g]
-                first_grad = c == chunks - 1
-                grad[g] = carry[c, g] if first_grad else ends[c][:, wide] * grad[g] + carry[c, g]
+            if c == chunks - 1:
+                grad[g] = carry[c, g]
+            elif c > 0 or carry_ref is not None:
+                grad[g] = ends[c][:, wide] * grad[g] + carry[c, g]
             db_ref[rows, thin] = db.astype(db_ref.dtype)
             dc_ref[rows, thin] = dc
-
-
-def inside(length, rate, x, dy, b, c, dt, kind, after, micros, name):
+    if carry_ref is not None:
+        for g in range(2):
+            for q in range(2):
+                carry_ref[2 * g + q] = grad[g][:, q * 256 : q * 256 + 256]
+
+
+def inside(length, x, dy, b, c, dt, upto, rest, kind, after, micros, name):
     n = x.shape[0]
     chunks = n // CH
 
@@ -436,14 +474,16 @@
     has_length = length is not None
     return call(
         functools.partial(inside_kernel, chunks, has_length),
-        [SMEM] * has_length + [SMEM, cols(n, 1024), cols(n, 1024), cols(n, 128), cols(n, 128), heads(n)],
-        (cols(n, 1024), cols(n, 128), cols(n, 128)),
+        [SMEM] * has_length + [cols(n, 1024)] * 2 + [cols(n, 128)] * 2 + [heads(n)] * 3,
+        (cols(n, 1024), cols(n, 128), cols(n, 128))
+        + (() if has_length else (pl.BlockSpec((4, 64, 256), lambda i: (i, 0, 0)),)),
         (
             jax.ShapeDtypeStruct(x.shape, kind),
             jax.ShapeDtypeStruct(b.shape, kind),
             jax.ShapeDtypeStruct(c.shape, F32),
-        ),
-        (*([length] if has_length else []), rate, x, dy, b, c, dt),
+        )
+        + (() if has_length else (jax.ShapeDtypeStruct((16, 64, 256), F32),)),
+        (*([length] if has_length else []), x, dy, b, c, dt, upto, rest),
         after,
         grid=(4,),
         scratch_shapes=[scratch(BF16)] * 4 + [scratch(F32)],
@@ -453,44 +493,46 @@
     )
 
 
-def state_of(ref, g, base):
-    return jnp.concatenate(
-        [ref[2 * g, base : base + 64, :], ref[2 * g + 1, base : base + 64, :]], axis=1
-    )
-
-
-def start_kernel(base, has_length, *refs):
-    if has_length:
-        len_ref, refs = refs[0], refs[1:]
-    else:
-        len_ref = None
-    rate_ref, dy_ref, dt_ref, state_ref, part_ref, dc_ref = refs
-    steps, live = masked_steps(dt_ref, len_ref)
-    upto, _, _ = sums(-steps * decay_rates(rate_ref, pl.program_id(0)), True)
-    weight = jnp.exp2(jnp.concatenate(upto, axis=1))
-    if live is not None:
-        weight = jnp.where(live, weight, 0.0)
-    yh, yl = split(widen(weight) * dy_ref[...].astype(F32))
+def diagonal(ref, q, j):
+    pair = ref[q, :, j * 128 : j * 128 + 128]
+    first = halves(64)
+    hi, lo = split(pair)
+    zero = jnp.zeros_like(hi)
+    rows = [jnp.where(first, v, zero) if h == 0 else jnp.where(first, zero, v) for v in (hi, lo) for h in (0, 1)]
+    return jnp.concatenate(rows, axis=0)
+
+
+def product(value, state, weight):
+    res = dot(value, state, 1, 1)
+    return (res[:, 0:128] + res[:, 128:256]) * weight
+
+
+def start_kernel(base, dy_ref, e_ref, state_ref, part_ref, dc_ref):
+    state_ref = state_ref.at[:, base : base + 64, :]
+    e_turned = e_ref[0]
+    pick = picker()
     out = []
     for g in range(2):
-        wide = slice(g * 512, g * 512 + 512)
-        hi, lo = split(state_of(state_ref, g, base))
-        res = dot(yh[:, wide], jnp.concatenate([hi, lo], axis=0), 1, 1)
-        out.append(res[:, 0:64] + res[:, 64:128] + dot(yl[:, wide], hi, 1, 1))
+        total = None
+        for q in (2 * g, 2 * g + 1):
+            e = dot(e_turned, pick[:, q * 256 : q * 256 + 256], 1, 0)
+            for j in range(2):
+                lanes = slice(q * 256 + j * 128, q * 256 + j * 128 + 128)
+                term = product(dy_ref[:, lanes], diagonal(state_ref, q, j), e[:, j * 128 : j * 128 + 128])
+                total = term if total is None else total + term
+        out.append(total[:, 0:64] + total[:, 64:128])
     dc_ref[...] = (part_ref[...] + jnp.concatenate(out, axis=1)).astype(BF16)
 
 
-def from_start(length, rate, dy, dt, states, base, part, after, name):
+def from_start(dy, e, states, base, part, after, name):
     n = dy.shape[0]
-    has_length = length is not None
-    return call(
-        functools.partial(start_kernel, base, has_length),
-        [SMEM] * has_length
-        + [SMEM, cols(n, 1024), heads(n)]
+    return call(
+        functools.partial(start_kernel, base),
+        [cols(n, 1024), turns(n)]
         + [pl.BlockSpec((4,) + states.shape[1:], lambda i: (i, 0, 0)), cols(n, 128)],
         (cols(n, 128),),
         (jax.ShapeDtypeStruct((n, 512), BF16),),
-        (*([length] if has_length else []), rate, dy, dt, states, part),
+        (dy, e, states, part),
         after,
         grid=(4,),
         compiler_params=limits(MOST),
@@ -499,33 +541,38 @@
     )
 
 
-def end_kernel(base, rate_ref, x_ref, b_ref, dt_ref, state_ref, dxp_ref, dbp_ref, dx_ref, db_ref):
-    steps = dt_ref[...]
-    _, after, _ = sums(-steps * decay_rates(rate_ref, pl.program_id(0)), True)
-    w = widen(steps * jnp.exp2(jnp.concatenate(after, axis=1)))
-    xh, xl = split(w * x_ref[...].astype(F32))
+def end_kernel(base, x_ref, b_ref, w_ref, state_ref, dxp_ref, dbp_ref, dx_ref, db_ref):
+    state_ref = state_ref.at[:, base : base + 64, :]
+    w_turned = w_ref[0]
+    pick = picker()
     out = []
     for g in range(2):
-        wide = slice(g * 512, g * 512 + 512)
+        total = None
         b_one = b_ref[:, g * 64 : g * 64 + 64]
-        hi, lo = split(state_of(state_ref, g, base))
-        both = jnp.concatenate([hi, lo], axis=0)
-        dx = dot(jnp.concatenate([b_one, b_one], axis=1), both, 1, 0) * w[:, wide]
-        dx_ref[:, wide] = (dxp_ref[:, wide] + dx).astype(BF16)
-        res = dot(xh[:, wide], both, 1, 1)
-        out.append(res[:, 0:64] + res[:, 64:128] + dot(xl[:, wide], hi, 1, 1))
+        b_two = jnp.concatenate([b_one, b_one], axis=1)
+        for q in (2 * g, 2 * g + 1):
+            wide = slice(q * 256, q * 256 + 256)
+            w = dot(w_turned, pick[:, wide], 1, 0)
+            hi, lo = split(state_ref[q])
+            dx = dot(b_two, jnp.concatenate([hi, lo], axis=0), 1, 0) * w
+            dx_ref[:, wide] = (dxp_ref[:, wide] + dx).astype(BF16)
+            for j in range(2):
+                lanes = slice(q * 256 + j * 128, q * 256 + j * 128 + 128)
+                term = product(x_ref[:, lanes], diagonal(state_ref, q, j), w[:, j * 128 : j * 128 + 128])
+                total = term if total is None else total + term
+        out.append(total[:, 0:64] + total[:, 64:128])
     db_ref[...] = (dbp_ref[...] + jnp.concatenate(out, axis=1)).astype(BF16)
 
 
-def from_end(rate, x, b, dt, states, base, dx_part, db_part):
+def from_end(x, b, w, states, base, dx_part, db_part):
     n = x.shape[0]
     return call(
         functools.partial(end_kernel, base),
-        [SMEM, cols(n, 1024), cols(n, 128), heads(n)]
+        [cols(n, 1024), cols(n, 128), turns(n)]
         + [pl.BlockSpec((4,) + states.shape[1:], lambda i: (i, 0, 0)), cols(n, 1024), cols(n, 128)],
         (cols(n, 1024), cols(n, 128)),
         (jax.ShapeDtypeStruct(x.shape, BF16), jax.ShapeDtypeStruct(b.shape, BF16)),
-        (rate, x, b, dt, states, dx_part, db_part),
+        (x, b, w, states, dx_part, db_part),
         grid=(4,),
         compiler_params=limits(MOST),
         cost_estimate=cost(10),
@@ -551,7 +598,7 @@
     x, dy, b, c = prompt_x[0], prompt_dy[0], prompt_b[0], prompt_c[0]
     yx, ydy, yb, yc = branch_x[0], branch_dy[0], branch_b[0], branch_c[0]
     dt, ydt = prompt_dt[0].T, branch_dt[0].T
-    rate = head_rate
+    rate = head_rate[None, :]
     leaf = lax.axis_index("leaf")
     place = jnp.stack([leaf // 2, leaf % 2]).astype(jnp.int32)
     swap = [(s, s ^ 1) for s in range(8)]
@@ -559,35 +606,35 @@
     def turn(value):
         return lax.all_to_all(value, "seq", 0, 0, tiled=True)
 
-    sent, t = first_message(lengths, parent, rate, x, b, dt, ydy, yc, ydt)
+    sent, upto, rest, yupto, yrest, e, w, ye = first_message(lengths, parent, rate, x, b, dt, ydy, yc, ydt)
     got = turn(sent)
-    csent, t = carry_message(rate, dy, c, dt, (t,))
-    dx_part, db_part, dc_part, t = inside(
-        None, rate, x, dy, b, c, dt, F32, (t,), 28, "prompt_inside"
-    )
-    second, end, _ = forward(got, csent, (t,))
+    dx_part, db_part, dc_part, csent = inside(
+        None, x, dy, b, c, dt, upto, rest, F32, (sent,), 28, "prompt_inside"
+    )
+    second, end = forward(got, csent, ())
     back = turn(second)
-    keep, send, _ = buckets(place, got, end)
+    keep, send = buckets(place, got, end)
     recv = lax.ppermute(send, "leaf", swap)
-    m1, m2, m3, own, t = pack(place, end, keep, recv)
+    m1, m2, m3, own = pack(place, end, keep, recv)
     received = [
         lax.ppermute(m, "leaf", [(s, (s + 2 * d) % 8) for s in range(8)])
         for d, m in ((1, m1), (2, m2), (3, m3))
     ]
-    ydx, ydb, ydc_part, t = inside(
-        lengths, rate, yx, ydy, yb, yc, ydt, BF16, (t,), 14, "branch_inside"
-    )
-    grads, t = states_back(
-        backward_kernel, (), (got, back, own, *received), (t,), "end_gradients"
-    )
+    ydx, ydb, ydc_part = inside(
+        lengths, yx, ydy, yb, yc, ydt, yupto, yrest, BF16, (own,), 14, "branch_inside"
+    )
+    (grads,) = states_back(
+        backward_kernel, (), (got, back, own, *received), (ydb,), "end_gradients"
+    )
+    sent_grads = grads
     grads = turn(grads)
-    dc, t = from_start(None, rate, dy, dt, back, 64, dc_part, (t,), "prompt_from_start")
-    starts, t = states_back(
-        starts_kernel, (place,), (got, end, recv, *received), (t,), "branch_starts"
+    (dc,) = from_start(dy, e, back, 64, dc_part, (sent_grads,), "prompt_from_start")
+    (starts,) = states_back(
+        starts_kernel, (place,), (got, end, recv, *received), (dc,), "branch_starts"
     )
     starts = turn(starts)
-    dx, db, t = from_end(rate, x, b, dt, grads, 0, dx_part, db_part)
-    ydc, _ = from_start(lengths, rate, ydy, ydt, starts, 0, ydc_part, (t,), "branch_from_start")
+    dx, db = from_end(x, b, w, grads, 0, dx_part, db_part)
+    (ydc,) = from_start(ydy, ye, starts, 0, ydc_part, (db,), "branch_from_start")
     return tuple(a[None] for a in (dx, db, dc, ydx, ydb, ydc))
 
 

time: 150 us -> 133 us (0.89)
  Pallas kernels: 98.2 us -> 79.3 us
  waiting for transfers between devices: 12 us -> 21.4 us
  starting transfers between devices: 31.7 us -> 26.2 us
    pallas_call x12 -> x11, Pallas kernels: 98.2 us -> 79.3 us  [call(): pl.pallas_call(kernel, in_specs=in_specs, out_specs=out_specs, out_shape=...]
    all_to_all x4, waiting for transfers between devices: 10.2 us -> 19.8 us  [turn(): return lax.all_to_all(value, 'seq', 0, 0, tiled=True)]
    all_to_all x4, starting transfers between devices: 25.2 us -> 19.6 us  [turn(): return lax.all_to_all(value, 'seq', 0, 0, tiled=True)]
    unnamed x16 -> x6, local copies, waits for them, and re-layouts: 4.57 us -> 3.52 us
  transfers between devices with their start and end apart: 8 -> 8, of which waited for: 3 -> 5; matrix products, arithmetic and copies ran while one was open for 0% -> 0% of each run, Pallas kernels for 52% -> 48%
where the time goes in v3:
time: 133 us
  Pallas kernels  79.3 us (60%)
  starting transfers between devices  26.2 us (20%)
  waiting for transfers between devices  21.4 us (16%)
  local copies, waits for them, and re-layouts  3.52 us (3%)
  between operations  2.04 us (2%)
    pallas_call x11, Pallas kernels, call(): pl.pallas_call(kernel, in_specs=in_specs, out_specs=out_specs, out_shape=...  79.3 us
    all_to_all x4, waiting for transfers between devices, turn(): return lax.all_to_all(value, 'seq', 0, 0, tiled=True)  19.8 us
    all_to_all x4, starting transfers between devices, turn(): return lax.all_to_all(value, 'seq', 0, 0, tiled=True)  19.6 us
    ppermute x3, starting transfers between devices, local(): lax.ppermute(m, 'leaf', [(s, (s + 2 * d) % 8) for s in range(8)])  6.55 us
    unnamed x6, local copies, waits for them, and re-layouts  3.52 us
  transfers between devices with their start and end apart: 8, of which 5 were waited for; matrix products, arithmetic and copies ran while one was open for 0% of the time, Pallas kernels for 48%

profile of v3, /device:TPU:0, one launch (start us, length us, event | category | flops | bytes accessed | tf_op | source)
XLA Modules:
  0.0 132.6 jit_solution(9972963677676807755)
XLA Ops:
  1.9 8.1 %first_message.1 = (f32[16,136,256]{2,1,0:T(8,128)}, f32[64,512]{1,0:T(8,128)}, f32[64,512]{1,0:T(8,128)}, f32[64,256]{1,0:T(8,128)}, f32[64,256]{1,0:T(8,128)},...) custom-call(s32[1]{0:T(128)S(6)} %copy.20.len_ref.refs_0_, ...), custom_call_target="tpu_custom_call" | custom-call | bytes 29520000 | tf_op jit(solution)/shard_map/first_message/pallas_call | solution.py:47
  10.0 7.1 %all-to-all-start = ((f32[16,136,256]{2,1,0:T(8,128)}), f32[16,136,256]{2,1,0:T(8,128)S(1)}, u32[]{:S(2)}, u32[]{:S(2)}) async-start(f32[16,136,256]{2,1,0:T(8,128)} %get-tuple-element.68), calls=%async_computation | async-start | bytes 4456448 | tf_op jit(solution)/shard_map/all_to_all | solution.py:607
  17.1 28.0 %prompt_inside.1 = (f32[512,4096]{1,0:T(8,128)}, f32[512,512]{1,0:T(8,128)}, f32[512,512]{1,0:T(8,128)}, f32[16,64,256]{2,1,0:T(8,128)}) custom-call(bf16[512,4096]{1,0:T(8,128)(2,1)} %bitcast.24, bf16[512,4096]{1,0:T(8,128)(2,1)} %bitcast.29, bf16[512,512]{1,0:T(8,128)(2,1)} %bitcast.32, bf16[512,512]{1,0:T(8,128)(2,1)} %bitcast.39, f32[64,512]{1,0:T(8,128)} %bitcast.38, ...), custom_call_target="tpu_custom_call" | custom-call | bytes 103320000 | tf_op jit(solution)/shard_map/prompt_inside/pallas_call | solution.py:47
  45.1 4.0 %all-to-all-done.got_ref.gotb_ref = f32[16,136,256]{2,1,0:T(8,128)S(1)} async-done(((f32[16,136,256]{2,1,0:T(8,128)}), f32[16,136,256]{2,1,0:T(8,128)S(1)}, u32[]{:S(2)}, u32[]{:S(2)}) %all-to-all-start) | async-done | bytes 2228256 | tf_op jit(solution)/shard_map/all_to_all | solution.py:607
  49.2 0.0 copy-start.1
  49.2 1.2 copy-done.1
  50.4 0.1 forward_scan.1
  50.5 0.0 copy-start
  50.5 1.3 copy-done
  51.9 4.4 %all-to-all-start.1 = ((f32[16,128,256]{2,1,0:T(8,128)}), f32[16,128,256]{2,1,0:T(8,128)}, u32[]{:S(2)}, u32[]{:S(2)}) async-start(f32[16,128,256]{2,1,0:T(8,128)} %copy-done), calls=%async_computation.1 | async-start | bytes 4194304 | tf_op jit(solution)/shard_map/all_to_all | solution.py:607
  56.3 0.1 pad_add_fusion.place_ref
  56.4 1.4 %buckets.1 = (f32[4,64,256]{2,1,0:T(8,128)S(1)}, f32[5,64,256]{2,1,0:T(8,128)S(1)}) custom-call(s32[2]{0:T(128)S(1)} %pad_add_fusion.place_ref, f32[16,136,256]{2,1,0:T(8,128)S(1)} %all-to-all-done.got_ref.gotb_ref, f32[64,256]{1,0:T(8,128)S(1)} %get-tuple-element.118.end_ref), custom_call_target="tpu_custom_call" | custom-call | bytes 3690000 | tf_op jit(solution)/shard_map/buckets/pallas_call | solution.py:47
  57.8 0.1 collective-permute-start
  57.9 1.6 %collective-permute-done.recv_ref = f32[5,64,256]{2,1,0:T(8,128)S(1)} collective-permute-done((f32[5,64,256]{2,1,0:T(8,128)S(1)}, f32[5,64,256]{2,1,0:T(8,128)S(1)}, u32[]{:S(2)}, u32[]{:S(2)}) %collective-permute-start) | collective-permute-done | bytes 327712 | tf_op jit(solution)/shard_map/ppermute | solution.py:617
  59.5 0.6 pack_leaf.1
  60.1 1.9 %collective-permute-start.1 = (f32[3,64,256]{2,1,0:T(8,128)S(1)}, f32[3,64,256]{2,1,0:T(8,128)S(1)}, u32[]{:S(2)}, u32[]{:S(2)}) collective-permute-start(f32[3,64,256]{2,1,0:T(8,128)S(1)} %get-tuple-element.84), channel_id=1, source_target_pairs={{0,2},{1,3},{2,4},{3,5},{4,6},{5,7},{6,0},{7,1},{8,10},{9,11},{10,... | collective-permute-start | bytes 589832 | tf_op jit(solution)/shard_map/ppermute | solution.py:620
  62.0 3.6 %collective-permute-start.2 = (f32[3,64,256]{2,1,0:T(8,128)S(1)}, f32[3,64,256]{2,1,0:T(8,128)S(1)}, u32[]{:S(2)}, u32[]{:S(2)}) collective-permute-start(f32[3,64,256]{2,1,0:T(8,128)S(1)} %get-tuple-element.85), channel_id=1, source_target_pairs={{0,4},{1,5},{2,6},{3,7},{4,0},{5,1},{6,2},{7,3},{8,12},{9,13},{10,... | collective-permute-start | bytes 589832 | tf_op jit(solution)/shard_map/ppermute | solution.py:620
  65.6 1.0 collective-permute-start.3
  66.6 13.9 %branch_inside.1 = (bf16[256,4096]{1,0:T(8,128)(2,1)}, bf16[256,512]{1,0:T(8,128)(2,1)}, f32[256,512]{1,0:T(8,128)}) custom-call(s32[1]{0:T(128)S(6)} %copy.20.len_ref.refs_0_, bf16[256,4096]{1,0:T(8,128)(2,1)} %bitcast.34, bf16[256,4096]{1,0:T(8,128)(2,1)} %bitcast.27, bf16[256,512]{1,0:T(8,128)(2,1)} %bitcast.43, bf16[256,512]{1,0:T(8,128)(2,1)} %bitcast.36, ...), custom_call_target="tpu_custom_call" | custom-call | bytes 51660000 | tf_op jit(solution)/shard_map/branch_inside/pallas_call | solution.py:47
  80.5 0.0 collective-permute-done.1.r1
  80.5 0.0 collective-permute-done.2.r2
  80.5 0.0 collective-permute-done.3.r3
  80.6 3.8 %all-to-all-done.1.carry_ref.state_ref = f32[16,128,256]{2,1,0:T(8,128)} async-done(((f32[16,128,256]{2,1,0:T(8,128)}), f32[16,128,256]{2,1,0:T(8,128)}, u32[]{:S(2)}, u32[]{:S(2)}) %all-to-all-start.1) | async-done | bytes 2097184 | tf_op jit(solution)/shard_map/all_to_all | solution.py:607
  84.4 2.7 %end_gradients.1 = f32[16,64,256]{2,1,0:T(8,128)} custom-call(f32[16,136,256]{2,1,0:T(8,128)S(1)} %all-to-all-done.got_ref.gotb_ref, f32[16,128,256]{2,1,0:T(8,128)} %all-to-all-done.1.carry_ref.state_ref, f32[64,256]{1,0:T(8,128)S(1)} %get-tuple-element.100.own_ref, f32[3,64,256]{2,1,0:T(8,128)S(1)} %collective-permute-done.1.r1, ...), custom_call_target="tpu_custom_call" | custom-call | bytes 5535000 | tf_op jit(solution)/shard_map/end_gradients/pallas_call | solution.py:47
  87.0 4.3 %all-to-all-start.2 = ((f32[16,64,256]{2,1,0:T(8,128)}), f32[16,64,256]{2,1,0:T(8,128)}, u32[]{:S(2)}, u32[]{:S(2)}) async-start(f32[16,64,256]{2,1,0:T(8,128)} %end_gradients.1), calls=%async_computation.2 | async-start | bytes 2097152 | tf_op jit(solution)/shard_map/all_to_all | solution.py:607
  91.4 7.2 %prompt_from_start.1 = bf16[512,512]{1,0:T(8,128)(2,1)} custom-call(bf16[512,4096]{1,0:T(8,128)(2,1)} %bitcast.30, bf16[4,512,32]{2,1,0:T(8,128)(2,1)} %get-tuple-element.111.e_ref, f32[16,128,256]{2,1,0:T(8,128)} %all-to-all-done.1.carry_ref.state_ref, f32[512,512]{1,0:T(8,128)} %get-tuple-element.113.part_ref), custom_call_target="tpu_custom_call" | custom-call | bytes 29520000 | tf_op jit(solution)/shard_map/prompt_from_start/pallas_call | solution.py:47
  98.5 2.3 %branch_starts.1 = f32[16,64,256]{2,1,0:T(8,128)} custom-call(s32[2]{0:T(128)S(1)} %pad_add_fusion.place_ref, f32[16,136,256]{2,1,0:T(8,128)S(1)} %all-to-all-done.got_ref.gotb_ref, f32[64,256]{1,0:T(8,128)S(1)} %get-tuple-element.118.end_ref, f32[5,64,256]{2,1,0:T(8,128)S(1)} %collective-permute-done.recv_ref, f32[3,64,256]{2,1,0:T(8,128)S(1)} %collective-permute-done.1.r1, ...), custom_call_target="tpu_custom_call" | custom-call | bytes 5535000 | tf_op jit(solution)/shard_map/branch_starts/pallas_call | solution.py:47
  100.9 6.1 %all-to-all-done.2.state_ref = f32[16,64,256]{2,1,0:T(8,128)} async-done(((f32[16,64,256]{2,1,0:T(8,128)}), f32[16,64,256]{2,1,0:T(8,128)}, u32[]{:S(2)}, u32[]{:S(2)}) %all-to-all-start.2) | async-done | bytes 1048608 | tf_op jit(solution)/shard_map/all_to_all | solution.py:607
  107.0 3.7 %all-to-all-start.3 = ((f32[16,64,256]{2,1,0:T(8,128)}), f32[16,64,256]{2,1,0:T(8,128)S(1)}, u32[]{:S(2)}, u32[]{:S(2)}) async-start(f32[16,64,256]{2,1,0:T(8,128)} %branch_starts.1), calls=%async_computation.3 | async-start | bytes 2097152 | tf_op jit(solution)/shard_map/all_to_all | solution.py:607
  110.6 9.8 %from_end.1 = (bf16[512,4096]{1,0:T(8,128)(2,1)}, bf16[512,512]{1,0:T(8,128)(2,1)}) custom-call(bf16[512,4096]{1,0:T(8,128)(2,1)} %bitcast.25, bf16[512,512]{1,0:T(8,128)(2,1)} %bitcast.33, bf16[4,512,32]{2,1,0:T(8,128)(2,1)} %get-tuple-element.67.w_ref, f32[16,64,256]{2,1,0:T(8,128)} %all-to-all-done.2.state_ref, f32[512,4096]{1,0:T(8,128)} %get-tuple-element.104.dxp_ref, ...), custom_call_target="tpu_custom_call" | custom-call | bytes 36900000 | tf_op jit(solution)/shard_map/from_end/pallas_call | solution.py:47
  120.5 5.9 %all-to-all-done.3.state_ref = f32[16,64,256]{2,1,0:T(8,128)S(1)} async-done(((f32[16,64,256]{2,1,0:T(8,128)}), f32[16,64,256]{2,1,0:T(8,128)S(1)}, u32[]{:S(2)}, u32[]{:S(2)}) %all-to-all-start.3) | async-done | bytes 1048608 | tf_op jit(solution)/shard_map/all_to_all | solution.py:607
  126.3 0.0 copy-start.2
  126.4 1.0 copy-done.2
  127.3 5.2 %branch_from_start.1 = bf16[256,512]{1,0:T(8,128)(2,1)} custom-call(bf16[256,4096]{1,0:T(8,128)(2,1)} %bitcast.28, bf16[4,256,32]{2,1,0:T(8,128)(2,1)} %get-tuple-element.125.e_ref, f32[16,64,256]{2,1,0:T(8,128)} %copy-done.2, f32[256,512]{1,0:T(8,128)} %get-tuple-element.127.part_ref), custom_call_target="tpu_custom_call" | custom-call | bytes 14760000 | tf_op jit(solution)/shard_map/branch_from_start/pallas_call | solution.py:47
Async XLA Ops:
  10.0 39.2 %all-to-all-start = ((f32[16,136,256]{2,1,0:T(8,128)}), f32[16,136,256]{2,1,0:T(8,128)S(1)}, u32[]{:S(2)}, u32[]{:S(2)}) async-start(f32[16,136,256]{2,1,0:T(8,128)} %get-tuple-element.68), calls=%async_computation | async-start | bytes 4456448 | tf_op jit(solution)/shard_map/all_to_all | solution.py:607
  49.2 1.2 copy-start.1
  50.5 1.3 copy-start
  51.9 32.5 %all-to-all-start.1 = ((f32[16,128,256]{2,1,0:T(8,128)}), f32[16,128,256]{2,1,0:T(8,128)}, u32[]{:S(2)}, u32[]{:S(2)}) async-start(f32[16,128,256]{2,1,0:T(8,128)} %copy-done), calls=%async_computation.1 | async-start | bytes 4194304 | tf_op jit(solution)/shard_map/all_to_all | solution.py:607
  57.8 1.7 %collective-permute-start = (f32[5,64,256]{2,1,0:T(8,128)S(1)}, f32[5,64,256]{2,1,0:T(8,128)S(1)}, u32[]{:S(2)}, u32[]{:S(2)}) collective-permute-start(f32[5,64,256]{2,1,0:T(8,128)S(1)} %get-tuple-element.82), channel_id=1, source_target_pairs={{0,1},{1,0},{2,3},{3,2},{4,5},{5,4},{6,7},{7,6},{8,9},{9,8},{10,11... | collective-permute-start | bytes 983048 | tf_op jit(solution)/shard_map/ppermute | solution.py:617
  60.1 20.4 %collective-permute-start.1 = (f32[3,64,256]{2,1,0:T(8,128)S(1)}, f32[3,64,256]{2,1,0:T(8,128)S(1)}, u32[]{:S(2)}, u32[]{:S(2)}) collective-permute-start(f32[3,64,256]{2,1,0:T(8,128)S(1)} %get-tuple-element.84), channel_id=1, source_target_pairs={{0,2},{1,3},{2,4},{3,5},{4,6},{5,7},{6,0},{7,1},{8,10},{9,11},{10,... | collective-permute-start | bytes 589832 | tf_op jit(solution)/shard_map/ppermute | solution.py:620
  62.0 18.5 %collective-permute-start.2 = (f32[3,64,256]{2,1,0:T(8,128)S(1)}, f32[3,64,256]{2,1,0:T(8,128)S(1)}, u32[]{:S(2)}, u32[]{:S(2)}) collective-permute-start(f32[3,64,256]{2,1,0:T(8,128)S(1)} %get-tuple-element.85), channel_id=1, source_target_pairs={{0,4},{1,5},{2,6},{3,7},{4,0},{5,1},{6,2},{7,3},{8,12},{9,13},{10,... | collective-permute-start | bytes 589832 | tf_op jit(solution)/shard_map/ppermute | solution.py:620
  65.6 14.9 %collective-permute-start.3 = (f32[3,64,256]{2,1,0:T(8,128)S(1)}, f32[3,64,256]{2,1,0:T(8,128)S(1)}, u32[]{:S(2)}, u32[]{:S(2)}) collective-permute-start(f32[3,64,256]{2,1,0:T(8,128)S(1)} %get-tuple-element.86), channel_id=1, source_target_pairs={{0,6},{1,7},{2,0},{3,1},{4,2},{5,3},{6,4},{7,5},{8,14},{9,15},{10,... | collective-permute-start | bytes 589832 | tf_op jit(solution)/shard_map/ppermute | solution.py:620
  87.0 20.0 %all-to-all-start.2 = ((f32[16,64,256]{2,1,0:T(8,128)}), f32[16,64,256]{2,1,0:T(8,128)}, u32[]{:S(2)}, u32[]{:S(2)}) async-start(f32[16,64,256]{2,1,0:T(8,128)} %end_gradients.1), calls=%async_computation.2 | async-start | bytes 2097152 | tf_op jit(solution)/shard_map/all_to_all | solution.py:607
  107.0 19.4 %all-to-all-start.3 = ((f32[16,64,256]{2,1,0:T(8,128)}), f32[16,64,256]{2,1,0:T(8,128)S(1)}, u32[]{:S(2)}, u32[]{:S(2)}) async-start(f32[16,64,256]{2,1,0:T(8,128)} %branch_starts.1), calls=%async_computation.3 | async-start | bytes 2097152 | tf_op jit(solution)/shard_map/all_to_all | solution.py:607
  126.3 1.0 copy-start.2

commit v4 on v3

--- a/solution.py
+++ b/solution.py
@@ -15,7 +15,7 @@
 F32 = jnp.float32
 BF16 = jnp.bfloat16
 BIG = 56
-MOST = 56
+MOST = 62
 VMEM = pl.BlockSpec(memory_space=pltpu.VMEM)
 SMEM = pl.BlockSpec(memory_space=pltpu.SMEM)
 
@@ -211,9 +211,9 @@
     )
 
 
-def decay_row(got_ref, i):
+def decay_row(got_ref, i, at):
     lane = lax.broadcasted_iota(jnp.int32, (1, 256), 1)
-    row = [got_ref[i, 128 + q : 129 + q, :] for q in range(4)]
+    row = [got_ref[i, at + q : at + q + 1, :] for q in range(4)]
     low = jnp.where(lane < 64, row[0], row[1])
     return jnp.where(lane < 128, low, jnp.where(lane < 192, row[2], row[3]))
 
@@ -223,7 +223,7 @@
     for i in range(16):
         out_ref[i, 0:64, :] = carry_ref[i]
         out_ref[i, 64:128, :] = state
-        state = decay_row(got_ref, i) * state + got_ref[i, 0:64, :]
+        state = decay_row(got_ref, i, 128) * state + got_ref[i, 0:64, :]
     end_ref[...] = state
 
 
@@ -293,20 +293,19 @@
     )
 
 
-def backward_kernel(got_ref, carry_ref, own_ref, r1, r2, r3, grad_ref):
+def backward_kernel(
+    place_ref, rows_ref, carry_ref, end_ref, recv_ref, own_ref, r1, r2, r3, out_ref
+):
+    z = place_ref[0]
+    core = place_ref[1]
     grad = own_ref[...] + r1[2] + r2[2] + r3[2]
     for i in range(15, -1, -1):
-        grad_ref[i] = grad
-        grad = decay_row(got_ref, i) * grad + carry_ref[i, 0:64, :]
-
-
-def starts_kernel(place_ref, gotb_ref, end_ref, recv_ref, r1, r2, r3, start_ref):
-    z = place_ref[0]
-    core = place_ref[1]
+        out_ref[i, 0:64, :] = grad
+        grad = decay_row(rows_ref, i, 0) * grad + carry_ref[i]
     mine = (end_ref[...], r1[0], r2[0], r3[0])
     theirs = (recv_ref[4], r1[1], r2[1], r3[1])
     for i in range(16):
-        owner = gotb_ref[i, 132:133, :]
+        owner = rows_ref[i, 4:5, :]
         start = jnp.zeros((64, 256), F32)
         for d in range(4):
             place = 2 * lax.rem(z + 4 - d, 4)
@@ -314,20 +313,28 @@
             there = (place + 1 - core).astype(F32)
             start = start + jnp.where(owner == here, mine[d], 0.0)
             start = start + jnp.where(owner == there, theirs[d], 0.0)
-        start_ref[i] = start
-
-
-def states_back(kernel, scalars, args, after, name):
-    return call(
-        kernel,
-        [SMEM] * len(scalars) + [VMEM] * len(args),
-        (VMEM,),
-        (jax.ShapeDtypeStruct((16, 64, 256), F32),),
-        (*scalars, *args),
-        after,
-        compiler_params=limits(12),
-        cost_estimate=cost(1.5),
-        name=name,
+        out_ref[i, 64:128, :] = start
+
+
+def backward(place, got, carry, end, recv, own, received):
+    return call(
+        backward_kernel,
+        [
+            SMEM,
+            pl.BlockSpec((16, 8, 256), lambda i: (0, 16, 0)),
+            pl.BlockSpec((16, 64, 256), lambda i: (0, 0, 0)),
+            whole(64, 256),
+            whole(5, 64, 256),
+            whole(64, 256),
+        ]
+        + [whole(3, 64, 256)] * 3,
+        (whole(16, 128, 256),),
+        (jax.ShapeDtypeStruct((16, 128, 256), F32),),
+        (place, got, carry, end, recv, own, *received),
+        grid=(1,),
+        compiler_params=limits(16),
+        cost_estimate=cost(2),
+        name="backward_scan",
     )
 
 
@@ -487,7 +494,7 @@
         after,
         grid=(4,),
         scratch_shapes=[scratch(BF16)] * 4 + [scratch(F32)],
-        compiler_params=limits(MOST),
+        compiler_params=limits(MOST if has_length else BIG),
         cost_estimate=cost(micros),
         name=name,
     )
@@ -564,19 +571,31 @@
     db_ref[...] = (dbp_ref[...] + jnp.concatenate(out, axis=1)).astype(BF16)
 
 
-def from_end(x, b, w, states, base, dx_part, db_part):
-    n = x.shape[0]
-    return call(
-        functools.partial(end_kernel, base),
+def tail_kernel(
+    x_ref, b_ref, w_ref, state_ref, dxp_ref, dbp_ref, ydy_ref, ye_ref, ydcp_ref, dx_ref, db_ref, ydc_ref
+):
+    end_kernel(0, x_ref, b_ref, w_ref, state_ref, dxp_ref, dbp_ref, dx_ref, db_ref)
+    start_kernel(64, ydy_ref, ye_ref, state_ref, ydcp_ref, ydc_ref)
+
+
+def from_states(x, b, w, states, dx_part, db_part, ydy, ye, ydc_part):
+    n, m = x.shape[0], ydy.shape[0]
+    return call(
+        tail_kernel,
         [cols(n, 1024), cols(n, 128), turns(n)]
-        + [pl.BlockSpec((4,) + states.shape[1:], lambda i: (i, 0, 0)), cols(n, 1024), cols(n, 128)],
-        (cols(n, 1024), cols(n, 128)),
-        (jax.ShapeDtypeStruct(x.shape, BF16), jax.ShapeDtypeStruct(b.shape, BF16)),
-        (x, b, w, states, dx_part, db_part),
+        + [pl.BlockSpec((4, 128, 256), lambda i: (i, 0, 0)), cols(n, 1024), cols(n, 128)]
+        + [cols(m, 1024), turns(m), cols(m, 128)],
+        (cols(n, 1024), cols(n, 128), cols(m, 128)),
+        (
+            jax.ShapeDtypeStruct(x.shape, BF16),
+            jax.ShapeDtypeStruct(b.shape, BF16),
+            jax.ShapeDtypeStruct((m, 512), BF16),
+        ),
+        (x, b, w, states, dx_part, db_part, ydy, ye, ydc_part),
         grid=(4,),
         compiler_params=limits(MOST),
-        cost_estimate=cost(10),
-        name="from_end",
+        cost_estimate=cost(12),
+        name="from_states",
     )
 
 
@@ -620,21 +639,13 @@
         lax.ppermute(m, "leaf", [(s, (s + 2 * d) % 8) for s in range(8)])
         for d, m in ((1, m1), (2, m2), (3, m3))
     ]
+    (third,) = backward(place, got, back, end, recv, own, received)
+    states = turn(third)
+    (dc,) = from_start(dy, e, back, 64, dc_part, (third,), "prompt_from_start")
     ydx, ydb, ydc_part = inside(
-        lengths, yx, ydy, yb, yc, ydt, yupto, yrest, BF16, (own,), 14, "branch_inside"
-    )
-    (grads,) = states_back(
-        backward_kernel, (), (got, back, own, *received), (ydb,), "end_gradients"
-    )
-    sent_grads = grads
-    grads = turn(grads)
-    (dc,) = from_start(dy, e, back, 64, dc_part, (sent_grads,), "prompt_from_start")
-    (starts,) = states_back(
-        starts_kernel, (place,), (got, end, recv, *received), (dc,), "branch_starts"
-    )
-    starts = turn(starts)
-    dx, db = from_end(x, b, w, grads, 0, dx_part, db_part)
-    (ydc,) = from_start(ydy, ye, starts, 0, ydc_part, (db,), "branch_from_start")
+        lengths, yx, ydy, yb, yc, ydt, yupto, yrest, BF16, (dc,), 14, "branch_inside"
+    )
+    dx, db, ydc = from_states(x, b, w, states, dx_part, db_part, ydy, ye, ydc_part)
     return tuple(a[None] for a in (dx, db, dc, ydx, ydb, ydc))
 
 

time: 133 us -> 132 us (level)
  waiting for transfers between devices: 21.4 us -> 29.6 us
  Pallas kernels: 79.3 us -> 72.5 us
  starting transfers between devices: 26.2 us -> 22.8 us
    ppermute x3, waiting for transfers between devices: 0.01 us -> 8.12 us  [local(): lax.ppermute(m, 'leaf', [(s, (s + 2 * d) % 8) for s in range(8)])]
    pallas_call x11 -> x9, Pallas kernels: 79.3 us -> 72.5 us  [call(): pl.pallas_call(kernel, in_specs=in_specs, out_specs=out_specs, out_shape=...]
    all_to_all x4 -> x3, starting transfers between devices: 19.6 us -> 16.2 us  [turn(): return lax.all_to_all(value, 'seq', 0, 0, tiled=True)]
    all_to_all x4 -> x3, waiting for transfers between devices: 19.8 us -> 19.8 us  [turn(): return lax.all_to_all(value, 'seq', 0, 0, tiled=True)]
  transfers between devices with their start and end apart: 8 -> 7, of which waited for: 5 -> 6; matrix products, arithmetic and copies ran while one was open for 0% -> 0% of each run, Pallas kernels for 48% -> 39%
where the time goes in v4:
time: 132 us; the launch traced here: 131 us
  Pallas kernels  72.5 us (55%)
  waiting for transfers between devices  29.6 us (22%)
  starting transfers between devices  22.8 us (17%)
  local copies, waits for them, and re-layouts  3.85 us (3%)
  between operations  2.18 us (2%)
    pallas_call x9, Pallas kernels, call(): pl.pallas_call(kernel, in_specs=in_specs, out_specs=out_specs, out_shape=...  72.5 us
    all_to_all x3, waiting for transfers between devices, turn(): return lax.all_to_all(value, 'seq', 0, 0, tiled=True)  19.8 us
    all_to_all x3, starting transfers between devices, turn(): return lax.all_to_all(value, 'seq', 0, 0, tiled=True)  16.2 us
    ppermute x3, waiting for transfers between devices, local(): lax.ppermute(m, 'leaf', [(s, (s + 2 * d) % 8) for s in range(8)])  8.12 us
    ppermute x3, starting transfers between devices, local(): lax.ppermute(m, 'leaf', [(s, (s + 2 * d) % 8) for s in range(8)])  6.55 us
    unnamed x6, local copies, waits for them, and re-layouts  3.85 us
  transfers between devices with their start and end apart: 7, of which 6 were waited for; matrix products, arithmetic and copies ran while one was open for 0% of the time, Pallas kernels for 39%

profile of v4, /device:TPU:0, one launch (start us, length us, event | category | flops | bytes accessed | tf_op | source)
XLA Modules:
  0.0 131.0 jit_solution(6462942495807999171)
XLA Ops:
  1.9 8.1 %first_message.1 = (f32[16,136,256]{2,1,0:T(8,128)}, f32[64,512]{1,0:T(8,128)}, f32[64,512]{1,0:T(8,128)}, f32[64,256]{1,0:T(8,128)}, f32[64,256]{1,0:T(8,128)},...) custom-call(s32[1]{0:T(128)S(6)} %copy.20.len_ref.refs_0_, ...), custom_call_target="tpu_custom_call" | custom-call | bytes 29520000 | tf_op jit(solution)/shard_map/first_message/pallas_call | solution.py:47
  10.0 7.1 %all-to-all-start = ((f32[16,136,256]{2,1,0:T(8,128)}), f32[16,136,256]{2,1,0:T(8,128)S(1)}, u32[]{:S(2)}, u32[]{:S(2)}) async-start(f32[16,136,256]{2,1,0:T(8,128)} %get-tuple-element.52), calls=%async_computation | async-start | bytes 4456448 | tf_op jit(solution)/shard_map/all_to_all | solution.py:626
  17.1 28.0 %prompt_inside.1 = (f32[512,4096]{1,0:T(8,128)}, f32[512,512]{1,0:T(8,128)}, f32[512,512]{1,0:T(8,128)}, f32[16,64,256]{2,1,0:T(8,128)}) custom-call(bf16[512,4096]{1,0:T(8,128)(2,1)} %bitcast.24, bf16[512,4096]{1,0:T(8,128)(2,1)} %bitcast.29, bf16[512,512]{1,0:T(8,128)(2,1)} %bitcast.32, bf16[512,512]{1,0:T(8,128)(2,1)} %bitcast.39, f32[64,512]{1,0:T(8,128)} %bitcast.38, ...), custom_call_target="tpu_custom_call" | custom-call | bytes 103320000 | tf_op jit(solution)/shard_map/prompt_inside/pallas_call | solution.py:47
  45.1 4.0 %all-to-all-done.got_ref.rows_ref = f32[16,136,256]{2,1,0:T(8,128)S(1)} async-done(((f32[16,136,256]{2,1,0:T(8,128)}), f32[16,136,256]{2,1,0:T(8,128)S(1)}, u32[]{:S(2)}, u32[]{:S(2)}) %all-to-all-start) | async-done | bytes 2228256 | tf_op jit(solution)/shard_map/all_to_all | solution.py:626
  49.1 0.0 copy-start.2
  49.2 1.2 copy-done.2
  50.4 0.1 forward_scan.1
  50.5 0.0 copy-start.1
  50.5 1.3 copy-done.1
  51.9 4.4 %all-to-all-start.1 = ((f32[16,128,256]{2,1,0:T(8,128)}), f32[16,128,256]{2,1,0:T(8,128)}, u32[]{:S(2)}, u32[]{:S(2)}) async-start(f32[16,128,256]{2,1,0:T(8,128)} %copy-done.1), calls=%async_computation.1 | async-start | bytes 4194304 | tf_op jit(solution)/shard_map/all_to_all | solution.py:626
  56.3 0.1 pad_add_fusion.place_ref
  56.4 1.4 %buckets.1 = (f32[4,64,256]{2,1,0:T(8,128)S(1)}, f32[5,64,256]{2,1,0:T(8,128)S(1)}) custom-call(s32[2]{0:T(128)S(1)} %pad_add_fusion.place_ref, f32[16,136,256]{2,1,0:T(8,128)S(1)} %all-to-all-done.got_ref.rows_ref, f32[64,256]{1,0:T(8,128)S(1)} %get-tuple-element.64.end_ref), custom_call_target="tpu_custom_call" | custom-call | bytes 3690000 | tf_op jit(solution)/shard_map/buckets/pallas_call | solution.py:47
  57.8 0.1 collective-permute-start
  57.9 1.6 %collective-permute-done.recv_ref = f32[5,64,256]{2,1,0:T(8,128)S(1)} collective-permute-done((f32[5,64,256]{2,1,0:T(8,128)S(1)}, f32[5,64,256]{2,1,0:T(8,128)S(1)}, u32[]{:S(2)}, u32[]{:S(2)}) %collective-permute-start) | collective-permute-done | bytes 327712 | tf_op jit(solution)/shard_map/ppermute | solution.py:636
  59.5 0.6 pack_leaf.1
  60.1 1.9 %collective-permute-start.1 = (f32[3,64,256]{2,1,0:T(8,128)S(1)}, f32[3,64,256]{2,1,0:T(8,128)S(1)}, u32[]{:S(2)}, u32[]{:S(2)}) collective-permute-start(f32[3,64,256]{2,1,0:T(8,128)S(1)} %get-tuple-element.68), channel_id=1, source_target_pairs={{0,2},{1,3},{2,4},{3,5},{4,6},{5,7},{6,0},{7,1},{8,10},{9,11},{10,... | collective-permute-start | bytes 589832 | tf_op jit(solution)/shard_map/ppermute | solution.py:639
  62.0 3.6 %collective-permute-start.2 = (f32[3,64,256]{2,1,0:T(8,128)S(1)}, f32[3,64,256]{2,1,0:T(8,128)S(1)}, u32[]{:S(2)}, u32[]{:S(2)}) collective-permute-start(f32[3,64,256]{2,1,0:T(8,128)S(1)} %get-tuple-element.69), channel_id=1, source_target_pairs={{0,4},{1,5},{2,6},{3,7},{4,0},{5,1},{6,2},{7,3},{8,12},{9,13},{10,... | collective-permute-start | bytes 589832 | tf_op jit(solution)/shard_map/ppermute | solution.py:639
  65.6 1.0 collective-permute-start.3
  66.6 2.7 %collective-permute-done.1.r1 = f32[3,64,256]{2,1,0:T(8,128)S(1)} collective-permute-done((f32[3,64,256]{2,1,0:T(8,128)S(1)}, f32[3,64,256]{2,1,0:T(8,128)S(1)}, u32[]{:S(2)}, u32[]{:S(2)}) %collective-permute-start.1) | collective-permute-done | bytes 196640 | tf_op jit(solution)/shard_map/ppermute | solution.py:639
  69.4 5.4 %collective-permute-done.2.r2 = f32[3,64,256]{2,1,0:T(8,128)S(1)} collective-permute-done((f32[3,64,256]{2,1,0:T(8,128)S(1)}, f32[3,64,256]{2,1,0:T(8,128)S(1)}, u32[]{:S(2)}, u32[]{:S(2)}) %collective-permute-start.2) | collective-permute-done | bytes 196640 | tf_op jit(solution)/shard_map/ppermute | solution.py:639
  74.8 0.0 collective-permute-done.3.r3
  74.8 9.6 %all-to-all-done.1.carry_ref.state_ref = f32[16,128,256]{2,1,0:T(8,128)} async-done(((f32[16,128,256]{2,1,0:T(8,128)}), f32[16,128,256]{2,1,0:T(8,128)}, u32[]{:S(2)}, u32[]{:S(2)}) %all-to-all-start.1) | async-done | bytes 2097184 | tf_op jit(solution)/shard_map/all_to_all | solution.py:626
  84.4 2.0 %backward_scan.1 = f32[16,128,256]{2,1,0:T(8,128)S(1)} custom-call(s32[2]{0:T(128)S(1)} %pad_add_fusion.place_ref, f32[16,136,256]{2,1,0:T(8,128)S(1)} %all-to-all-done.got_ref.rows_ref, f32[16,128,256]{2,1,0:T(8,128)} %all-to-all-done.1.carry_ref.state_ref, f32[64,256]{1,0:T(8,128)S(1)} %get-tuple-element.64.end_ref, ...), custom_call_target="tpu_custom_call" | custom-call | bytes 7380000 | tf_op jit(solution)/shard_map/backward_scan/pallas_call | solution.py:47
  86.4 0.0 copy-start
  86.4 1.3 copy-done
  87.7 4.6 %all-to-all-start.2 = ((f32[16,128,256]{2,1,0:T(8,128)}), f32[16,128,256]{2,1,0:T(8,128)}, u32[]{:S(2)}, u32[]{:S(2)}) async-start(f32[16,128,256]{2,1,0:T(8,128)} %copy-done), calls=%async_computation.2 | async-start | bytes 4194304 | tf_op jit(solution)/shard_map/all_to_all | solution.py:626
  92.3 7.2 %prompt_from_start.1 = bf16[512,512]{1,0:T(8,128)(2,1)} custom-call(bf16[512,4096]{1,0:T(8,128)(2,1)} %bitcast.30, bf16[4,512,32]{2,1,0:T(8,128)(2,1)} %get-tuple-element.79.e_ref, f32[16,128,256]{2,1,0:T(8,128)} %all-to-all-done.1.carry_ref.state_ref, f32[512,512]{1,0:T(8,128)} %get-tuple-element.81.part_ref), custom_call_target="tpu_custom_call" | custom-call | bytes 29520000 | tf_op jit(solution)/shard_map/prompt_from_start/pallas_call | solution.py:47
  99.5 13.9 %branch_inside.1 = (bf16[256,4096]{1,0:T(8,128)(2,1)}, bf16[256,512]{1,0:T(8,128)(2,1)}, f32[256,512]{1,0:T(8,128)}) custom-call(s32[1]{0:T(128)S(6)} %copy.20.len_ref.refs_0_, bf16[256,4096]{1,0:T(8,128)(2,1)} %bitcast.34, bf16[256,4096]{1,0:T(8,128)(2,1)} %bitcast.27, bf16[256,512]{1,0:T(8,128)(2,1)} %bitcast.43, bf16[256,512]{1,0:T(8,128)(2,1)} %bitcast.36, ...), custom_call_target="tpu_custom_call" | custom-call | bytes 51660000 | tf_op jit(solution)/shard_map/branch_inside/pallas_call | solution.py:47
  113.4 6.2 %all-to-all-done.2.state_ref = f32[16,128,256]{2,1,0:T(8,128)} async-done(((f32[16,128,256]{2,1,0:T(8,128)}), f32[16,128,256]{2,1,0:T(8,128)}, u32[]{:S(2)}, u32[]{:S(2)}) %all-to-all-start.2) | async-done | bytes 2097184 | tf_op jit(solution)/shard_map/all_to_all | solution.py:626
  119.6 11.2 %from_states.1 = (bf16[512,4096]{1,0:T(8,128)(2,1)}, bf16[512,512]{1,0:T(8,128)(2,1)}, bf16[256,512]{1,0:T(8,128)(2,1)}) custom-call(bf16[512,4096]{1,0:T(8,128)(2,1)} %bitcast.25, bf16[512,512]{1,0:T(8,128)(2,1)} %bitcast.33, bf16[4,512,32]{2,1,0:T(8,128)(2,1)} %get-tuple-element.51.w_ref, f32[16,128,256]{2,1,0:T(8,128)} %all-to-all-done.2.state_ref, ...), custom_call_target="tpu_custom_call" | custom-call | bytes 44280000 | tf_op jit(solution)/shard_map/from_states/pallas_call | solution.py:47
Async XLA Ops:
  10.0 39.2 %all-to-all-start = ((f32[16,136,256]{2,1,0:T(8,128)}), f32[16,136,256]{2,1,0:T(8,128)S(1)}, u32[]{:S(2)}, u32[]{:S(2)}) async-start(f32[16,136,256]{2,1,0:T(8,128)} %get-tuple-element.52), calls=%async_computation | async-start | bytes 4456448 | tf_op jit(solution)/shard_map/all_to_all | solution.py:626
  49.1 1.2 copy-start.2
  50.5 1.3 %copy-start.1 = (f32[16,128,256]{2,1,0:T(8,128)}, f32[16,128,256]{2,1,0:T(8,128)S(1)}, u32[]{:S(2)}) copy-start(f32[16,128,256]{2,1,0:T(8,128)S(1)} %get-tuple-element.63) | copy-start | bytes 6291460
  51.9 32.5 %all-to-all-start.1 = ((f32[16,128,256]{2,1,0:T(8,128)}), f32[16,128,256]{2,1,0:T(8,128)}, u32[]{:S(2)}, u32[]{:S(2)}) async-start(f32[16,128,256]{2,1,0:T(8,128)} %copy-done.1), calls=%async_computation.1 | async-start | bytes 4194304 | tf_op jit(solution)/shard_map/all_to_all | solution.py:626
  57.8 1.7 %collective-permute-start = (f32[5,64,256]{2,1,0:T(8,128)S(1)}, f32[5,64,256]{2,1,0:T(8,128)S(1)}, u32[]{:S(2)}, u32[]{:S(2)}) collective-permute-start(f32[5,64,256]{2,1,0:T(8,128)S(1)} %get-tuple-element.65), channel_id=1, source_target_pairs={{0,1},{1,0},{2,3},{3,2},{4,5},{5,4},{6,7},{7,6},{8,9},{9,8},{10,11... | collective-permute-start | bytes 983048 | tf_op jit(solution)/shard_map/ppermute | solution.py:636
  60.1 9.3 %collective-permute-start.1 = (f32[3,64,256]{2,1,0:T(8,128)S(1)}, f32[3,64,256]{2,1,0:T(8,128)S(1)}, u32[]{:S(2)}, u32[]{:S(2)}) collective-permute-start(f32[3,64,256]{2,1,0:T(8,128)S(1)} %get-tuple-element.68), channel_id=1, source_target_pairs={{0,2},{1,3},{2,4},{3,5},{4,6},{5,7},{6,0},{7,1},{8,10},{9,11},{10,... | collective-permute-start | bytes 589832 | tf_op jit(solution)/shard_map/ppermute | solution.py:639
  62.0 12.7 %collective-permute-start.2 = (f32[3,64,256]{2,1,0:T(8,128)S(1)}, f32[3,64,256]{2,1,0:T(8,128)S(1)}, u32[]{:S(2)}, u32[]{:S(2)}) collective-permute-start(f32[3,64,256]{2,1,0:T(8,128)S(1)} %get-tuple-element.69), channel_id=1, source_target_pairs={{0,4},{1,5},{2,6},{3,7},{4,0},{5,1},{6,2},{7,3},{8,12},{9,13},{10,... | collective-permute-start | bytes 589832 | tf_op jit(solution)/shard_map/ppermute | solution.py:639
  65.6 9.1 %collective-permute-start.3 = (f32[3,64,256]{2,1,0:T(8,128)S(1)}, f32[3,64,256]{2,1,0:T(8,128)S(1)}, u32[]{:S(2)}, u32[]{:S(2)}) collective-permute-start(f32[3,64,256]{2,1,0:T(8,128)S(1)} %get-tuple-element.70), channel_id=1, source_target_pairs={{0,6},{1,7},{2,0},{3,1},{4,2},{5,3},{6,4},{7,5},{8,14},{9,15},{10,... | collective-permute-start | bytes 589832 | tf_op jit(solution)/shard_map/ppermute | solution.py:639
  86.4 1.3 %copy-start = (f32[16,128,256]{2,1,0:T(8,128)}, f32[16,128,256]{2,1,0:T(8,128)S(1)}, u32[]{:S(2)}) copy-start(f32[16,128,256]{2,1,0:T(8,128)S(1)} %backward_scan.1) | copy-start | bytes 6291460
  87.7 31.9 %all-to-all-start.2 = ((f32[16,128,256]{2,1,0:T(8,128)}), f32[16,128,256]{2,1,0:T(8,128)}, u32[]{:S(2)}, u32[]{:S(2)}) async-start(f32[16,128,256]{2,1,0:T(8,128)} %copy-done), calls=%async_computation.2 | async-start | bytes 4194304 | tf_op jit(solution)/shard_map/all_to_all | solution.py:626

commit v5 on v4

--- a/solution.py
+++ b/solution.py
@@ -580,19 +580,22 @@
 
 def from_states(x, b, w, states, dx_part, db_part, ydy, ye, ydc_part):
     n, m = x.shape[0], ydy.shape[0]
+    wide = lambda k: pl.BlockSpec((k // 2, 1024), lambda i, j: (j, i))
+    thin = lambda k: pl.BlockSpec((k // 2, 128), lambda i, j: (j, i))
+    turned_half = lambda k: pl.BlockSpec((1, k // 2, 32), lambda i, j: (i, j, 0))
     return call(
         tail_kernel,
-        [cols(n, 1024), cols(n, 128), turns(n)]
-        + [pl.BlockSpec((4, 128, 256), lambda i: (i, 0, 0)), cols(n, 1024), cols(n, 128)]
-        + [cols(m, 1024), turns(m), cols(m, 128)],
-        (cols(n, 1024), cols(n, 128), cols(m, 128)),
+        [wide(n), thin(n), turned_half(n)]
+        + [pl.BlockSpec((4, 128, 256), lambda i, j: (i, 0, 0)), wide(n), thin(n)]
+        + [wide(m), turned_half(m), thin(m)],
+        (wide(n), thin(n), thin(m)),
         (
             jax.ShapeDtypeStruct(x.shape, BF16),
             jax.ShapeDtypeStruct(b.shape, BF16),
             jax.ShapeDtypeStruct((m, 512), BF16),
         ),
         (x, b, w, states, dx_part, db_part, ydy, ye, ydc_part),
-        grid=(4,),
+        grid=(4, 2),
         compiler_params=limits(MOST),
         cost_estimate=cost(12),
         name="from_states",

time: 132 us -> 133 us (level)
  Pallas kernels: 72.5 us -> 74.3 us
    pallas_call x9, Pallas kernels: 72.5 us -> 74.3 us  [call(): pl.pallas_call(kernel, in_specs=in_specs, out_specs=out_specs, out_shape=...]
  transfers between devices with their start and end apart: 7 -> 7, of which waited for: 6 -> 6; matrix products, arithmetic and copies ran while one was open for 0% -> 0% of each run, Pallas kernels for 39% -> 38%
where the time goes in v5:
time: 133 us
  Pallas kernels  74.3 us (56%)
  waiting for transfers between devices  29.6 us (22%)
  starting transfers between devices  22.8 us (17%)
  local copies, waits for them, and re-layouts  3.85 us (3%)
  between operations  2.12 us (2%)
    pallas_call x9, Pallas kernels, call(): pl.pallas_call(kernel, in_specs=in_specs, out_specs=out_specs, out_shape=...  74.3 us
    all_to_all x3, waiting for transfers between devices, turn(): return lax.all_to_all(value, 'seq', 0, 0, tiled=True)  19.8 us
    all_to_all x3, starting transfers between devices, turn(): return lax.all_to_all(value, 'seq', 0, 0, tiled=True)  16.2 us
    ppermute x3, waiting for transfers between devices, local(): lax.ppermute(m, 'leaf', [(s, (s + 2 * d) % 8) for s in range(8)])  8.12 us
    ppermute x3, starting transfers between devices, local(): lax.ppermute(m, 'leaf', [(s, (s + 2 * d) % 8) for s in range(8)])  6.55 us
    unnamed x6, local copies, waits for them, and re-layouts  3.85 us
  transfers between devices with their start and end apart: 7, of which 6 were waited for; matrix products, arithmetic and copies ran while one was open for 0% of the time, Pallas kernels for 38%

profile of v5, /device:TPU:0, one launch (start us, length us, event | category | flops | bytes accessed | tf_op | source)
XLA Modules:
  0.0 132.7 jit_solution(64676518202747325)
XLA Ops:
  1.9 8.1 %first_message.1 = (f32[16,136,256]{2,1,0:T(8,128)}, f32[64,512]{1,0:T(8,128)}, f32[64,512]{1,0:T(8,128)}, f32[64,256]{1,0:T(8,128)}, f32[64,256]{1,0:T(8,128)},...) custom-call(s32[1]{0:T(128)S(6)} %copy.20.len_ref.refs_0_, ...), custom_call_target="tpu_custom_call" | custom-call | bytes 29520000 | tf_op jit(solution)/shard_map/first_message/pallas_call | solution.py:47
  10.0 7.1 %all-to-all-start = ((f32[16,136,256]{2,1,0:T(8,128)}), f32[16,136,256]{2,1,0:T(8,128)S(1)}, u32[]{:S(2)}, u32[]{:S(2)}) async-start(f32[16,136,256]{2,1,0:T(8,128)} %get-tuple-element.52), calls=%async_computation | async-start | bytes 4456448 | tf_op jit(solution)/shard_map/all_to_all | solution.py:629
  17.1 28.0 %prompt_inside.1 = (f32[512,4096]{1,0:T(8,128)}, f32[512,512]{1,0:T(8,128)}, f32[512,512]{1,0:T(8,128)}, f32[16,64,256]{2,1,0:T(8,128)}) custom-call(bf16[512,4096]{1,0:T(8,128)(2,1)} %bitcast.24, bf16[512,4096]{1,0:T(8,128)(2,1)} %bitcast.29, bf16[512,512]{1,0:T(8,128)(2,1)} %bitcast.32, bf16[512,512]{1,0:T(8,128)(2,1)} %bitcast.39, f32[64,512]{1,0:T(8,128)} %bitcast.38, ...), custom_call_target="tpu_custom_call" | custom-call | bytes 103320000 | tf_op jit(solution)/shard_map/prompt_inside/pallas_call | solution.py:47
  45.1 4.0 %all-to-all-done.got_ref.rows_ref = f32[16,136,256]{2,1,0:T(8,128)S(1)} async-done(((f32[16,136,256]{2,1,0:T(8,128)}), f32[16,136,256]{2,1,0:T(8,128)S(1)}, u32[]{:S(2)}, u32[]{:S(2)}) %all-to-all-start) | async-done | bytes 2228256 | tf_op jit(solution)/shard_map/all_to_all | solution.py:629
  49.1 0.0 copy-start.2
  49.2 1.2 copy-done.2
  50.4 0.1 forward_scan.1
  50.5 0.0 copy-start.1
  50.5 1.3 copy-done.1
  51.9 4.4 %all-to-all-start.1 = ((f32[16,128,256]{2,1,0:T(8,128)}), f32[16,128,256]{2,1,0:T(8,128)}, u32[]{:S(2)}, u32[]{:S(2)}) async-start(f32[16,128,256]{2,1,0:T(8,128)} %copy-done.1), calls=%async_computation.1 | async-start | bytes 4194304 | tf_op jit(solution)/shard_map/all_to_all | solution.py:629
  56.3 0.1 pad_add_fusion.place_ref
  56.4 1.4 %buckets.1 = (f32[4,64,256]{2,1,0:T(8,128)S(1)}, f32[5,64,256]{2,1,0:T(8,128)S(1)}) custom-call(s32[2]{0:T(128)S(1)} %pad_add_fusion.place_ref, f32[16,136,256]{2,1,0:T(8,128)S(1)} %all-to-all-done.got_ref.rows_ref, f32[64,256]{1,0:T(8,128)S(1)} %get-tuple-element.64.end_ref), custom_call_target="tpu_custom_call" | custom-call | bytes 3690000 | tf_op jit(solution)/shard_map/buckets/pallas_call | solution.py:47
  57.8 0.1 collective-permute-start
  57.9 1.6 %collective-permute-done.recv_ref = f32[5,64,256]{2,1,0:T(8,128)S(1)} collective-permute-done((f32[5,64,256]{2,1,0:T(8,128)S(1)}, f32[5,64,256]{2,1,0:T(8,128)S(1)}, u32[]{:S(2)}, u32[]{:S(2)}) %collective-permute-start) | collective-permute-done | bytes 327712 | tf_op jit(solution)/shard_map/ppermute | solution.py:639
  59.5 0.6 pack_leaf.1
  60.1 1.9 %collective-permute-start.1 = (f32[3,64,256]{2,1,0:T(8,128)S(1)}, f32[3,64,256]{2,1,0:T(8,128)S(1)}, u32[]{:S(2)}, u32[]{:S(2)}) collective-permute-start(f32[3,64,256]{2,1,0:T(8,128)S(1)} %get-tuple-element.68), channel_id=1, source_target_pairs={{0,2},{1,3},{2,4},{3,5},{4,6},{5,7},{6,0},{7,1},{8,10},{9,11},{10,... | collective-permute-start | bytes 589832 | tf_op jit(solution)/shard_map/ppermute | solution.py:642
  62.0 3.6 %collective-permute-start.2 = (f32[3,64,256]{2,1,0:T(8,128)S(1)}, f32[3,64,256]{2,1,0:T(8,128)S(1)}, u32[]{:S(2)}, u32[]{:S(2)}) collective-permute-start(f32[3,64,256]{2,1,0:T(8,128)S(1)} %get-tuple-element.69), channel_id=1, source_target_pairs={{0,4},{1,5},{2,6},{3,7},{4,0},{5,1},{6,2},{7,3},{8,12},{9,13},{10,... | collective-permute-start | bytes 589832 | tf_op jit(solution)/shard_map/ppermute | solution.py:642
  65.6 1.0 collective-permute-start.3
  66.6 2.7 %collective-permute-done.1.r1 = f32[3,64,256]{2,1,0:T(8,128)S(1)} collective-permute-done((f32[3,64,256]{2,1,0:T(8,128)S(1)}, f32[3,64,256]{2,1,0:T(8,128)S(1)}, u32[]{:S(2)}, u32[]{:S(2)}) %collective-permute-start.1) | collective-permute-done | bytes 196640 | tf_op jit(solution)/shard_map/ppermute | solution.py:642
  69.4 5.4 %collective-permute-done.2.r2 = f32[3,64,256]{2,1,0:T(8,128)S(1)} collective-permute-done((f32[3,64,256]{2,1,0:T(8,128)S(1)}, f32[3,64,256]{2,1,0:T(8,128)S(1)}, u32[]{:S(2)}, u32[]{:S(2)}) %collective-permute-start.2) | collective-permute-done | bytes 196640 | tf_op jit(solution)/shard_map/ppermute | solution.py:642
  74.8 0.0 collective-permute-done.3.r3
  74.8 9.6 %all-to-all-done.1.carry_ref.state_ref = f32[16,128,256]{2,1,0:T(8,128)} async-done(((f32[16,128,256]{2,1,0:T(8,128)}), f32[16,128,256]{2,1,0:T(8,128)}, u32[]{:S(2)}, u32[]{:S(2)}) %all-to-all-start.1) | async-done | bytes 2097184 | tf_op jit(solution)/shard_map/all_to_all | solution.py:629
  84.4 2.0 %backward_scan.1 = f32[16,128,256]{2,1,0:T(8,128)S(1)} custom-call(s32[2]{0:T(128)S(1)} %pad_add_fusion.place_ref, f32[16,136,256]{2,1,0:T(8,128)S(1)} %all-to-all-done.got_ref.rows_ref, f32[16,128,256]{2,1,0:T(8,128)} %all-to-all-done.1.carry_ref.state_ref, f32[64,256]{1,0:T(8,128)S(1)} %get-tuple-element.64.end_ref, ...), custom_call_target="tpu_custom_call" | custom-call | bytes 7380000 | tf_op jit(solution)/shard_map/backward_scan/pallas_call | solution.py:47
  86.4 0.0 copy-start
  86.4 1.3 copy-done
  87.7 4.6 %all-to-all-start.2 = ((f32[16,128,256]{2,1,0:T(8,128)}), f32[16,128,256]{2,1,0:T(8,128)}, u32[]{:S(2)}, u32[]{:S(2)}) async-start(f32[16,128,256]{2,1,0:T(8,128)} %copy-done), calls=%async_computation.2 | async-start | bytes 4194304 | tf_op jit(solution)/shard_map/all_to_all | solution.py:629
  92.3 7.2 %prompt_from_start.1 = bf16[512,512]{1,0:T(8,128)(2,1)} custom-call(bf16[512,4096]{1,0:T(8,128)(2,1)} %bitcast.30, bf16[4,512,32]{2,1,0:T(8,128)(2,1)} %get-tuple-element.79.e_ref, f32[16,128,256]{2,1,0:T(8,128)} %all-to-all-done.1.carry_ref.state_ref, f32[512,512]{1,0:T(8,128)} %get-tuple-element.81.part_ref), custom_call_target="tpu_custom_call" | custom-call | bytes 29520000 | tf_op jit(solution)/shard_map/prompt_from_start/pallas_call | solution.py:47
  99.5 13.9 %branch_inside.1 = (bf16[256,4096]{1,0:T(8,128)(2,1)}, bf16[256,512]{1,0:T(8,128)(2,1)}, f32[256,512]{1,0:T(8,128)}) custom-call(s32[1]{0:T(128)S(6)} %copy.20.len_ref.refs_0_, bf16[256,4096]{1,0:T(8,128)(2,1)} %bitcast.34, bf16[256,4096]{1,0:T(8,128)(2,1)} %bitcast.27, bf16[256,512]{1,0:T(8,128)(2,1)} %bitcast.43, bf16[256,512]{1,0:T(8,128)(2,1)} %bitcast.36, ...), custom_call_target="tpu_custom_call" | custom-call | bytes 51660000 | tf_op jit(solution)/shard_map/branch_inside/pallas_call | solution.py:47
  113.4 6.2 %all-to-all-done.2.state_ref = f32[16,128,256]{2,1,0:T(8,128)} async-done(((f32[16,128,256]{2,1,0:T(8,128)}), f32[16,128,256]{2,1,0:T(8,128)}, u32[]{:S(2)}, u32[]{:S(2)}) %all-to-all-start.2) | async-done | bytes 2097184 | tf_op jit(solution)/shard_map/all_to_all | solution.py:629
  119.6 13.0 %from_states.1 = (bf16[512,4096]{1,0:T(8,128)(2,1)}, bf16[512,512]{1,0:T(8,128)(2,1)}, bf16[256,512]{1,0:T(8,128)(2,1)}) custom-call(bf16[512,4096]{1,0:T(8,128)(2,1)} %bitcast.25, bf16[512,512]{1,0:T(8,128)(2,1)} %bitcast.33, bf16[4,512,32]{2,1,0:T(8,128)(2,1)} %get-tuple-element.51.w_ref, f32[16,128,256]{2,1,0:T(8,128)} %all-to-all-done.2.state_ref, ...), custom_call_target="tpu_custom_call" | custom-call | bytes 44280000 | tf_op jit(solution)/shard_map/from_states/pallas_call | solution.py:47
Async XLA Ops:
  10.0 39.2 %all-to-all-start = ((f32[16,136,256]{2,1,0:T(8,128)}), f32[16,136,256]{2,1,0:T(8,128)S(1)}, u32[]{:S(2)}, u32[]{:S(2)}) async-start(f32[16,136,256]{2,1,0:T(8,128)} %get-tuple-element.52), calls=%async_computation | async-start | bytes 4456448 | tf_op jit(solution)/shard_map/all_to_all | solution.py:629
  49.1 1.2 copy-start.2
  50.5 1.3 copy-start.1
  51.9 32.5 %all-to-all-start.1 = ((f32[16,128,256]{2,1,0:T(8,128)}), f32[16,128,256]{2,1,0:T(8,128)}, u32[]{:S(2)}, u32[]{:S(2)}) async-start(f32[16,128,256]{2,1,0:T(8,128)} %copy-done.1), calls=%async_computation.1 | async-start | bytes 4194304 | tf_op jit(solution)/shard_map/all_to_all | solution.py:629
  57.8 1.7 %collective-permute-start = (f32[5,64,256]{2,1,0:T(8,128)S(1)}, f32[5,64,256]{2,1,0:T(8,128)S(1)}, u32[]{:S(2)}, u32[]{:S(2)}) collective-permute-start(f32[5,64,256]{2,1,0:T(8,128)S(1)} %get-tuple-element.65), channel_id=1, source_target_pairs={{0,1},{1,0},{2,3},{3,2},{4,5},{5,4},{6,7},{7,6},{8,9},{9,8},{10,11... | collective-permute-start | bytes 983048 | tf_op jit(solution)/shard_map/ppermute | solution.py:639
  60.1 9.3 %collective-permute-start.1 = (f32[3,64,256]{2,1,0:T(8,128)S(1)}, f32[3,64,256]{2,1,0:T(8,128)S(1)}, u32[]{:S(2)}, u32[]{:S(2)}) collective-permute-start(f32[3,64,256]{2,1,0:T(8,128)S(1)} %get-tuple-element.68), channel_id=1, source_target_pairs={{0,2},{1,3},{2,4},{3,5},{4,6},{5,7},{6,0},{7,1},{8,10},{9,11},{10,... | collective-permute-start | bytes 589832 | tf_op jit(solution)/shard_map/ppermute | solution.py:642
  62.0 12.7 %collective-permute-start.2 = (f32[3,64,256]{2,1,0:T(8,128)S(1)}, f32[3,64,256]{2,1,0:T(8,128)S(1)}, u32[]{:S(2)}, u32[]{:S(2)}) collective-permute-start(f32[3,64,256]{2,1,0:T(8,128)S(1)} %get-tuple-element.69), channel_id=1, source_target_pairs={{0,4},{1,5},{2,6},{3,7},{4,0},{5,1},{6,2},{7,3},{8,12},{9,13},{10,... | collective-permute-start | bytes 589832 | tf_op jit(solution)/shard_map/ppermute | solution.py:642
  65.6 9.1 %collective-permute-start.3 = (f32[3,64,256]{2,1,0:T(8,128)S(1)}, f32[3,64,256]{2,1,0:T(8,128)S(1)}, u32[]{:S(2)}, u32[]{:S(2)}) collective-permute-start(f32[3,64,256]{2,1,0:T(8,128)S(1)} %get-tuple-element.70), channel_id=1, source_target_pairs={{0,6},{1,7},{2,0},{3,1},{4,2},{5,3},{6,4},{7,5},{8,14},{9,15},{10,... | collective-permute-start | bytes 589832 | tf_op jit(solution)/shard_map/ppermute | solution.py:642
  86.4 1.3 copy-start
  87.7 31.9 %all-to-all-start.2 = ((f32[16,128,256]{2,1,0:T(8,128)}), f32[16,128,256]{2,1,0:T(8,128)}, u32[]{:S(2)}, u32[]{:S(2)}) async-start(f32[16,128,256]{2,1,0:T(8,128)} %copy-done), calls=%async_computation.2 | async-start | bytes 4194304 | tf_op jit(solution)/shard_map/all_to_all | solution.py:629
